TPU v7x, 32 devices: a whole 2x2x4 slice. The times are simulated.
32 devices in a mesh: dp: 8 (over z, core), ctx: 4 (over y, x).
Axes of the slice: x: 2, y: 2, z: 4, core: 2. Of those that a mesh axis runs over, the one named last changes fastest.
Arguments:
- byte_ids: int32 [8, 2048], P('dp', 'ctx'), may hold values from 0 to 255
- lengths: int32 [8, 4], P('dp'), may hold values from 64 to 1856, as said below
- embed: bfloat16 [256, 768], P(None, ('dp', 'ctx')), may hold values from -6 to 6
- conv_weight: bfloat16 [4, 768], P(None, ('dp', 'ctx')), may hold values from -3 to 3
- conv_bias: bfloat16 [768], P(('dp', 'ctx')), may hold values from -2 to 2
- scorer: bfloat16 [768], P(('dp', 'ctx')), may hold values from -0.4375 to 0.4375
- norm_attn: bfloat16 [2, 768], P(None, ('dp', 'ctx')), may hold values from 0.5 to 1.5
- query_w: bfloat16 [2, 768, 768], P(None, ('dp', 'ctx')), may hold values from -0.0546875 to 0.0546875
- key_w: bfloat16 [2, 768, 768], P(None, ('dp', 'ctx')), may hold values from -0.21875 to 0.21875
- value_w: bfloat16 [2, 768, 768], P(None, ('dp', 'ctx')), may hold values from -0.21875 to 0.21875
- attn_out_w: bfloat16 [2, 768, 768], P(None, ('dp', 'ctx')), may hold values from -1.25 to 1.25
- norm_ffn: bfloat16 [2, 768], P(None, ('dp', 'ctx')), may hold values from 0.5 to 1.5
- gate_w: bfloat16 [2, 768, 2048], P(None, ('dp', 'ctx')), may hold values from -0.21875 to 0.21875
- up_w: bfloat16 [2, 768, 2048], P(None, ('dp', 'ctx')), may hold values from -0.21875 to 0.21875
- down_w: bfloat16 [2, 2048, 768], P(None, ('dp', 'ctx')), may hold values from -0.125 to 0.125
- out_grad: bfloat16 [8, 1024, 768], P('dp', 'ctx'), may hold values from -6 to 6
Outputs:
- encoded: bfloat16 [8, 1024, 768], P('dp', 'ctx')
- grad_embed: float32 [256, 768], P(None, ('dp', 'ctx'))
- grad_conv_weight: float32 [4, 768], P(None, ('dp', 'ctx'))
- grad_conv_bias: float32 [768], P(('dp', 'ctx'))
- grad_scorer: float32 [768], P(('dp', 'ctx'))
- grad_norm_attn: float32 [2, 768], P(None, ('dp', 'ctx'))
- grad_query_w: float32 [2, 768, 768], P(None, ('dp', 'ctx'))
- grad_key_w: float32 [2, 768, 768], P(None, ('dp', 'ctx'))
- grad_value_w: float32 [2, 768, 768], P(None, ('dp', 'ctx'))
- grad_attn_out_w: float32 [2, 768, 768], P(None, ('dp', 'ctx'))
- grad_norm_ffn: float32 [2, 768], P(None, ('dp', 'ctx'))
- grad_gate_w: float32 [2, 768, 2048], P(None, ('dp', 'ctx'))
- grad_up_w: float32 [2, 768, 2048], P(None, ('dp', 'ctx'))
- grad_down_w: float32 [2, 2048, 768], P(None, ('dp', 'ctx'))
Inputs may be any that keep to these rules, and one draw needn't show every extreme that they name: `lengths`: every length is even; each group holds 4 sequences packed end to end from its first byte, followed by padding; in each group one sequence starts among the first 512 bytes and ends among the last 512 bytes.
All inputs are finite; a program needn't handle non-finite values.
Results may differ from a plain program's by a relative error of at most 0.019.
Values may be sent and summed in bfloat16 or wider, within the bound.
A program may use at most 256 MiB of HBM per device.

v0:
```python
import jax
import jax.numpy as jnp
from jax import lax
from jax.sharding import PartitionSpec as P

HEADS = 12
HEAD_DIM = 64


NORM_EPS = 1e-06
NEG_FILL = -1000000000.0
PRECISE = lax.Precision.HIGHEST


def padded(shard, sides, width):
    for axis, dim in sides:
        count, length = (lax.axis_size(axis), shard.shape[dim])
        up = [(i, (i + 1) % count) for i in range(count - 1)]
        down = [(j, i) for i, j in up]
        last = lax.slice_in_dim(shard, length - width, length, axis=dim)
        leading = lax.slice_in_dim(shard, 0, width, axis=dim)
        before = lax.ppermute(last, axis, up)
        after = lax.ppermute(leading, axis, down)
        shard = jnp.concatenate([before, shard, after], axis=dim)
    return shard


def rms_scale(values, gain):
    return values * lax.rsqrt(jnp.mean(values * values, -1, keepdims=True) + NORM_EPS) * gain


def gated_unit(gate_act, up_act):
    return jax.nn.gelu(gate_act, approximate=True) * up_act


def segment_of(places, ends):
    return jnp.sum((places[:, None] >= ends[None, :]).astype(jnp.int32), 1)


def offset_in(places, segs, ends, seq_lengths):
    starts = ends - seq_lengths
    picks = segs[:, None] == jnp.arange(ends.shape[0], dtype=jnp.int32)[None, :]
    return places - jnp.sum(jnp.where(picks, starts[None, :], 0), 1)


def gbst_mix(byte_ext, valid_ext, seg_ext, rel_ext, embed_t, conv_w, conv_b, scorer_v):
    width_ext = byte_ext.shape[0]
    byte_count = width_ext - 10
    onehot = (byte_ext[:, None] == jnp.arange(embed_t.shape[0], dtype=jnp.int32)[None, :]).astype(
        jnp.float32
    )
    onehot = onehot * valid_ext[:, None]
    embedded = jnp.dot(onehot, embed_t, precision=PRECISE)
    conv_span = width_ext - 3
    conv_out = conv_b[None, :] + sum(
        (
            conv_w[tap][None, :]
            * embedded[tap : tap + conv_span]
            * (seg_ext[tap : tap + conv_span] == seg_ext[1 : 1 + conv_span]).astype(jnp.float32)[
                :, None
            ]
            for tap in range(4)
        )
    )
    conv_out = conv_out * valid_ext[1 : 1 + conv_span, None]
    own_seg = seg_ext[5 : 5 + byte_count]
    own_rel = rel_ext[5 : 5 + byte_count]
    pooled_list = []
    for block_size in (1, 2, 3, 4):
        pooled = jnp.zeros((byte_count, embed_t.shape[1]), jnp.float32)
        for shift_by in range(1 - block_size, block_size):
            same = (seg_ext[5 + shift_by : 5 + shift_by + byte_count] == own_seg) & (
                (own_rel + shift_by) // block_size == own_rel // block_size
            )
            weight = jnp.where(same, 1.0 / block_size, 0.0).astype(jnp.float32)
            pooled = pooled + weight[:, None] * conv_out[4 + shift_by : 4 + shift_by + byte_count]
        pooled_list.append(pooled)
    stacked = jnp.stack(pooled_list)
    logits = jnp.einsum("bnd,d->bn", stacked, scorer_v, precision=PRECISE)
    choose = jax.nn.softmax(logits, 0)
    chosen = jnp.sum(choose[..., None] * stacked, 0)
    return chosen.reshape(byte_count // 2, 2, -1).mean(1)


def block_scores(q_heads, key_block, q_seg, key_seg_row):
    scores = jnp.einsum("qhd,khd->hqk", q_heads, key_block, preferred_element_type=jnp.float32)
    same = q_seg[None, :, None] == key_seg_row[None, None, :]
    return jnp.where(same, scores, NEG_FILL)


def softmax_totals(q_heads, q_seg, key_blocks, seg_blocks):
    row_count, head_count = (q_heads.shape[0], q_heads.shape[1])

    def softmax_block_step(state_pair, block_item):
        top_score, exp_total = state_pair
        key_block, seg_row = block_item
        scores = block_scores(q_heads, key_block, q_seg, seg_row)
        new_top = jnp.maximum(top_score, jnp.max(scores, -1))
        exp_total = exp_total * jnp.exp(top_score - new_top) + jnp.sum(
            jnp.exp(scores - new_top[..., None]), -1
        )
        return ((new_top, exp_total), None)

    initial = (
        jnp.full((head_count, row_count), NEG_FILL, jnp.float32),
        jnp.zeros((head_count, row_count), jnp.float32),
    )
    (top_score, exp_total), _ = lax.scan(softmax_block_step, initial, (key_blocks, seg_blocks))
    return top_score + jnp.log(exp_total)


def weighted_values(q_heads, q_seg, key_blocks, value_blocks, seg_blocks, log_total):

    def weighted_block_step(running, block_item):
        key_block, value_block, seg_row = block_item
        attn_probs = jnp.exp(
            block_scores(q_heads, key_block, q_seg, seg_row) - log_total[..., None]
        )
        running = running + jnp.einsum(
            "hqk,khd->qhd",
            attn_probs.astype(jnp.bfloat16),
            value_block,
            preferred_element_type=jnp.float32,
        )
        return (running, None)

    running, _ = lax.scan(
        weighted_block_step,
        jnp.zeros(q_heads.shape, jnp.float32),
        (key_blocks, value_blocks, seg_blocks),
    )
    return running


def attention_back(q_heads, q_seg, key_blocks, value_blocks, seg_blocks, log_total, grad_heads):

    def inner_step(running, block_item):
        key_block, value_block, seg_row = block_item
        attn_probs = jnp.exp(
            block_scores(q_heads, key_block, q_seg, seg_row) - log_total[..., None]
        )
        grad_probs = jnp.einsum(
            "qhd,khd->hqk", grad_heads, value_block, preferred_element_type=jnp.float32
        )
        return (running + jnp.sum(attn_probs * grad_probs, -1), None)

    inner_sum, _ = lax.scan(
        inner_step, jnp.zeros(log_total.shape, jnp.float32), (key_blocks, value_blocks, seg_blocks)
    )

    def grad_step(running, block_item):
        key_block, value_block, seg_row = block_item
        attn_probs = jnp.exp(
            block_scores(q_heads, key_block, q_seg, seg_row) - log_total[..., None]
        )
        grad_probs = jnp.einsum(
            "qhd,khd->hqk", grad_heads, value_block, preferred_element_type=jnp.float32
        )
        grad_scores = (attn_probs * (grad_probs - inner_sum[..., None])).astype(jnp.bfloat16)
        running = running + jnp.einsum(
            "hqk,khd->qhd", grad_scores, key_block, preferred_element_type=jnp.float32
        )
        grad_key = jnp.einsum(
            "hqk,qhd->khd", grad_scores, q_heads, preferred_element_type=jnp.float32
        )
        grad_value = jnp.einsum(
            "hqk,qhd->khd",
            attn_probs.astype(jnp.bfloat16),
            grad_heads,
            preferred_element_type=jnp.float32,
        )
        return (running, (grad_key, grad_value))

    grad_query, key_parts = lax.scan(
        grad_step, jnp.zeros(q_heads.shape, jnp.float32), (key_blocks, value_blocks, seg_blocks)
    )
    grad_key, grad_value = key_parts
    merged = grad_key.shape[2] * grad_key.shape[3]
    return (grad_query, inner_sum, grad_key.reshape(-1, merged), grad_value.reshape(-1, merged))


def layer_forward(stream_in, weights, masks):
    gain_attn, w_query, w_key, w_value, w_out, gain_ffn, w_gate, w_up, w_down = weights
    q_seg, tok_seg, seg_blocks = masks
    row_count = stream_in.shape[0]
    normed = rms_scale(stream_in, gain_attn.astype(jnp.float32)).astype(jnp.bfloat16)
    query_act = jnp.dot(normed, w_query, preferred_element_type=jnp.float32).astype(jnp.bfloat16)
    key_act = jnp.dot(normed, w_key, preferred_element_type=jnp.float32).astype(jnp.bfloat16)
    value_act = jnp.dot(normed, w_value, preferred_element_type=jnp.float32).astype(jnp.bfloat16)
    key_all, value_all = (
        lax.all_gather(key_act, "ctx", axis=0, tiled=True),
        lax.all_gather(value_act, "ctx", axis=0, tiled=True),
    )
    block_count, block_rows = seg_blocks.shape
    q_heads = query_act.reshape(row_count, HEADS, HEAD_DIM)
    key_own = key_act.reshape(row_count, HEADS, HEAD_DIM)
    value_own = value_act.reshape(row_count, HEADS, HEAD_DIM)
    key_blocks = key_all.reshape(block_count, block_rows, HEADS, HEAD_DIM)
    value_blocks = value_all.reshape(block_count, block_rows, HEADS, HEAD_DIM)
    log_total = softmax_totals(q_heads, q_seg, key_blocks, seg_blocks)
    attended = weighted_values(q_heads, q_seg, key_blocks, value_blocks, seg_blocks, log_total)
    attended = attended.reshape(row_count, -1).astype(jnp.bfloat16)
    middle = stream_in + jnp.dot(attended, w_out, preferred_element_type=jnp.float32)
    normed_ffn = rms_scale(middle, gain_ffn.astype(jnp.float32)).astype(jnp.bfloat16)
    gate_act = jnp.dot(normed_ffn, w_gate, preferred_element_type=jnp.float32)
    up_act = jnp.dot(normed_ffn, w_up, preferred_element_type=jnp.float32)
    hidden = gated_unit(gate_act, up_act).astype(jnp.bfloat16)
    result = middle + jnp.dot(hidden, w_down, preferred_element_type=jnp.float32)
    saved = (
        normed,
        q_heads,
        key_own,
        value_own,
        key_blocks,
        value_blocks,
        log_total,
        attended,
        middle,
        normed_ffn,
        gate_act,
        up_act,
        hidden,
    )
    return (result, saved)


def layer_backward(stream_in, weights, masks, grad_out):
    gain_attn, w_query, w_key, w_value, w_out, gain_ffn, w_gate, w_up, w_down = weights
    q_seg, tok_seg, seg_blocks = masks
    _, saved = layer_forward(stream_in, weights, masks)
    (
        normed,
        q_heads,
        key_own,
        value_own,
        key_blocks,
        value_blocks,
        log_total,
        attended,
        middle,
        normed_ffn,
        gate_act,
        up_act,
        hidden,
    ) = saved
    row_count = stream_in.shape[0]
    grad_f = grad_out.astype(jnp.bfloat16)
    d_down = jnp.dot(hidden.T, grad_f, preferred_element_type=jnp.float32)
    grad_hidden = jnp.dot(grad_f, w_down.T, preferred_element_type=jnp.float32)
    _, gated_back = jax.vjp(gated_unit, gate_act, up_act)
    grad_gate, grad_up = gated_back(grad_hidden)
    grad_gate = grad_gate.astype(jnp.bfloat16)
    grad_up = grad_up.astype(jnp.bfloat16)
    d_gate = jnp.dot(normed_ffn.T, grad_gate, preferred_element_type=jnp.float32)
    d_up = jnp.dot(normed_ffn.T, grad_up, preferred_element_type=jnp.float32)
    grad_nffn = jnp.dot(grad_gate, w_gate.T, preferred_element_type=jnp.float32) + jnp.dot(
        grad_up, w_up.T, preferred_element_type=jnp.float32
    )
    _, norm_back = jax.vjp(rms_scale, middle, gain_ffn.astype(jnp.float32))
    grad_mid, d_gain_ffn = norm_back(grad_nffn)
    grad_mid = grad_mid + grad_out
    grad_att = grad_mid.astype(jnp.bfloat16)
    d_out = jnp.dot(attended.T, grad_att, preferred_element_type=jnp.float32)
    grad_heads = jnp.dot(grad_att, w_out.T, preferred_element_type=jnp.float32).astype(jnp.bfloat16)
    grad_heads = grad_heads.reshape(row_count, HEADS, HEAD_DIM)
    grad_query, inner_sum, grad_key_all, grad_value_all = attention_back(
        q_heads, q_seg, key_blocks, value_blocks, seg_blocks, log_total, grad_heads
    )
    grad_key, grad_value = (
        lax.psum_scatter(
            grad_key_all.astype(jnp.bfloat16), "ctx", scatter_dimension=0, tiled=True
        ).astype(jnp.float32),
        lax.psum_scatter(
            grad_value_all.astype(jnp.bfloat16), "ctx", scatter_dimension=0, tiled=True
        ).astype(jnp.float32),
    )
    grad_query = grad_query.reshape(row_count, -1).astype(jnp.bfloat16)
    grad_key = grad_key.astype(jnp.bfloat16)
    grad_value = grad_value.astype(jnp.bfloat16)
    d_query = jnp.dot(normed.T, grad_query, preferred_element_type=jnp.float32)
    d_key = jnp.dot(normed.T, grad_key, preferred_element_type=jnp.float32)
    d_value = jnp.dot(normed.T, grad_value, preferred_element_type=jnp.float32)
    grad_normed = (
        jnp.dot(grad_query, w_query.T, preferred_element_type=jnp.float32)
        + jnp.dot(grad_key, w_key.T, preferred_element_type=jnp.float32)
        + jnp.dot(grad_value, w_value.T, preferred_element_type=jnp.float32)
    )
    _, first_back = jax.vjp(rms_scale, stream_in, gain_attn.astype(jnp.float32))
    grad_in, d_gain_attn = first_back(grad_normed)
    grad_in = grad_in + grad_mid
    return (
        grad_in,
        (d_gain_attn, d_query, d_key, d_value, d_out, d_gain_ffn, d_gate, d_up, d_down),
    )


def on_device(
    byte_ids,
    lengths,
    embed,
    conv_weight,
    conv_bias,
    scorer,
    norm_attn,
    query_w,
    key_w,
    value_w,
    attn_out_w,
    norm_ffn,
    gate_w,
    up_w,
    down_w,
    out_grad,
):
    ctx_count = lax.axis_size("ctx")
    ctx_place = lax.axis_index("ctx")
    byte_count = byte_ids.shape[1]
    tok_count = byte_count // 2
    seq_lengths = lengths[0]
    ends = jnp.cumsum(seq_lengths)
    total_bytes = ends[-1]
    first_byte = ctx_place * byte_count
    byte_ext = padded(byte_ids[0], (("ctx", 0),), 5)
    ext_places = first_byte - 5 + jnp.arange(byte_count + 10, dtype=jnp.int32)
    valid_ext = ((ext_places >= 0) & (ext_places < total_bytes)).astype(jnp.float32)
    seg_ext = segment_of(ext_places, ends)
    rel_ext = offset_in(ext_places, seg_ext, ends, seq_lengths)
    group_tok = tok_count * ctx_count
    block_rows = min(512, group_tok)
    tok_seg = segment_of(2 * jnp.arange(group_tok, dtype=jnp.int32), ends)
    q_seg = segment_of(first_byte + 2 * jnp.arange(tok_count, dtype=jnp.int32), ends)
    seg_blocks = tok_seg.reshape(group_tok // block_rows, block_rows)
    masks = (q_seg, tok_seg, seg_blocks)
    embed_full, conv_full, bias_full, scorer_full = (
        lax.all_gather(embed, ("dp", "ctx"), axis=1, tiled=True),
        lax.all_gather(conv_weight, ("dp", "ctx"), axis=1, tiled=True),
        lax.all_gather(conv_bias, ("dp", "ctx"), axis=0, tiled=True),
        lax.all_gather(scorer, ("dp", "ctx"), axis=0, tiled=True),
    )

    def gbst_local(embed_t, conv_w, conv_b, scorer_v):
        return gbst_mix(byte_ext, valid_ext, seg_ext, rel_ext, embed_t, conv_w, conv_b, scorer_v)

    stream, gbst_back = jax.vjp(
        gbst_local,
        embed_full.astype(jnp.float32),
        conv_full.astype(jnp.float32),
        bias_full.astype(jnp.float32),
        scorer_full.astype(jnp.float32),
    )
    layer_count = query_w.shape[0]
    kept_weights = []
    inputs = []
    for layer_index in range(layer_count):
        weights = (
            lax.all_gather(norm_attn[layer_index], ("dp", "ctx"), axis=0, tiled=True),
            lax.all_gather(query_w[layer_index], ("dp", "ctx"), axis=0, tiled=True),
            lax.all_gather(key_w[layer_index], ("dp", "ctx"), axis=0, tiled=True),
            lax.all_gather(value_w[layer_index], ("dp", "ctx"), axis=0, tiled=True),
            lax.all_gather(attn_out_w[layer_index], ("dp", "ctx"), axis=0, tiled=True),
            lax.all_gather(norm_ffn[layer_index], ("dp", "ctx"), axis=0, tiled=True),
            lax.all_gather(gate_w[layer_index], ("dp", "ctx"), axis=0, tiled=True),
            lax.all_gather(up_w[layer_index], ("dp", "ctx"), axis=0, tiled=True),
            lax.all_gather(down_w[layer_index], ("dp", "ctx"), axis=0, tiled=True),
        )
        kept_weights.append(weights)
        inputs.append(stream)
        stream, _ = layer_forward(stream, weights, masks)
    encoded = stream.astype(jnp.bfloat16)[None]
    grad_stream = out_grad[0].astype(jnp.float32)
    collected = [[] for _ in range(9)]
    for layer_index in reversed(range(layer_count)):
        weights = (
            lax.all_gather(norm_attn[layer_index], ("dp", "ctx"), axis=0, tiled=True),
            lax.all_gather(query_w[layer_index], ("dp", "ctx"), axis=0, tiled=True),
            lax.all_gather(key_w[layer_index], ("dp", "ctx"), axis=0, tiled=True),
            lax.all_gather(value_w[layer_index], ("dp", "ctx"), axis=0, tiled=True),
            lax.all_gather(attn_out_w[layer_index], ("dp", "ctx"), axis=0, tiled=True),
            lax.all_gather(norm_ffn[layer_index], ("dp", "ctx"), axis=0, tiled=True),
            lax.all_gather(gate_w[layer_index], ("dp", "ctx"), axis=0, tiled=True),
            lax.all_gather(up_w[layer_index], ("dp", "ctx"), axis=0, tiled=True),
            lax.all_gather(down_w[layer_index], ("dp", "ctx"), axis=0, tiled=True),
        )
        grad_stream, partial_grads = layer_backward(
            inputs[layer_index], weights, masks, grad_stream
        )
        shards = (
            lax.psum_scatter(partial_grads[0], ("dp", "ctx"), scatter_dimension=0, tiled=True),
            lax.psum_scatter(partial_grads[1], ("dp", "ctx"), scatter_dimension=0, tiled=True),
            lax.psum_scatter(partial_grads[2], ("dp", "ctx"), scatter_dimension=0, tiled=True),
            lax.psum_scatter(partial_grads[3], ("dp", "ctx"), scatter_dimension=0, tiled=True),
            lax.psum_scatter(partial_grads[4], ("dp", "ctx"), scatter_dimension=0, tiled=True),
            lax.psum_scatter(partial_grads[5], ("dp", "ctx"), scatter_dimension=0, tiled=True),
            lax.psum_scatter(partial_grads[6], ("dp", "ctx"), scatter_dimension=0, tiled=True),
            lax.psum_scatter(partial_grads[7], ("dp", "ctx"), scatter_dimension=0, tiled=True),
            lax.psum_scatter(partial_grads[8], ("dp", "ctx"), scatter_dimension=0, tiled=True),
        )
        for position in range(9):
            collected[position].append(shards[position])
    stacked = [jnp.stack(column[::-1]) for column in collected]
    grad_embed_t, grad_conv_w, grad_conv_b, grad_scorer_v = gbst_back(grad_stream)
    grad_embed, grad_conv_weight, grad_conv_bias, grad_scorer = (
        lax.psum_scatter(grad_embed_t, ("dp", "ctx"), scatter_dimension=1, tiled=True),
        lax.psum_scatter(grad_conv_w, ("dp", "ctx"), scatter_dimension=1, tiled=True),
        lax.psum_scatter(grad_conv_b, ("dp", "ctx"), scatter_dimension=0, tiled=True),
        lax.psum_scatter(grad_scorer_v, ("dp", "ctx"), scatter_dimension=0, tiled=True),
    )
    return (
        encoded,
        grad_embed,
        grad_conv_weight,
        grad_conv_bias,
        grad_scorer,
        stacked[0],
        stacked[1],
        stacked[2],
        stacked[3],
        stacked[4],
        stacked[5],
        stacked[6],
        stacked[7],
        stacked[8],
    )


def solution(mesh):
    placed = (
        P("dp", "ctx"),
        P("dp", None),
        P(None, ("dp", "ctx")),
        P(None, ("dp", "ctx")),
        P(("dp", "ctx")),
        P(("dp", "ctx")),
        P(None, ("dp", "ctx")),
        P(None, ("dp", "ctx"), None),
        P(None, ("dp", "ctx"), None),
        P(None, ("dp", "ctx"), None),
        P(None, ("dp", "ctx"), None),
        P(None, ("dp", "ctx")),
        P(None, ("dp", "ctx"), None),
        P(None, ("dp", "ctx"), None),
        P(None, ("dp", "ctx"), None),
        P("dp", "ctx", None),
    )
    return jax.shard_map(
        on_device,
        mesh=mesh,
        in_specs=placed,
        out_specs=(
            P("dp", "ctx", None),
            P(None, ("dp", "ctx")),
            P(None, ("dp", "ctx")),
            P(("dp", "ctx")),
            P(("dp", "ctx")),
            P(None, ("dp", "ctx")),
            P(None, ("dp", "ctx"), None),
            P(None, ("dp", "ctx"), None),
            P(None, ("dp", "ctx"), None),
            P(None, ("dp", "ctx"), None),
            P(None, ("dp", "ctx")),
            P(None, ("dp", "ctx"), None),
            P(None, ("dp", "ctx"), None),
            P(None, ("dp", "ctx"), None),
        ),
        check_vma=False,
    )
```

profile of v0, /device:TPU:0, one launch (start us, length us, event | category | flops | bytes accessed | tf_op | source)
XLA Modules:
  0.0 2895.2 jit_solution(12849660721864131915)
XLA Ops:
  12.2 5.5 collective-permute-start
  25.3 40.8 %all-reduce.38 = (bf16[768]{0:T(1024)(128)(2,1)S(1)}, bf16[768]{0:T(1024)(128)(2,1)S(1)}, bf16[768]{0:T(1024)(128)(2,1)S(1)}, bf16[768]{0:T(1024)(128)(2,1)S(1)}...) all-reduce(bf16[768]{0:T(1024)(128)(2,1)S(1)} %dynamic-update-slice, ...), channel_id=1, replica_groups=mesh['dp'=8,'ctx'=4] {'dp','ctx'}, use_global_device_ids=true, to_apply=%add.25 | all-reduce | flops 4608 | bytes 18432
  66.6 68.9 %all_gather.102 = bf16[256,768]{0,1:T(8,128)(2,1)S(1)} all-gather(bf16[256,24]{0,1:T(8,128)(2,1)} %param.34), channel_id=1, replica_groups=mesh['dp'=8,'ctx'=4] {'dp','ctx'}, dimensions={1}, use_global_device_ids=true | all-gather | bytes 405504 | tf_op jit(solution)/shard_map/all_gather | solution.py:335
  136.4 64.0 %all-gather.18 = bf16[32,24,4]{1,2,0:T(4,128)(2,1)S(1)} all-gather(bf16[1,24,4]{1,2,0:T(4,128)(2,1)} %bitcast.700), channel_id=1, replica_groups=mesh['dp'=8,'ctx'=4] {'dp','ctx'}, dimensions={0}, use_global_device_ids=true | all-gather | bytes 6336 | tf_op jit(solution)/shard_map/all_gather | solution.py:336
  230.2 17.8 all-gather.40.cloned.1.call-done
  253.9 15.7 while.118
  257.8 4.0 exponential_reduce_fusion.4
  265.7 3.9 exponential_reduce_fusion.4
  269.6 11.7 all-gather.38.cloned.1.call-done
  283.9 3.9 reshape.549
  290.7 8.6 while.119
  290.9 4.0 fusion.458
  295.0 4.2 fusion.458
  301.0 37.1 %all-gather.52.cloned.1.call-done = bf16[1,768,768]{2,1,0:T(8,128)(2,1)} async-done(((bf16[1,24,768]{2,1,0:T(8,128)(2,1)}), bf16[1,768,768]{2,1,0:T(8,128)(2,1)}) %all-gather.52.cloned.1.call-update) | async-done | bytes 1179664 | tf_op jit(solution)/shard_map/all_gather | solution.py:360
  341.1 58.5 %all-gather.54.cloned.1.call-done = bf16[1,768,2048]{2,1,0:T(8,128)(2,1)} async-done(((bf16[1,24,2048]{2,1,0:T(8,128)(2,1)}), bf16[1,768,2048]{2,1,0:T(8,128)(2,1)}) %all-gather.54.cloned.1.call-update) | async-done | bytes 3145744 | tf_op jit(solution)/shard_map/all_gather | solution.py:362
  399.6 4.3 fusion.150
  403.9 57.1 %all-gather.56.cloned.1.call-done = bf16[1,768,2048]{2,1,0:T(8,128)(2,1)} async-done(((bf16[1,24,2048]{2,1,0:T(8,128)(2,1)}), bf16[1,768,2048]{2,1,0:T(8,128)(2,1)}) %all-gather.56.cloned.1.call-update) | async-done | bytes 3145744 | tf_op jit(solution)/shard_map/all_gather | solution.py:363
  461.0 5.0 multiply_convert_fusion.3
  466.1 56.3 %all-gather.58.cloned.1.call-done = bf16[1,2048,768]{2,1,0:T(8,128)(2,1)} async-done(((bf16[1,64,768]{2,1,0:T(8,128)(2,1)}), bf16[1,2048,768]{2,1,0:T(8,128)(2,1)}) %all-gather.58.cloned.1.call-update) | async-done | bytes 3145744 | tf_op jit(solution)/shard_map/all_gather | solution.py:364
  525.5 52.5 %all-gather.60.cloned.1.call-done = bf16[1,768,768]{2,1,0:T(8,128)(2,1)} async-done(((bf16[1,24,768]{2,1,0:T(8,128)(2,1)}), bf16[1,768,768]{2,1,0:T(8,128)(2,1)}) %all-gather.60.cloned.1.call-update) | async-done | bytes 1179664 | tf_op jit(solution)/shard_map/all_gather | solution.py:359
  580.6 53.3 %all-gather.62.cloned.1.call-done = bf16[1,768,768]{2,1,0:T(8,128)(2,1)} async-done(((bf16[1,24,768]{2,1,0:T(8,128)(2,1)}), bf16[1,768,768]{2,1,0:T(8,128)(2,1)}) %all-gather.62.cloned.1.call-update) | async-done | bytes 1179664 | tf_op jit(solution)/shard_map/all_gather | solution.py:358
  638.4 51.4 %all-gather.64.cloned.1.call-done = bf16[1,768,768]{2,1,0:T(8,128)(2,1)} async-done(((bf16[1,24,768]{2,1,0:T(8,128)(2,1)}), bf16[1,768,768]{2,1,0:T(8,128)(2,1)}) %all-gather.64.cloned.1.call-update) | async-done | bytes 1179664 | tf_op jit(solution)/shard_map/all_gather | solution.py:357
  691.7 59.0 %all-gather.72.cloned.1.call-done = bf16[1,2048,768]{2,1,0:T(8,128)(2,1)} async-done(((bf16[1,64,768]{2,1,0:T(8,128)(2,1)}), bf16[1,2048,768]{2,1,0:T(8,128)(2,1)}) %all-gather.72.cloned.1.call-update) | async-done | bytes 3145744 | tf_op jit(solution)/shard_map/all_gather | solution.py:364
  750.7 4.3 fusion.128
  754.9 27.8 all-gather.42.cloned.1.call-done
  789.9 26.1 all-gather.44.cloned.1.call-done
  821.9 15.6 while.120
  825.8 3.9 exponential_reduce_fusion.5
  833.6 3.9 exponential_reduce_fusion.5
  837.6 8.7 while.121
  837.7 4.0 fusion.466
  842.0 4.3 fusion.466
  848.2 24.7 all-gather.66.cloned.1.call-done
  875.6 58.6 %all-gather.70.cloned.1.call-done = bf16[1,768,2048]{2,1,0:T(8,128)(2,1)} async-done(((bf16[1,24,2048]{2,1,0:T(8,128)(2,1)}), bf16[1,768,2048]{2,1,0:T(8,128)(2,1)}) %all-gather.70.cloned.1.call-update) | async-done | bytes 3145744 | tf_op jit(solution)/shard_map/all_gather | solution.py:363
  934.2 4.2 fusion.134
  938.4 57.0 %all-gather.68.cloned.1.call-done = bf16[1,768,2048]{2,1,0:T(8,128)(2,1)} async-done(((bf16[1,24,2048]{2,1,0:T(8,128)(2,1)}), bf16[1,768,2048]{2,1,0:T(8,128)(2,1)}) %all-gather.68.cloned.1.call-update) | async-done | bytes 3145744 | tf_op jit(solution)/shard_map/all_gather | solution.py:362
  995.4 6.2 fusion.165
  1008.9 6.7 while.122
  1018.2 24.9 while.123
  1054.3 23.4 reduce-scatter.21.cloned.1.call-done
  1079.8 31.6 %reduce-scatter.23.cloned.1.call-done = bf16[256,768]{0,1:T(8,128)(2,1)} async-done(((bf16[1024,768]{0,1:T(8,128)(2,1)}), bf16[256,768]{0,1:T(8,128)(2,1)}) %reduce-scatter.23.cloned.1.call-update) | async-done | bytes 393232 | tf_op jit(solution)/shard_map/reduce_scatter | solution.py:273
  1126.6 10.5 while.124
  1139.8 29.4 %while.125 = (s32[]{:T(128)}, f32[256,12,64]{0,2,1:T(8,128)}, bf16[2,512,12,64]{1,3,2,0:T(8,128)(2,1)}, bf16[2,512,12,64]{1,3,2,0:T(8,128)(2,1)}, bf16[2,512,12,...) while((s32[]{:T(128)}, f32[256,12,64]{0,2,1:T(8,128)}, ...), condition=%wide.region_39.40_spmd.clone, body=%wide.region_38.39_spmd.clone.sunk | while | flops 1019740160 | bytes 111005232 | solution.py:174
  1192.5 12.4 reduce-scatter.25.cloned.1.call-done
  1210.8 28.0 reduce-scatter.27.cloned.1.call-done
  1273.3 3.8 fusion.199
  1282.7 3.8 reshape.558
  1297.6 8.3 multiply_reduce_fusion.5
  1309.2 40.5 %all-reduce.37 = (f32[4,768]{1,0:T(4,128)S(1)}, f32[768]{0:T(1024)S(1)}, f32[768]{0:T(1024)S(1)}, f32[768]{0:T(1024)S(1)}, f32[768]{0:T(1024)S(1)}, /*index=5*/f32[768]{0:T(1024)S(1)}, f32[768]{0:T(1024)S(1)}) all-reduce(f32[4,768]{1,0:T(4,128)S(1)} %pad_add_fusion, ...), channel_id=25, replica_groups=mesh['dp'=8,'ctx'=4] {'dp','ctx'}, use_global_device_ids=true, to_apply=%region_50.51.clone | all-reduce | flops 7680 | bytes 61440
  1353.5 4.5 fusion.166
  1358.7 88.7 %reduce-scatter.31.cloned.1.call-done = f32[24,768]{1,0:T(8,128)} async-done(((f32[768,768]{1,0:T(8,128)}), f32[24,768]{1,0:T(8,128)}) %reduce-scatter.31.cloned.1.call-update) | async-done | bytes 73744 | tf_op jit(solution)/shard_map/reduce_scatter | solution.py:389
  1449.7 101.2 %reduce-scatter.45.cloned.1.call-done = f32[24,768]{1,0:T(8,128)} async-done(((f32[768,768]{1,0:T(8,128)}), f32[24,768]{1,0:T(8,128)}) %reduce-scatter.45.cloned.1.call-update) | async-done | bytes 73744 | tf_op jit(solution)/shard_map/reduce_scatter | solution.py:392
  1550.9 104.0 %reduce-scatter.43.cloned.1.call-done = f32[24,768]{1,0:T(8,128)} async-done(((f32[768,768]{1,0:T(8,128)}), f32[24,768]{1,0:T(8,128)}) %reduce-scatter.43.cloned.1.call-update) | async-done | bytes 73744 | tf_op jit(solution)/shard_map/reduce_scatter | solution.py:392
  1656.5 101.8 %reduce-scatter.37.cloned.1.call-done = f32[24,768]{1,0:T(8,128)} async-done(((f32[768,768]{1,0:T(8,128)}), f32[24,768]{1,0:T(8,128)}) %reduce-scatter.37.cloned.1.call-update) | async-done | bytes 73744 | tf_op jit(solution)/shard_map/reduce_scatter | solution.py:390
  1758.2 104.1 %reduce-scatter.35.cloned.1.call-done = f32[24,768]{1,0:T(8,128)} async-done(((f32[768,768]{1,0:T(8,128)}), f32[24,768]{1,0:T(8,128)}) %reduce-scatter.35.cloned.1.call-update) | async-done | bytes 73744 | tf_op jit(solution)/shard_map/reduce_scatter | solution.py:390
  1863.9 101.8 %reduce-scatter.41.cloned.1.call-done = f32[24,768]{1,0:T(8,128)} async-done(((f32[768,768]{1,0:T(8,128)}), f32[24,768]{1,0:T(8,128)}) %reduce-scatter.41.cloned.1.call-update) | async-done | bytes 73744 | tf_op jit(solution)/shard_map/reduce_scatter | solution.py:391
  1965.7 104.1 %reduce-scatter.39.cloned.1.call-done = f32[24,768]{1,0:T(8,128)} async-done(((f32[768,768]{1,0:T(8,128)}), f32[24,768]{1,0:T(8,128)}) %reduce-scatter.39.cloned.1.call-update) | async-done | bytes 73744 | tf_op jit(solution)/shard_map/reduce_scatter | solution.py:391
  2071.4 117.5 %reduce-scatter.57.cloned.1.call-done = f32[64,768]{1,0:T(8,128)} async-done(((f32[2048,768]{1,0:T(8,128)}), f32[64,768]{1,0:T(8,128)}) %reduce-scatter.57.cloned.1.call-update) | async-done | bytes 196624 | tf_op jit(solution)/shard_map/reduce_scatter | solution.py:396
  2188.8 120.4 %reduce-scatter.55.cloned.1.call-done = f32[64,768]{1,0:T(8,128)} async-done(((f32[2048,768]{1,0:T(8,128)}), f32[64,768]{1,0:T(8,128)}) %reduce-scatter.55.cloned.1.call-update) | async-done | bytes 196624 | tf_op jit(solution)/shard_map/reduce_scatter | solution.py:396
  2311.0 117.2 %reduce-scatter.49.cloned.1.call-done = f32[24,2048]{1,0:T(8,128)} async-done(((f32[768,2048]{1,0:T(8,128)}), f32[24,2048]{1,0:T(8,128)}) %reduce-scatter.49.cloned.1.call-update) | async-done | bytes 196624 | tf_op jit(solution)/shard_map/reduce_scatter | solution.py:394
  2428.2 120.2 %reduce-scatter.47.cloned.1.call-done = f32[24,2048]{1,0:T(8,128)} async-done(((f32[768,2048]{1,0:T(8,128)}), f32[24,2048]{1,0:T(8,128)}) %reduce-scatter.47.cloned.1.call-update) | async-done | bytes 196624 | tf_op jit(solution)/shard_map/reduce_scatter | solution.py:394
  2550.2 117.6 %reduce-scatter.53.cloned.1.call-done = f32[24,2048]{1,0:T(8,128)} async-done(((f32[768,2048]{1,0:T(8,128)}), f32[24,2048]{1,0:T(8,128)}) %reduce-scatter.53.cloned.1.call-update) | async-done | bytes 196624 | tf_op jit(solution)/shard_map/reduce_scatter | solution.py:395
  2667.9 120.0 %reduce-scatter.51.cloned.1.call-done = f32[24,2048]{1,0:T(8,128)} async-done(((f32[768,2048]{1,0:T(8,128)}), f32[24,2048]{1,0:T(8,128)}) %reduce-scatter.51.cloned.1.call-update) | async-done | bytes 196624 | tf_op jit(solution)/shard_map/reduce_scatter | solution.py:395
  2789.7 98.5 %reduce-scatter.29.cloned.1.call-done = f32[256,24]{0,1:T(8,128)} async-done(((f32[256,768]{0,1:T(8,128)}), f32[256,24]{0,1:T(8,128)}) %reduce-scatter.29.cloned.1.call-update) | async-done | bytes 24592 | tf_op jit(solution)/shard_map/reduce_scatter | solution.py:403
  (808 shorter events, 315.2 us)
Async XLA Ops:
  7.2 209.1 %all-gather.48.cloned.1.call-start = ((), (), s32[]{:S(2)}) async-start(), calls=%async_computation.43 | async-start | bytes 1216512 | tf_op jit(solution)/shard_map/all_gather | solution.py:358
  8.7 210.4 %all-gather.46.cloned.1.call-start = ((), (), s32[]{:S(2)}) async-start(), calls=%async_computation.42 | async-start | bytes 1216512 | tf_op jit(solution)/shard_map/all_gather | solution.py:359
  10.2 218.1 %all-gather.50.cloned.1.call-start = ((), (), s32[]{:S(2)}) async-start(), calls=%async_computation.44 | async-start | bytes 1216512 | tf_op jit(solution)/shard_map/all_gather | solution.py:357
  11.0 190.3 %collective-permute-start.1 = (s32[5]{0:T(128)S(1)}, s32[5]{0:T(128)S(1)}, u32[]{:S(2)}, u32[]{:S(2)}) collective-permute-start(s32[5]{0:T(128)S(1)} %get-tuple-element.1391), channel_id=1, source_target_pairs={{1,0},{2,1},{3,2},{5,4},{6,5},{7,6},{9,8},{10,9},{11,10},{13,12},{... | collective-permute-start | bytes 68 | tf_op jit(solution)/shard_map/ppermute | solution.py:23
  12.2 189.0 %collective-permute-start = (s32[5]{0:T(128)S(1)}, s32[5]{0:T(128)S(1)}, u32[]{:S(2)}, u32[]{:S(2)}) collective-permute-start(s32[5]{0:T(128)S(1)} %get-tuple-element.1390), channel_id=1, source_target_pairs={{0,1},{1,2},{2,3},{4,5},{5,6},{6,7},{8,9},{9,10},{10,11},{12,13},{... | collective-permute-start | bytes 68 | tf_op jit(solution)/shard_map/ppermute | solution.py:22
  19.2 228.9 %all-gather.40.cloned.1.call-start = ((), (), s32[]{:S(2)}) async-start(), calls=%async_computation.20 | async-start | bytes 1966080 | tf_op jit(solution)/shard_map/all_gather | solution.py:191
  136.1 67.8 %copy-start.125 = (f32[522]{0:T(1024)}, f32[522]{0:T(1024)S(1)}, u32[]{:S(2)}) copy-start(f32[522]{0:T(1024)S(1)} %fusion.264) | copy-start | bytes 6268
  136.2 67.7 %copy-start.139 = (f32[519]{0:T(1024)}, f32[519]{0:T(1024)S(1)}, u32[]{:S(2)}) copy-start(f32[519]{0:T(1024)S(1)} %slice.212) | copy-start | bytes 6232
  136.4 67.5 %copy-start.115 = (f32[519]{0:T(1024)}, f32[519]{0:T(1024)S(1)}, u32[]{:S(2)}) copy-start(f32[519]{0:T(1024)S(1)} %get-tuple-element.1387) | copy-start | bytes 6232
  136.4 67.6 %copy-start.117 = (f32[519]{0:T(1024)}, f32[519]{0:T(1024)S(1)}, u32[]{:S(2)}) copy-start(f32[519]{0:T(1024)S(1)} %get-tuple-element.1388) | copy-start | bytes 6232
  136.4 67.6 %copy-start.119 = (f32[519]{0:T(1024)}, f32[519]{0:T(1024)S(1)}, u32[]{:S(2)}) copy-start(f32[519]{0:T(1024)S(1)} %get-tuple-element.1389) | copy-start | bytes 6232
  215.3 122.9 %copy-start.11 = (f32[256,768]{1,0:T(8,128)}, f32[256,768]{1,0:T(8,128)S(1)}, u32[]{:S(2)}) copy-start(f32[256,768]{1,0:T(8,128)S(1)} %reduce_sum.274) | copy-start | bytes 2359300
  219.0 62.4 %all-gather.38.cloned.1.call-start = ((), (), s32[]{:S(2)}) async-start(), calls=%async_computation.19 | async-start | bytes 1966080 | tf_op jit(solution)/shard_map/all_gather | solution.py:192
  221.7 116.4 %all-gather.52.cloned.1.call-start = ((), (), s32[]{:S(2)}) async-start(), calls=%async_computation.45 | async-start | bytes 1216512 | tf_op jit(solution)/shard_map/all_gather | solution.py:360
  222.5 177.2 %all-gather.54.cloned.1.call-start = ((), (), s32[]{:S(2)}) async-start(), calls=%async_computation.46 | async-start | bytes 3244032 | tf_op jit(solution)/shard_map/all_gather | solution.py:362
  223.2 237.8 %all-gather.56.cloned.1.call-start = ((), (), s32[]{:S(2)}) async-start(), calls=%async_computation.47 | async-start | bytes 3244032 | tf_op jit(solution)/shard_map/all_gather | solution.py:363
  224.0 298.4 %all-gather.58.cloned.1.call-start = ((), (), s32[]{:S(2)}) async-start(), calls=%async_computation.48 | async-start | bytes 3244032 | tf_op jit(solution)/shard_map/all_gather | solution.py:364
  224.8 353.3 %all-gather.60.cloned.1.call-start = ((), (), s32[]{:S(2)}) async-start(), calls=%async_computation.49 | async-start | bytes 1216512 | tf_op jit(solution)/shard_map/all_gather | solution.py:359
  225.4 408.6 %all-gather.62.cloned.1.call-start = ((), (), s32[]{:S(2)}) async-start(), calls=%async_computation.50 | async-start | bytes 1216512 | tf_op jit(solution)/shard_map/all_gather | solution.py:358
  226.1 463.7 %all-gather.64.cloned.1.call-start = ((), (), s32[]{:S(2)}) async-start(), calls=%async_computation.51 | async-start | bytes 1216512 | tf_op jit(solution)/shard_map/all_gather | solution.py:357
  226.7 524.0 %all-gather.72.cloned.1.call-start = ((), (), s32[]{:S(2)}) async-start(), calls=%async_computation.55 | async-start | bytes 3244032 | tf_op jit(solution)/shard_map/all_gather | solution.py:364
  227.4 555.3 %all-gather.42.cloned.1.call-start = ((), (), s32[]{:S(2)}) async-start(), calls=%async_computation.21 | async-start | bytes 1966080 | tf_op jit(solution)/shard_map/all_gather | solution.py:192
  228.2 111.9 %copy-start.123 = (f32[768]{0:T(1024)}, f32[768]{0:T(1024)S(1)}, u32[]{:S(2)}) copy-start(f32[768]{0:T(1024)S(1)} %convert_element_type.275) | copy-start | bytes 9220
  340.1 63.8 %copy-start.185 = (f32[256]{0:T(256)}, f32[256]{0:T(256)S(1)}, u32[]{:S(2)}) copy-start(f32[256]{0:T(256)S(1)} %get-tuple-element.1398) | copy-start | bytes 3076
  340.1 63.8 %copy-start.177 = (f32[256]{0:T(256)}, f32[256]{0:T(256)S(1)}, u32[]{:S(2)}) copy-start(f32[256]{0:T(256)S(1)} %fusion.302) | copy-start | bytes 3076
  341.1 119.9 %copy-start.41 = (bf16[256,768]{1,0:T(8,128)(2,1)}, bf16[256,768]{1,0:T(8,128)(2,1)S(1)}, u32[]{:S(2)}) copy-start(bf16[256,768]{1,0:T(8,128)(2,1)S(1)} %multiply_convert_fusion.6) | copy-start | bytes 1179652
  403.9 118.5 %copy-start.32 = (f32[256,768]{1,0:T(8,128)S(1)}, f32[256,768]{1,0:T(8,128)}, u32[]{:S(2)}) copy-start(f32[256,768]{1,0:T(8,128)} %copy-done.31) | copy-start | bytes 2359300
  466.0 59.3 %copy-start.80 = (bf16[256,2048]{1,0:T(8,128)(2,1)}, bf16[256,2048]{1,0:T(8,128)(2,1)S(1)}, u32[]{:S(2)}) copy-start(bf16[256,2048]{1,0:T(8,128)(2,1)S(1)} %get-tuple-element.1400) | copy-start | bytes 3145732
  525.3 55.2 %copy-start.194 = (f32[256]{0:T(256)}, f32[256]{0:T(256)S(1)}, u32[]{:S(2)}) copy-start(f32[256]{0:T(256)S(1)} %get-tuple-element.1402) | copy-start | bytes 3076
  525.4 347.5 %copy-start.34 = (f32[256,768]{1,0:T(8,128)}, f32[256,768]{1,0:T(8,128)S(1)}, u32[]{:S(2)}) copy-start(f32[256,768]{1,0:T(8,128)S(1)} %get-tuple-element.1403) | copy-start | bytes 2359300
  525.4 55.2 %copy-start.179 = (f32[256]{0:T(256)}, f32[256]{0:T(256)S(1)}, u32[]{:S(2)}) copy-start(f32[256]{0:T(256)S(1)} %fusion.303) | copy-start | bytes 3076
  525.5 164.2 %copy-start.17 = (bf16[256,768]{1,0:T(8,128)(2,1)}, bf16[256,768]{1,0:T(8,128)(2,1)S(1)}, u32[]{:S(2)}) copy-start(bf16[256,768]{1,0:T(8,128)(2,1)S(1)} %multiply_convert_fusion.5) | copy-start | bytes 1179652
  580.6 235.4 %all-gather.44.cloned.1.call-start = ((), (), s32[]{:S(2)}) async-start(), calls=%async_computation.22 | async-start | bytes 1966080 | tf_op jit(solution)/shard_map/all_gather | solution.py:191
  636.5 114.2 %copy-start.64 = (bf16[1,256,768]{2,1,0:T(8,128)(2,1)S(1)}, bf16[1,256,768]{2,1,0:T(8,128)(2,1)}, u32[]{:S(2)}) copy-start(bf16[1,256,768]{2,1,0:T(8,128)(2,1)} %param.47) | copy-start | bytes 1179652
  636.5 236.4 %all-gather.66.cloned.1.call-start = ((), (), s32[]{:S(2)}) async-start(), calls=%async_computation.52 | async-start | bytes 1216512 | tf_op jit(solution)/shard_map/all_gather | solution.py:360
  637.1 297.1 %all-gather.70.cloned.1.call-start = ((), (), s32[]{:S(2)}) async-start(), calls=%async_computation.54 | async-start | bytes 3244032 | tf_op jit(solution)/shard_map/all_gather | solution.py:363
  637.7 357.8 %all-gather.68.cloned.1.call-start = ((), (), s32[]{:S(2)}) async-start(), calls=%async_computation.53 | async-start | bytes 3244032 | tf_op jit(solution)/shard_map/all_gather | solution.py:362
  638.2 439.5 %reduce-scatter.21.cloned.1.call-start = ((), (), s32[]{:S(2)}) async-start(), calls=%async_computation.23 | async-start | bytes 1966080 | tf_op jit(solution)/shard_map/reduce_scatter | solution.py:270
  874.9 131.3 %copy-start.29 = (f32[256,768]{1,0:T(8,128)}, f32[256,768]{1,0:T(8,128)S(1)}, u32[]{:S(2)}) copy-start(f32[256,768]{1,0:T(8,128)S(1)} %get-tuple-element.1405) | copy-start | bytes 2359300
  875.4 63.0 %copy-start.181 = (f32[256]{0:T(256)}, f32[256]{0:T(256)S(1)}, u32[]{:S(2)}) copy-start(f32[256]{0:T(256)S(1)} %fusion.304) | copy-start | bytes 3076
  875.6 119.9 %copy-start.43 = (bf16[256,768]{1,0:T(8,128)(2,1)}, bf16[256,768]{1,0:T(8,128)(2,1)S(1)}, u32[]{:S(2)}) copy-start(bf16[256,768]{1,0:T(8,128)(2,1)S(1)} %multiply_convert_fusion.4) | copy-start | bytes 1179652
  1047.8 63.7 %reduce-scatter.23.cloned.1.call-start = ((), (), s32[]{:S(2)}) async-start(), calls=%async_computation.24 | async-start | bytes 1966080 | tf_op jit(solution)/shard_map/reduce_scatter | solution.py:273
  1051.5 153.4 %reduce-scatter.25.cloned.1.call-start = ((), (), s32[]{:S(2)}) async-start(), calls=%async_computation.25 | async-start | bytes 1966080 | tf_op jit(solution)/shard_map/reduce_scatter | solution.py:270
  1054.3 57.1 %copy-start.35 = (f32[256,768]{1,0:T(8,128)S(1)}, f32[256,768]{1,0:T(8,128)}, u32[]{:S(2)}) copy-start(f32[256,768]{1,0:T(8,128)} %copy-done.34) | copy-start | bytes 2359300
  1054.3 57.1 %copy-start.55 = (bf16[1,768,768]{2,1,0:T(8,128)(2,1)S(1)}, bf16[1,768,768]{2,1,0:T(8,128)(2,1)}, u32[]{:S(2)}) copy-start(bf16[1,768,768]{2,1,0:T(8,128)(2,1)} %all-gather.60.cloned.1.call-done) | copy-start | bytes 3538948
  1054.3 57.2 %copy-start.180 = (f32[256]{0:T(256)S(1)}, f32[256]{0:T(256)}, u32[]{:S(2)}) copy-start(f32[256]{0:T(256)} %copy-done.179) | copy-start | bytes 3076
  1173.8 65.0 %reduce-scatter.27.cloned.1.call-start = ((), (), s32[]{:S(2)}) async-start(), calls=%async_computation.26 | async-start | bytes 1966080 | tf_op jit(solution)/shard_map/reduce_scatter | solution.py:273
  1177.1 181.6 %reduce-scatter.33.cloned.1.call-start = ((), (), s32[]{:S(2)}) async-start(), calls=%async_computation.29 | async-start | bytes 2433024 | tf_op jit(solution)/shard_map/reduce_scatter | solution.py:389
  1179.1 268.3 %reduce-scatter.31.cloned.1.call-start = ((), (), s32[]{:S(2)}) async-start(), calls=%async_computation.28 | async-start | bytes 2433024 | tf_op jit(solution)/shard_map/reduce_scatter | solution.py:389
  1183.0 367.9 %reduce-scatter.45.cloned.1.call-start = ((), (), s32[]{:S(2)}) async-start(), calls=%async_computation.35 | async-start | bytes 2433024 | tf_op jit(solution)/shard_map/reduce_scatter | solution.py:392
  1186.1 468.7 %reduce-scatter.43.cloned.1.call-start = ((), (), s32[]{:S(2)}) async-start(), calls=%async_computation.34 | async-start | bytes 2433024 | tf_op jit(solution)/shard_map/reduce_scatter | solution.py:392
  1189.3 568.9 %reduce-scatter.37.cloned.1.call-start = ((), (), s32[]{:S(2)}) async-start(), calls=%async_computation.31 | async-start | bytes 2433024 | tf_op jit(solution)/shard_map/reduce_scatter | solution.py:390
  1192.2 670.1 %reduce-scatter.35.cloned.1.call-start = ((), (), s32[]{:S(2)}) async-start(), calls=%async_computation.30 | async-start | bytes 2433024 | tf_op jit(solution)/shard_map/reduce_scatter | solution.py:390
  1207.9 757.8 %reduce-scatter.41.cloned.1.call-start = ((), (), s32[]{:S(2)}) async-start(), calls=%async_computation.33 | async-start | bytes 2433024 | tf_op jit(solution)/shard_map/reduce_scatter | solution.py:391
  1210.8 859.0 %reduce-scatter.39.cloned.1.call-start = ((), (), s32[]{:S(2)}) async-start(), calls=%async_computation.32 | async-start | bytes 2433024 | tf_op jit(solution)/shard_map/reduce_scatter | solution.py:391
  1241.8 947.0 %reduce-scatter.57.cloned.1.call-start = ((), (), s32[]{:S(2)}) async-start(), calls=%async_computation.41 | async-start | bytes 6488064 | tf_op jit(solution)/shard_map/reduce_scatter | solution.py:396
  1246.8 1062.3 %reduce-scatter.55.cloned.1.call-start = ((), (), s32[]{:S(2)}) async-start(), calls=%async_computation.40 | async-start | bytes 6488064 | tf_op jit(solution)/shard_map/reduce_scatter | solution.py:396
  1252.0 1176.2 %reduce-scatter.49.cloned.1.call-start = ((), (), s32[]{:S(2)}) async-start(), calls=%async_computation.37 | async-start | bytes 6488064 | tf_op jit(solution)/shard_map/reduce_scatter | solution.py:394
  1257.0 1291.4 %reduce-scatter.47.cloned.1.call-start = ((), (), s32[]{:S(2)}) async-start(), calls=%async_computation.36 | async-start | bytes 6488064 | tf_op jit(solution)/shard_map/reduce_scatter | solution.py:394
  1262.1 1405.8 %reduce-scatter.53.cloned.1.call-start = ((), (), s32[]{:S(2)}) async-start(), calls=%async_computation.39 | async-start | bytes 6488064 | tf_op jit(solution)/shard_map/reduce_scatter | solution.py:395
  1266.9 1520.9 %reduce-scatter.51.cloned.1.call-start = ((), (), s32[]{:S(2)}) async-start(), calls=%async_computation.38 | async-start | bytes 6488064 | tf_op jit(solution)/shard_map/reduce_scatter | solution.py:395
  1271.8 1616.3 %reduce-scatter.29.cloned.1.call-start = ((), (), s32[]{:S(2)}) async-start(), calls=%async_computation.27 | async-start | bytes 811008 | tf_op jit(solution)/shard_map/reduce_scatter | solution.py:403
  1306.0 45.5 %copy-start.130 = (f32[768]{0:T(1024)S(1)}, f32[768]{0:T(1024)}, u32[]{:S(2)}) copy-start(f32[768]{0:T(1024)} %copy-done.129) | copy-start | bytes 9220
  1306.0 45.5 %copy-start.132 = (f32[768]{0:T(1024)S(1)}, f32[768]{0:T(1024)}, u32[]{:S(2)}) copy-start(f32[768]{0:T(1024)} %copy-done.131) | copy-start | bytes 9220
  (204 other events, 808.8 us)
Sparse Core Ops, SparseCore 0:
  11.5 56.7 all-gather.47
  71.8 53.3 all-gather.45
  128.6 53.1 all-gather.49
  219.0 28.9 all-gather.39
  250.3 30.9 all-gather.37
  284.1 54.0 all-gather.51
  341.6 57.9 all-gather.53
  403.1 57.8 all-gather.55
  464.5 57.8 all-gather.57
  525.1 52.8 all-gather.59
  580.9 52.9 all-gather.61
  636.7 52.9 all-gather.63
  692.6 57.9 all-gather.71
  752.9 29.7 all-gather.41
  785.0 30.9 all-gather.43
  818.8 54.0 all-gather.65
  876.2 57.9 all-gather.69
  937.5 57.8 all-gather.67
  1047.9 29.7 reduce-scatter.20
  1080.5 30.8 reduce-scatter.22
  1173.9 30.9 reduce-scatter.24
  1207.9 30.9 reduce-scatter.26
  1244.2 99.2 reduce-scatter.32
  1349.4 97.9 reduce-scatter.30
  1452.7 98.0 reduce-scatter.44
  1556.9 97.9 reduce-scatter.42
  1660.0 98.1 reduce-scatter.36
  1764.4 97.9 reduce-scatter.34
  1867.6 98.0 reduce-scatter.40
  1971.7 98.0 reduce-scatter.38
  2075.4 113.3 reduce-scatter.56
  2195.4 113.7 reduce-scatter.54
  2314.7 113.4 reduce-scatter.48
  2434.8 113.6 reduce-scatter.46
  2554.1 113.7 reduce-scatter.52
  2674.3 113.5 reduce-scatter.50
  2793.4 94.6 reduce-scatter.28
where the time goes:
time: 2900 us
  waiting for transfers between devices  2270 us (78%)
  blocking collectives  214 us (7%)
  matrix products  211 us (7%)
  local copies, waits for them, and re-layouts  109 us (4%)
  other arithmetic  67 us (2%)
    reduce_scatter x2, waiting for transfers between devices, on_device(): lax.psum_scatter(partial_grads[8], ('dp', 'ctx'), scatter_dimension=0, ti...  238 us
    reduce_scatter x2, waiting for transfers between devices, on_device(): lax.psum_scatter(partial_grads[7], ('dp', 'ctx'), scatter_dimension=0, ti...  238 us
    reduce_scatter x2, waiting for transfers between devices, on_device(): lax.psum_scatter(partial_grads[6], ('dp', 'ctx'), scatter_dimension=0, ti...  237 us
    reduce_scatter x2, waiting for transfers between devices, on_device(): lax.psum_scatter(partial_grads[2], ('dp', 'ctx'), scatter_dimension=0, ti...  206 us
    reduce_scatter x2, waiting for transfers between devices, on_device(): lax.psum_scatter(partial_grads[3], ('dp', 'ctx'), scatter_dimension=0, ti...  206 us
    reduce_scatter x2, waiting for transfers between devices, on_device(): lax.psum_scatter(partial_grads[4], ('dp', 'ctx'), scatter_dimension=0, ti...  205 us
    all_gather x2, waiting for transfers between devices, on_device(): lax.all_gather(up_w[layer_index], ('dp', 'ctx'), axis=0, tiled=True)  116 us
    all_gather x2, waiting for transfers between devices, on_device(): lax.all_gather(gate_w[layer_index], ('dp', 'ctx'), axis=0, tiled=True)  116 us
  transfers between devices with their start and end apart: 39, of which 33 were waited for; matrix products, arithmetic and copies ran while one was open for 9% of the time, Pallas kernels for 0%

commit v1 on v0

--- a/solution.py
+++ b/solution.py
@@ -1,10 +1,268 @@
+import functools
 import jax
 import jax.numpy as jnp
 from jax import lax
+from jax.experimental import pallas as pl
+from jax.experimental.pallas import tpu as pltpu
 from jax.sharding import PartitionSpec as P
+MESH = pl.DeviceIdType.MESH
+CORES = 2
+
+
+def grid_of():
+    dp, ctx = lax.axis_size("dp"), lax.axis_size("ctx")
+    rows = 2 if ctx % 2 == 0 else 1
+    return dp // CORES, rows, ctx // rows
+
+
+def place_of():
+    _, _, nx = grid_of()
+    d, c = lax.axis_index("dp"), lax.axis_index("ctx")
+    return d // CORES, d % CORES, c // nx, c % nx
+
+
+def device(z, core, y, x):
+    _, _, nx = grid_of()
+    return (z * CORES + core, y * nx + x)
+
+
+def peers():
+    nz, ny, nx = grid_of()
+    z, core, y, x = place_of()
+    zs = [lax.rem(z + i, nz) for i in range(1, nz)]
+    ys = [lax.rem(y + i, ny) for i in range(1, ny)]
+    xs = [lax.rem(x + i, nx) for i in range(1, nx)]
+    return zs, ys, xs
+
+
+def greet(extra=()):
+    z, core, y, x = place_of()
+    zs, ys, xs = peers()
+    barrier = pltpu.get_barrier_semaphore()
+    targets = [device(p, core, y, x) for p in zs]
+    targets += [device(z, core, p, x) for p in ys]
+    targets += [device(z, core, y, p) for p in xs]
+    targets += [device(z, 1 - core, y, x)]
+    targets += list(extra)
+    for target in targets:
+        pl.semaphore_signal(barrier, inc=1, device_id=target, device_id_type=MESH)
+    pl.semaphore_wait(barrier, len(targets))
+
+
+def remote(src, dst, sems, k, target):
+    return pltpu.make_async_remote_copy(
+        src_ref=src, dst_ref=dst, send_sem=sems.at[0, k], recv_sem=sems.at[1, k],
+        device_id=target, device_id_type=MESH)
+
+
+def halves(width):
+    left = -(-width // 256) * 128
+    return pl.ds(0, left), pl.ds(left, width - left)
+
+
+class GatherChunk:
+    def __init__(self, shard, out, sems, local_sem):
+        self.shard, self.out, self.sems, self.local_sem = shard, out, sems, local_sem
+        self.halves = halves(shard.shape[-1])
+        self.started = []
+
+    @staticmethod
+    def count():
+        nz, ny, nx = grid_of()
+        return (nz - 1) + 2 * (nx - 1) + 2 * (ny - 1) + 1
+
+    def send(self, where, target, kind):
+        k = sum(len(group) for group in self.started) + len(self.current)
+        copy = remote(self.out.at[where], self.out.at[where], self.sems, k, target)
+        copy.start()
+        self.current.append(copy)
+
+    def stage(self, number):
+        z, core, y, x = place_of()
+        zs, ys, xs = peers()
+        left, right = self.halves
+        if number > 1:
+            for copy in self.started[-1]:
+                copy.wait_recv()
+        self.current = []
+        if number == 0:
+            own = pltpu.make_async_copy(self.shard, self.out.at[z, core, y, x], self.local_sem)
+            own.start()
+            for i, p in enumerate(zs):
+                copy = remote(self.shard, self.out.at[z, core, y, x], self.sems, i, device(p, core, y, x))
+                copy.start()
+                self.current.append(copy)
+            self.own = own
+        elif number == 1:
+            for copy in self.started[-1]:
+                copy.wait_recv()
+            self.own.wait()
+            for p in xs:
+                self.send((slice(None), core, y, x, slice(None), left), device(z, core, y, p), 0)
+            for p in ys:
+                self.send((slice(None), core, y, x, slice(None), right), device(z, core, p, x), 0)
+        elif number == 2:
+            for p in ys:
+                self.send((slice(None), core, y, slice(None), slice(None), left), device(z, core, p, x), 0)
+            for p in xs:
+                self.send((slice(None), core, slice(None), x, slice(None), right), device(z, core, y, p), 0)
+        elif number == 3:
+            self.send((slice(None), core), device(z, 1 - core, y, x), 0)
+        self.started.append(self.current)
+        if number == 4:
+            for group in self.started:
+                for copy in group:
+                    copy.wait_send()
+
+
+def gather_kernel(n, *refs):
+    shards, outs, (sems, local_sems) = refs[:n], refs[n:2 * n], refs[2 * n:]
+    greet()
+    chunks = [GatherChunk(shards[i], outs[i], sems.at[i], local_sems.at[i]) for i in range(n)]
+    for t in range(n + 4):
+        for number in range(4):
+            if 0 <= t - number < n:
+                chunks[t - number].stage(number)
+    for chunk in chunks:
+        chunk.stage(4)
+
+
+def gather_all(shards, collective_id):
+    nz, ny, nx = grid_of()
+    n = len(shards)
+    outs = pl.pallas_call(
+        functools.partial(gather_kernel, n),
+        out_shape=[jax.ShapeDtypeStruct((nz, CORES, ny, nx) + s.shape, s.dtype) for s in shards],
+        in_specs=[pl.BlockSpec(memory_space=pl.ANY)] * n,
+        out_specs=[pl.BlockSpec(memory_space=pl.ANY)] * n,
+        scratch_shapes=[pltpu.SemaphoreType.DMA((n, 2, GatherChunk.count())), pltpu.SemaphoreType.DMA((n,))],
+        compiler_params=pltpu.CompilerParams(collective_id=collective_id, has_side_effects=True),
+        name="gather_weights",
+    )(*shards)
+    return [o.reshape((-1,) + o.shape[5:]) for o in outs]
+
+
+def add_into(dst, src, lead):
+    if not lead:
+        dst[...] = (dst[...].astype(jnp.float32) + src[...].astype(jnp.float32)).astype(dst.dtype)
+        return
+
+    def body(i, carry):
+        add_into(dst.at[i], src.at[i], lead[1:])
+        return carry
+    lax.fori_loop(0, lead[0], body, 0)
+
+
+class ScatterChunk:
+    def __init__(self, parts, out, held, across, first, second, last, sems, local_sem):
+        self.parts, self.out, self.held, self.across = parts, out, held, across
+        self.first, self.second, self.last, self.sems, self.local_sem = first, second, last, sems, local_sem
+        self.halves = halves(parts.shape[-1])
+        self.copies = []
+        self.k = 0
+
+    count = GatherChunk.count
+
+    @staticmethod
+    def scratch(shape, dtype):
+        nz, ny, nx = grid_of()
+        r, n = shape
+        return [pltpu.VMEM((nz, ny, nx, r, n), dtype), pltpu.VMEM((nz, ny, nx, r, n), dtype),
+                pltpu.VMEM((nx - 1, nz, ny, r, halves(n)[0].size), dtype), pltpu.VMEM((ny - 1, nz, nx, r, halves(n)[1].size), dtype),
+                pltpu.VMEM((ny - 1, nz, r, halves(n)[0].size), dtype), pltpu.VMEM((nx - 1, nz, r, halves(n)[1].size), dtype),
+                pltpu.VMEM((nz - 1, r, n), dtype)]
+
+    def send(self, src, dst, target):
+        copy = remote(src, dst, self.sems, self.k, target)
+        self.k += 1
+        copy.start()
+        self.current.append(copy)
+
+    def stage(self, number):
+        nz, ny, nx = grid_of()
+        z, core, y, x = place_of()
+        zs, ys, xs = peers()
+        left, right = self.halves
+        held = self.held
+        every = slice(None)
+        if number:
+            for copy in self.current:
+                copy.wait_recv()
+        done = self.current if number else []
+        self.current = []
+        if number == 0:
+            self.own = pltpu.make_async_copy(self.parts.at[:, core], held, self.local_sem)
+            self.own.start()
+            self.send(self.parts.at[:, 1 - core], self.across, device(z, 1 - core, y, x))
+        elif number == 1:
+            self.own.wait()
+            add_into(held, self.across, (nz, ny, nx))
+            for i, p in enumerate(xs):
+                self.send(held.at[:, :, p, :, left], self.first[0].at[i], device(z, core, y, p))
+            for i, p in enumerate(ys):
+                self.send(held.at[:, p, :, :, right], self.first[1].at[i], device(z, core, p, x))
+        elif number == 2:
+            for i in range(nx - 1):
+                add_into(held.at[:, :, x, :, left], self.first[0].at[i], (nz, ny))
+            for i in range(ny - 1):
+                add_into(held.at[:, y, :, :, right], self.first[1].at[i], (nz, nx))
+            for i, p in enumerate(ys):
+                self.send(held.at[:, p, x, :, left], self.second[0].at[i], device(z, core, p, x))
+            for i, p in enumerate(xs):
+                self.send(held.at[:, y, p, :, right], self.second[1].at[i], device(z, core, y, p))
+        elif number == 3:
+            for i in range(ny - 1):
+                add_into(held.at[:, y, x, :, left], self.second[0].at[i], (nz,))
+            for i in range(nx - 1):
+                add_into(held.at[:, y, x, :, right], self.second[1].at[i], (nz,))
+            for i, p in enumerate(zs):
+                self.send(held.at[p, y, x], self.last.at[i], device(p, core, y, x))
+        elif number == 4:
+            total = held[z, y, x].astype(jnp.float32)
+            for i in range(nz - 1):
+                total = total + self.last[i].astype(jnp.float32)
+            self.out[...] = total
+        self.copies += done
+        if number == 4:
+            for copy in self.copies:
+                copy.wait_send()
+
+
+def scatter_kernel(n, *refs):
+    parts, outs, rest = refs[:n], refs[n:2 * n], refs[2 * n:]
+    sems, local_sems = rest[-2:]
+    greet()
+    chunks = []
+    for i in range(n):
+        s = rest[7 * i:7 * i + 7]
+        chunks.append(ScatterChunk(parts[i], outs[i], s[0], s[1], s[2:4], s[4:6], s[6], sems.at[i], local_sems.at[i]))
+    for t in range(n + 4):
+        for number in range(5):
+            if 0 <= t - number < n:
+                chunks[t - number].stage(number)
+
+
+def scatter_all(parts, collective_id):
+    nz, ny, nx = grid_of()
+    n = len(parts)
+    devices = nz * CORES * ny * nx
+    parts = [p.reshape((nz, CORES, ny, nx, p.shape[0] // devices) + p.shape[1:]) for p in parts]
+    scratch = []
+    for p in parts:
+        scratch += ScatterChunk.scratch(p.shape[4:], p.dtype)
+    return pl.pallas_call(
+        functools.partial(scatter_kernel, n),
+        out_shape=[jax.ShapeDtypeStruct(p.shape[4:], jnp.float32) for p in parts],
+        in_specs=[pl.BlockSpec(memory_space=pl.ANY)] * n,
+        out_specs=[pl.BlockSpec(memory_space=pltpu.VMEM)] * n,
+        scratch_shapes=scratch + [pltpu.SemaphoreType.DMA((n, 2, GatherChunk.count())), pltpu.SemaphoreType.DMA((n,))],
+        compiler_params=pltpu.CompilerParams(collective_id=collective_id, has_side_effects=True, vmem_limit_bytes=60 << 20),
+        name="scatter_grads",
+    )(*parts)
 
 HEADS = 12
 HEAD_DIM = 64
+CONV = 4
 
 
 NORM_EPS = 1e-06
@@ -187,10 +445,8 @@
     query_act = jnp.dot(normed, w_query, preferred_element_type=jnp.float32).astype(jnp.bfloat16)
     key_act = jnp.dot(normed, w_key, preferred_element_type=jnp.float32).astype(jnp.bfloat16)
     value_act = jnp.dot(normed, w_value, preferred_element_type=jnp.float32).astype(jnp.bfloat16)
-    key_all, value_all = (
-        lax.all_gather(key_act, "ctx", axis=0, tiled=True),
-        lax.all_gather(value_act, "ctx", axis=0, tiled=True),
-    )
+    both = lax.all_gather(jnp.concatenate([key_act, value_act], 1), "ctx", axis=0, tiled=True)
+    key_all, value_all = both[:, : both.shape[1] // 2], both[:, both.shape[1] // 2 :]
     block_count, block_rows = seg_blocks.shape
     q_heads = query_act.reshape(row_count, HEADS, HEAD_DIM)
     key_own = key_act.reshape(row_count, HEADS, HEAD_DIM)
@@ -224,10 +480,9 @@
     return (result, saved)
 
 
-def layer_backward(stream_in, weights, masks, grad_out):
+def layer_backward(stream_in, weights, masks, saved, grad_out):
     gain_attn, w_query, w_key, w_value, w_out, gain_ffn, w_gate, w_up, w_down = weights
     q_seg, tok_seg, seg_blocks = masks
-    _, saved = layer_forward(stream_in, weights, masks)
     (
         normed,
         q_heads,
@@ -266,14 +521,10 @@
     grad_query, inner_sum, grad_key_all, grad_value_all = attention_back(
         q_heads, q_seg, key_blocks, value_blocks, seg_blocks, log_total, grad_heads
     )
-    grad_key, grad_value = (
-        lax.psum_scatter(
-            grad_key_all.astype(jnp.bfloat16), "ctx", scatter_dimension=0, tiled=True
-        ).astype(jnp.float32),
-        lax.psum_scatter(
-            grad_value_all.astype(jnp.bfloat16), "ctx", scatter_dimension=0, tiled=True
-        ).astype(jnp.float32),
-    )
+    both = lax.psum_scatter(
+        jnp.concatenate([grad_key_all, grad_value_all], 1).astype(jnp.bfloat16), "ctx", scatter_dimension=0, tiled=True
+    )
+    grad_key, grad_value = both[:, : both.shape[1] // 2], both[:, both.shape[1] // 2 :]
     grad_query = grad_query.reshape(row_count, -1).astype(jnp.bfloat16)
     grad_key = grad_key.astype(jnp.bfloat16)
     grad_value = grad_value.astype(jnp.bfloat16)
@@ -292,6 +543,17 @@
         grad_in,
         (d_gain_attn, d_query, d_key, d_value, d_out, d_gain_ffn, d_gate, d_up, d_down),
     )
+
+
+def packed_small(embed, conv_weight, conv_bias, scorer, norm_attn, norm_ffn):
+    rows = jnp.concatenate([embed, conv_weight, conv_bias[None], scorer[None], norm_attn, norm_ffn], 0).T
+    return jnp.pad(rows, ((0, 0), (0, -rows.shape[1] % 128)))
+
+
+def split_small(rows, vocab, layers):
+    at = vocab + CONV
+    return (rows[:vocab], rows[vocab:at], rows[at], rows[at + 1], rows[at + 2 : at + 2 + layers],
+            rows[at + 2 + layers : at + 2 + 2 * layers])
 
 
 def on_device(
@@ -314,10 +576,14 @@
 ):
     ctx_count = lax.axis_size("ctx")
     ctx_place = lax.axis_index("ctx")
+    layer_count = query_w.shape[0]
+    vocab = embed.shape[0]
+    model = query_w.shape[2]
     byte_count = byte_ids.shape[1]
     tok_count = byte_count // 2
     seq_lengths = lengths[0]
-    ends = jnp.cumsum(seq_lengths)
+    at = jnp.arange(seq_lengths.shape[0])
+    ends = jnp.sum(jnp.where(at[:, None] >= at[None, :], seq_lengths[None, :], 0), 1).astype(jnp.int32)
     total_bytes = ends[-1]
     first_byte = ctx_place * byte_count
     byte_ext = padded(byte_ids[0], (("ctx", 0),), 5)
@@ -331,12 +597,15 @@
     q_seg = segment_of(first_byte + 2 * jnp.arange(tok_count, dtype=jnp.int32), ends)
     seg_blocks = tok_seg.reshape(group_tok // block_rows, block_rows)
     masks = (q_seg, tok_seg, seg_blocks)
-    embed_full, conv_full, bias_full, scorer_full = (
-        lax.all_gather(embed, ("dp", "ctx"), axis=1, tiled=True),
-        lax.all_gather(conv_weight, ("dp", "ctx"), axis=1, tiled=True),
-        lax.all_gather(conv_bias, ("dp", "ctx"), axis=0, tiled=True),
-        lax.all_gather(scorer, ("dp", "ctx"), axis=0, tiled=True),
-    )
+
+    small = packed_small(embed, conv_weight, conv_bias, scorer, norm_attn, norm_ffn)
+    shards = [small]
+    for layer in range(layer_count):
+        shards.append(jnp.concatenate([query_w[layer], key_w[layer], value_w[layer], attn_out_w[layer]], 1))
+        shards.append(jnp.concatenate([gate_w[layer], up_w[layer]], 1))
+        shards.append(down_w[layer])
+    small_full, *full = [a.reshape(-1, a.shape[-1]) for a in gather_all(shards, 0)]
+    embed_full, conv_full, bias_full, scorer_full, norm_a, norm_f = split_small(small_full.T, vocab, layer_count)
 
     def gbst_local(embed_t, conv_w, conv_b, scorer_v):
         return gbst_mix(byte_ext, valid_ext, seg_ext, rel_ext, embed_t, conv_w, conv_b, scorer_v)
@@ -348,78 +617,47 @@
         bias_full.astype(jnp.float32),
         scorer_full.astype(jnp.float32),
     )
-    layer_count = query_w.shape[0]
-    kept_weights = []
-    inputs = []
-    for layer_index in range(layer_count):
-        weights = (
-            lax.all_gather(norm_attn[layer_index], ("dp", "ctx"), axis=0, tiled=True),
-            lax.all_gather(query_w[layer_index], ("dp", "ctx"), axis=0, tiled=True),
-            lax.all_gather(key_w[layer_index], ("dp", "ctx"), axis=0, tiled=True),
-            lax.all_gather(value_w[layer_index], ("dp", "ctx"), axis=0, tiled=True),
-            lax.all_gather(attn_out_w[layer_index], ("dp", "ctx"), axis=0, tiled=True),
-            lax.all_gather(norm_ffn[layer_index], ("dp", "ctx"), axis=0, tiled=True),
-            lax.all_gather(gate_w[layer_index], ("dp", "ctx"), axis=0, tiled=True),
-            lax.all_gather(up_w[layer_index], ("dp", "ctx"), axis=0, tiled=True),
-            lax.all_gather(down_w[layer_index], ("dp", "ctx"), axis=0, tiled=True),
-        )
-        kept_weights.append(weights)
-        inputs.append(stream)
-        stream, _ = layer_forward(stream, weights, masks)
+    kept = []
+    for layer in range(layer_count):
+        attn, ffn, down = full[3 * layer : 3 * layer + 3]
+        weights = (norm_a[layer], attn[:, :model], attn[:, model : 2 * model], attn[:, 2 * model : 3 * model],
+                   attn[:, 3 * model :], norm_f[layer], ffn[:, : ffn.shape[1] // 2], ffn[:, ffn.shape[1] // 2 :], down)
+        before = stream
+        stream, saved = layer_forward(stream, weights, masks)
+        kept.append((before, weights, saved))
     encoded = stream.astype(jnp.bfloat16)[None]
     grad_stream = out_grad[0].astype(jnp.float32)
-    collected = [[] for _ in range(9)]
-    for layer_index in reversed(range(layer_count)):
-        weights = (
-            lax.all_gather(norm_attn[layer_index], ("dp", "ctx"), axis=0, tiled=True),
-            lax.all_gather(query_w[layer_index], ("dp", "ctx"), axis=0, tiled=True),
-            lax.all_gather(key_w[layer_index], ("dp", "ctx"), axis=0, tiled=True),
-            lax.all_gather(value_w[layer_index], ("dp", "ctx"), axis=0, tiled=True),
-            lax.all_gather(attn_out_w[layer_index], ("dp", "ctx"), axis=0, tiled=True),
-            lax.all_gather(norm_ffn[layer_index], ("dp", "ctx"), axis=0, tiled=True),
-            lax.all_gather(gate_w[layer_index], ("dp", "ctx"), axis=0, tiled=True),
-            lax.all_gather(up_w[layer_index], ("dp", "ctx"), axis=0, tiled=True),
-            lax.all_gather(down_w[layer_index], ("dp", "ctx"), axis=0, tiled=True),
-        )
-        grad_stream, partial_grads = layer_backward(
-            inputs[layer_index], weights, masks, grad_stream
-        )
-        shards = (
-            lax.psum_scatter(partial_grads[0], ("dp", "ctx"), scatter_dimension=0, tiled=True),
-            lax.psum_scatter(partial_grads[1], ("dp", "ctx"), scatter_dimension=0, tiled=True),
-            lax.psum_scatter(partial_grads[2], ("dp", "ctx"), scatter_dimension=0, tiled=True),
-            lax.psum_scatter(partial_grads[3], ("dp", "ctx"), scatter_dimension=0, tiled=True),
-            lax.psum_scatter(partial_grads[4], ("dp", "ctx"), scatter_dimension=0, tiled=True),
-            lax.psum_scatter(partial_grads[5], ("dp", "ctx"), scatter_dimension=0, tiled=True),
-            lax.psum_scatter(partial_grads[6], ("dp", "ctx"), scatter_dimension=0, tiled=True),
-            lax.psum_scatter(partial_grads[7], ("dp", "ctx"), scatter_dimension=0, tiled=True),
-            lax.psum_scatter(partial_grads[8], ("dp", "ctx"), scatter_dimension=0, tiled=True),
-        )
-        for position in range(9):
-            collected[position].append(shards[position])
-    stacked = [jnp.stack(column[::-1]) for column in collected]
-    grad_embed_t, grad_conv_w, grad_conv_b, grad_scorer_v = gbst_back(grad_stream)
-    grad_embed, grad_conv_weight, grad_conv_bias, grad_scorer = (
-        lax.psum_scatter(grad_embed_t, ("dp", "ctx"), scatter_dimension=1, tiled=True),
-        lax.psum_scatter(grad_conv_w, ("dp", "ctx"), scatter_dimension=1, tiled=True),
-        lax.psum_scatter(grad_conv_b, ("dp", "ctx"), scatter_dimension=0, tiled=True),
-        lax.psum_scatter(grad_scorer_v, ("dp", "ctx"), scatter_dimension=0, tiled=True),
-    )
+    partial = []
+    gains = []
+    for layer in reversed(range(layer_count)):
+        before, weights, saved = kept[layer]
+        grad_stream, grads = layer_backward(before, weights, masks, saved, grad_stream)
+        d_gain_attn, d_query, d_key, d_value, d_out, d_gain_ffn, d_gate, d_up, d_down = grads
+        partial = [jnp.concatenate([d_query, d_key, d_value, d_out], 1), jnp.concatenate([d_gate, d_up], 1), d_down] + partial
+        gains = [(d_gain_attn, d_gain_ffn)] + gains
+    grads = gbst_back(grad_stream)
+    small_grad = packed_small(*grads, jnp.stack([a for a, _ in gains]), jnp.stack([f for _, f in gains]))
+    outs = scatter_all([p.astype(jnp.bfloat16) for p in [small_grad] + partial], 1)
+    small_out, *rest = outs
+    g_embed, g_conv, g_bias, g_scorer, g_norm_a, g_norm_f = split_small(small_out.T, vocab, layer_count)
+    attn_out, ffn_out, down_out = rest[0::3], rest[1::3], rest[2::3]
+    columns = [jnp.stack([a[:, i * model : (i + 1) * model] for a in attn_out]) for i in range(4)]
+    wide = ffn_out[0].shape[1] // 2
     return (
         encoded,
-        grad_embed,
-        grad_conv_weight,
-        grad_conv_bias,
-        grad_scorer,
-        stacked[0],
-        stacked[1],
-        stacked[2],
-        stacked[3],
-        stacked[4],
-        stacked[5],
-        stacked[6],
-        stacked[7],
-        stacked[8],
+        g_embed,
+        g_conv,
+        g_bias,
+        g_scorer,
+        g_norm_a,
+        columns[0],
+        columns[1],
+        columns[2],
+        columns[3],
+        g_norm_f,
+        jnp.stack([a[:, :wide] for a in ffn_out]),
+        jnp.stack([a[:, wide:] for a in ffn_out]),
+        jnp.stack(down_out),
     )
 
 

time: 2900 us -> 826 us (0.28)
  waiting for transfers between devices: 2270 us -> 132 us
  Pallas kernels: 0 us -> 300 us
  blocking collectives: 214 us -> 0 us
    reduce_scatter x19 -> x2, waiting for transfers between devices: 1610 us -> 49.7 us  [layer_backward(): lax.psum_scatter(jnp.concatenate([grad_key_all, grad_value_all], 1).astyp...]
    all_gather x18 -> x2, waiting for transfers between devices: 649 us -> 82.7 us  [layer_forward(): lax.all_gather(jnp.concatenate([key_act, value_act], 1), 'ctx', axis=0, t...]
    pallas_call x0 -> x2, Pallas kernels: none -> 300 us  [the longest x1 150 us: gather_all(): pl.pallas_call(functools.partial(gather_kernel, n), out_shape=[jax.ShapeD...]
    all_gather x2 -> x0, blocking collectives: 133 us -> none  [the longest x1 68.9 us: on_device(): lax.all_gather(embed, ('dp', 'ctx'), axis=1, tiled=True)]
    unnamed x2 -> x0, blocking collectives: 81.3 us -> none
  transfers between devices with their start and end apart: 39 -> 6, of which waited for: 33 -> 4; matrix products, arithmetic and copies ran while one was open for 9% -> 7% of each run, Pallas kernels for 0% -> 18%
where the time goes in v1:
time: 826 us; the launch traced here: 819 us
  Pallas kernels  300 us (36%)
  matrix products  183 us (22%)
  waiting for transfers between devices  132 us (16%)
  local copies, waits for them, and re-layouts  103 us (12%)
  other arithmetic  74 us (9%)
  between operations  17.1 us (2%)
    pallas_call x1, Pallas kernels, gather_all(): pl.pallas_call(functools.partial(gather_kernel, n), out_shape=[jax.ShapeD...  150 us
    pallas_call x1, Pallas kernels, scatter_all(): pl.pallas_call(functools.partial(scatter_kernel, n), out_shape=[jax.Shape...  149 us
    all_gather x2, waiting for transfers between devices, layer_forward(): lax.all_gather(jnp.concatenate([key_act, value_act], 1), 'ctx', axis=0, t...  82.7 us
    reduce_scatter x2, waiting for transfers between devices, layer_backward(): lax.psum_scatter(jnp.concatenate([grad_key_all, grad_value_all], 1).astyp...  49.7 us
    dot_general x12, matrix products, block_scores(): jnp.einsum('qhd,khd->hqk', q_heads, key_block, preferred_element_type=jnp...  27.7 us
    unnamed x347, local copies, waits for them, and re-layouts  27.5 us
    dot_general x4, matrix products, weighted_block_step(): jnp.einsum('hqk,khd->qhd', attn_probs.astype(jnp.bfloat16), value_block,...  16.5 us
  transfers between devices with their start and end apart: 6, of which 4 were waited for; matrix products, arithmetic and copies ran while one was open for 7% of the time, Pallas kernels for 18%

profile of v1, /device:TPU:0, one launch (start us, length us, event | category | flops | bytes accessed | tf_op | source)
XLA Modules:
  0.0 818.9 jit_solution(11620409207444093846)
XLA Ops:
  9.3 5.5 collective-permute-start
  27.4 150.3 %gather_weights.1 = (bf16[4,2,2,2,24,384]{5,4,3,2,1,0:T(8,128)(2,1)}, bf16[4,2,2,2,24,3072]{5,4,3,2,1,0:T(8,128)(2,1)}, bf16[4,2,2,2,24,4096]{5,4,3,2,1,0:T(8,12...) custom-call(bf16[24,384]{1,0:T(8,128)(2,1)} %pad.81.refs_0_, ...), custom_call_target="tpu_custom_call" | custom-call | tf_op jit(solution)/shard_map/gather_weights/pallas_call | solution.py:133
  187.0 3.1 fusion.266
  202.2 45.3 %all-gather.3.cloned.1.call-done = bf16[1024,1536]{1,0:T(8,128)(2,1)} async-done(((bf16[256,1536]{1,0:T(8,128)(2,1)}), bf16[1024,1536]{1,0:T(8,128)(2,1)}) %all-gather.3.cloned.1.call-update) | async-done | bytes 3145744 | tf_op jit(solution)/shard_map/all_gather | solution.py:448
  247.5 3.7 fusion.311
  255.5 2.9 copy.189
  264.3 15.4 %while.100 = (s32[]{:T(128)}, f32[12,256]{1,0:T(8,128)S(1)}, f32[12,256]{1,0:T(8,128)S(1)}, s32[256]{0:T(256)S(1)}, s32[2,512]{1,0:T(2,128)S(1)}, /*index=5*/bf1...) while((s32[]{:T(128)}, f32[12,256]{1,0:T(8,128)S(1)}, ...), condition=%wide.region_13.14_spmd.clone, body=%wide.region_10.13_spmd.clone.sunk | while | flops 209337344 | bytes 14322808 | solution.py:366
  264.4 3.6 fusion.434
  268.1 3.9 exponential_reduce_fusion.4
  272.2 3.6 fusion.434
  275.8 3.9 exponential_reduce_fusion.4
  279.7 8.6 %while.101 = (s32[]{:T(128)}, f32[256,12,64]{0,2,1:T(8,128)}, bf16[2,512,12,64]{1,3,2,0:T(8,128)(2,1)}, s32[256]{0:T(256)S(1)}, s32[2,512]{1,0:T(2,128)S(1)}, /*...) while((s32[]{:T(128)}, f32[256,12,64]{0,2,1:T(8,128)}, ...), condition=%wide.region_15.16_spmd.clone, body=%wide.region_14.15_spmd.clone.sunk | while | flops 407896064 | bytes 3826298 | solution.py:385
  279.9 4.0 fusion.440
  284.1 4.3 fusion.440
  293.0 3.2 fusion.142
  296.2 5.3 multiply_convert_fusion.3
  305.6 4.3 convolution_bitcast_fusion.2
  311.8 37.4 %all-gather.5.cloned.1.call-done = bf16[1024,1536]{1,0:T(8,128)(2,1)} async-done(((bf16[256,1536]{1,0:T(8,128)(2,1)}), bf16[1024,1536]{1,0:T(8,128)(2,1)}) %all-gather.5.cloned.1.call-update) | async-done | bytes 3145744 | tf_op jit(solution)/shard_map/all_gather | solution.py:448
  349.2 3.7 fusion.310
  357.0 2.9 copy.195
  365.7 15.4 %while.102 = (s32[]{:T(128)}, f32[12,256]{1,0:T(8,128)S(1)}, f32[12,256]{1,0:T(8,128)S(1)}, s32[256]{0:T(256)S(1)}, s32[2,512]{1,0:T(2,128)S(1)}, /*index=5*/bf1...) while((s32[]{:T(128)}, f32[12,256]{1,0:T(8,128)S(1)}, ...), condition=%wide.region_21.22_spmd.clone, body=%wide.region_18.21_spmd.clone.sunk | while | flops 209337344 | bytes 14322808 | solution.py:366
  365.9 3.6 fusion.442
  369.6 3.9 exponential_reduce_fusion.5
  373.6 3.6 fusion.442
  377.3 3.9 exponential_reduce_fusion.5
  381.2 8.8 %while.103 = (s32[]{:T(128)}, f32[256,12,64]{0,2,1:T(8,128)}, bf16[2,512,12,64]{1,3,2,0:T(8,128)(2,1)}, s32[256]{0:T(256)S(1)}, s32[2,512]{1,0:T(2,128)S(1)}, /*...) while((s32[]{:T(128)}, f32[256,12,64]{0,2,1:T(8,128)}, ...), condition=%wide.region_23.24_spmd.clone, body=%wide.region_22.23_spmd.clone.sunk | while | flops 407896064 | bytes 3826298 | solution.py:385
  381.4 4.0 fusion.448
  385.6 4.2 fusion.448
  393.4 3.1 fusion.130
  396.6 5.6 fusion.157
  408.4 6.5 while.104
  417.6 26.9 %while.105 = (s32[]{:T(128)}, f32[256,12,64]{0,2,1:T(8,128)}, bf16[2,512,12,64]{1,3,2,0:T(8,128)(2,1)}, bf16[2,512,12,64]{1,3,2,0:T(8,128)(2,1)}, bf16[2,512,12,...) while((s32[]{:T(128)}, f32[256,12,64]{0,2,1:T(8,128)}, ...), condition=%wide.region_30.31_spmd.clone, body=%wide.region_29.30_spmd.clone.sunk | while | flops 1019740160 | bytes 123580000 | solution.py:432
  419.8 2.7 fusion.466
  422.6 2.8 fusion.467
  433.1 2.7 fusion.466
  435.9 3.0 fusion.467
  444.5 3.0 copy.204
  459.3 37.9 %reduce-scatter.3.cloned.1.call-done = bf16[256,1536]{0,1:T(8,128)(2,1)} async-done(((bf16[1024,1536]{0,1:T(8,128)(2,1)}), bf16[256,1536]{0,1:T(8,128)(2,1)}) %reduce-scatter.3.cloned.1.call-update) | async-done | bytes 786448 | tf_op jit(solution)/shard_map/reduce_scatter | solution.py:524
  499.3 2.7 multiply_reduce_fusion.8
  502.3 4.2 fusion.150
  513.2 10.5 %while.106 = (s32[]{:T(128)}, f32[12,256]{1,0:T(8,128)S(1)}, s32[256]{0:T(256)S(1)}, s32[2,512]{1,0:T(2,128)S(1)}, bf16[2,512,12,64]{1,3,2,0:T(8,128)(2,1)}, /*i...) while((s32[]{:T(128)}, f32[12,256]{1,0:T(8,128)S(1)}, ...), condition=%wide.region_36.37_spmd.clone, body=%wide.region_34.36_spmd.clone.sunk | while | flops 409078784 | bytes 15277195 | solution.py:405
  515.6 2.9 fusion.473
  520.8 2.9 fusion.473
  526.4 29.3 %while.107 = (s32[]{:T(128)}, f32[256,12,64]{0,2,1:T(8,128)}, bf16[2,512,12,64]{1,3,2,0:T(8,128)(2,1)}, bf16[2,512,12,64]{1,3,2,0:T(8,128)(2,1)}, bf16[2,512,12,...) while((s32[]{:T(128)}, f32[256,12,64]{0,2,1:T(8,128)}, ...), condition=%wide.region_38.39_spmd.clone, body=%wide.region_37.38_spmd.clone.sunk | while | flops 1019740160 | bytes 111005232 | solution.py:432
  529.0 3.2 fusion.485
  532.3 2.8 fusion.486
  537.2 2.6 bitcast_dynamic-update-slice_fusion.11
  543.5 3.2 fusion.485
  546.8 3.0 fusion.486
  551.8 2.6 bitcast_dynamic-update-slice_fusion.11
  555.8 3.0 copy.211
  570.8 2.7 convolution_convert_fusion
  575.3 3.4 pad_maximum_fusion.2.refs_5_
  587.8 2.8 convolution_convert_fusion.3
  593.0 3.5 pad_maximum_fusion.1.refs_2_
  596.5 11.8 %reduce-scatter.5.cloned.1.call-done = bf16[256,1536]{0,1:T(8,128)(2,1)} async-done(((bf16[1024,1536]{0,1:T(8,128)(2,1)}), bf16[256,1536]{0,1:T(8,128)(2,1)}) %reduce-scatter.5.cloned.1.call-update) | async-done | bytes 786448 | tf_op jit(solution)/shard_map/reduce_scatter | solution.py:524
  614.4 3.3 reshape.622
  617.7 2.8 multiply_reduce_fusion
  622.8 3.1 fusion.191
  628.5 6.9 multiply_reduce_fusion.5
  637.4 3.0 convolution_reduce_fusion
  640.5 2.8 fusion.183
  646.3 2.5 pad_maximum_fusion.3.refs_1_
  648.8 149.5 %scatter_grads.1 = (f32[24,384]{1,0:T(8,128)}, f32[24,3072]{1,0:T(8,128)}, f32[24,4096]{1,0:T(8,128)}, f32[64,768]{1,0:T(8,128)}, f32[24,3072]{1,0:T(8,128)}, /*index=5*/f32[24,4096]{1,0:T(8,128)}, f32[64,768]{1,0:T(8,128)}) custom-call(bf16[4,2,2,2,24,384]{5,4,3,2,1,0:T(8,128)(2,1)} %bitcast.662, ...), custom_call_target="tpu_custom_call" | custom-call | tf_op jit(solution)/shard_map/scatter_grads/pallas_call | solution.py:253
  (721 shorter events, 193.6 us)
Async XLA Ops:
  7.2 18.1 %copy-start.168 = (bf16[256,24]{0,1:T(8,128)(2,1)S(1)}, bf16[256,24]{0,1:T(8,128)(2,1)}, u32[]{:S(2)}) copy-start(bf16[256,24]{0,1:T(8,128)(2,1)} %param.34) | copy-start | bytes 36868
  7.2 240.3 %all-gather.3.cloned.1.call-start = ((), (), s32[]{:S(2)}) async-start(), calls=%async_computation.2 | async-start | bytes 3932160 | tf_op jit(solution)/shard_map/all_gather | solution.py:448
  8.0 173.3 %collective-permute-start.1 = (s32[5]{0:T(128)S(1)}, s32[5]{0:T(128)S(1)}, u32[]{:S(2)}, u32[]{:S(2)}) collective-permute-start(s32[5]{0:T(128)S(1)} %get-tuple-element.1283), channel_id=1, source_target_pairs={{1,0},{2,1},{3,2},{5,4},{6,5},{7,6},{9,8},{10,9},{11,10},{13,12},{... | collective-permute-start | bytes 68 | tf_op jit(solution)/shard_map/ppermute | solution.py:281
  9.3 172.1 %collective-permute-start = (s32[5]{0:T(128)S(1)}, s32[5]{0:T(128)S(1)}, u32[]{:S(2)}, u32[]{:S(2)}) collective-permute-start(s32[5]{0:T(128)S(1)} %get-tuple-element.1282), channel_id=1, source_target_pairs={{0,1},{1,2},{2,3},{4,5},{5,6},{6,7},{8,9},{9,10},{10,11},{12,13},{... | collective-permute-start | bytes 68 | tf_op jit(solution)/shard_map/ppermute | solution.py:280
  25.9 153.2 %copy-start.188 = (s32[1,4]{1,0:T(1,128)S(1)}, s32[1,4]{1,0:T(1,128)}, u32[]{:S(2)}) copy-start(s32[1,4]{1,0:T(1,128)} %param.33) | copy-start | bytes 52
  26.7 154.6 %copy-start.178 = (s32[1,512]{1,0:T(1,128)S(1)}, s32[1,512]{1,0:T(1,128)}, u32[]{:S(2)}) copy-start(s32[1,512]{1,0:T(1,128)} %param.32) | copy-start | bytes 6148
  179.1 8.0 copy-start.74
  179.2 16.0 %copy-start.112 = (f32[768]{0:T(1024)}, f32[768]{0:T(1024)S(1)}, u32[]{:S(2)}) copy-start(f32[768]{0:T(1024)S(1)} %get-tuple-element.1038) | copy-start | bytes 9220
  179.2 113.6 %copy-start.128 = (f32[768]{0:T(1024)}, f32[768]{0:T(1024)S(1)}, u32[]{:S(2)}) copy-start(f32[768]{0:T(1024)S(1)} %get-tuple-element.1037) | copy-start | bytes 9220
  181.1 3.5 copy-start.146
  181.1 3.5 copy-start.148
  181.1 3.5 copy-start.154
  184.6 5.7 copy-start.26
  194.4 96.4 %copy-start.13 = (f32[256,768]{1,0:T(8,128)}, f32[256,768]{1,0:T(8,128)S(1)}, u32[]{:S(2)}) copy-start(f32[256,768]{1,0:T(8,128)S(1)} %reduce_sum.290) | copy-start | bytes 2359300
  195.3 4.9 copy-start.60
  200.0 149.2 %all-gather.5.cloned.1.call-start = ((), (), s32[]{:S(2)}) async-start(), calls=%async_computation.3 | async-start | bytes 3932160 | tf_op jit(solution)/shard_map/all_gather | solution.py:448
  289.0 3.8 copy-start
  289.0 3.8 copy-start.3
  292.8 8.8 %copy-start.68 = (f32[256,768]{1,0:T(8,128)}, f32[256,768]{1,0:T(8,128)S(1)}, u32[]{:S(2)}) copy-start(f32[256,768]{1,0:T(8,128)S(1)} %get-tuple-element.1287) | copy-start | bytes 2359300
  293.0 9.9 %slice-start = ((s8[4718592]{0:T(1024)(128)(4,1)}), s8[4194304]{0:T(1024)(128)(4,1)S(1)}, s32[]{:S(2)}) async-start(s8[4718592]{0:T(1024)(128)(4,1)} %bitcast.630), calls=%async_computation.6 | async-start | bytes 8388608
  296.2 5.4 copy-start.189
  296.2 5.4 copy-start.186
  296.2 6.7 slice-start.1
  302.7 88.5 %copy-start.16 = (f32[256,768]{1,0:T(8,128)}, f32[256,768]{1,0:T(8,128)S(1)}, u32[]{:S(2)}) copy-start(f32[256,768]{1,0:T(8,128)S(1)} %get-tuple-element.1291) | copy-start | bytes 2359300
  302.9 7.0 copy-start.62
  305.0 192.2 %reduce-scatter.3.cloned.1.call-start = ((), (), s32[]{:S(2)}) async-start(), calls=%async_computation.4 | async-start | bytes 3932160 | tf_op jit(solution)/shard_map/reduce_scatter | solution.py:524
  393.2 12.0 %copy-start.39 = (f32[256,768]{1,0:T(8,128)}, f32[256,768]{1,0:T(8,128)S(1)}, u32[]{:S(2)}) copy-start(f32[256,768]{1,0:T(8,128)S(1)} %get-tuple-element.1293) | copy-start | bytes 2359300
  393.4 8.8 %slice-start.4 = ((s8[6291456]{0:T(1024)(128)(4,1)}), s8[4194304]{0:T(1024)(128)(4,1)S(1)}, s32[]{:S(2)}) async-start(s8[6291456]{0:T(1024)(128)(4,1)} %bitcast.703), calls=%async_computation.10 | async-start | bytes 8388608
  396.6 5.6 slice-start.5
  419.0 3.6 copy-start.5
  422.6 4.8 copy-start.6
  427.4 3.6 copy-start.2
  427.4 3.6 copy-start.90
  427.4 3.6 copy-start.167
  432.2 3.6 copy-start.5
  435.9 5.0 copy-start.6
  440.9 3.6 copy-start.2
  440.9 3.6 copy-start.90
  440.9 3.6 copy-start.167
  453.1 3.5 copy-start.11
  453.1 155.2 %reduce-scatter.5.cloned.1.call-start = ((), (), s32[]{:S(2)}) async-start(), calls=%async_computation.5 | async-start | bytes 3932160 | tf_op jit(solution)/shard_map/reduce_scatter | solution.py:524
  459.3 40.0 %copy-start.17 = (f32[256,768]{1,0:T(8,128)S(1)}, f32[256,768]{1,0:T(8,128)}, u32[]{:S(2)}) copy-start(f32[256,768]{1,0:T(8,128)} %copy-done.16) | copy-start | bytes 2359300
  459.3 40.0 %copy-start.136 = (f32[256]{0:T(256)S(1)}, f32[256]{0:T(256)}, u32[]{:S(2)}) copy-start(f32[256]{0:T(256)} %copy-done.135) | copy-start | bytes 3076
  497.2 5.1 copy-start.187
  499.3 7.2 slice-start.2
  502.3 7.8 copy-start.37
  502.3 4.2 slice-start.3
  532.2 4.9 copy-start.8
  537.1 3.8 copy-start.92
  537.1 3.8 copy-start.94
  546.8 5.0 copy-start.8
  551.8 3.8 copy-start.92
  551.8 3.8 copy-start.94
  575.3 3.5 copy-start.80
  596.5 13.8 %copy-start.15 = (f32[256,768]{1,0:T(8,128)S(1)}, f32[256,768]{1,0:T(8,128)}, u32[]{:S(2)}) copy-start(f32[256,768]{1,0:T(8,128)} %copy-done.13) | copy-start | bytes 2359300
  596.5 13.8 %copy-start.175 = (f32[256]{0:T(256)S(1)}, f32[256]{0:T(256)}, u32[]{:S(2)}) copy-start(f32[256]{0:T(256)} %copy-done.173) | copy-start | bytes 3076
  628.5 7.0 copy-start.119
  628.5 7.0 copy-start.121
  628.5 7.0 copy-start.123
  628.5 7.0 copy-start.125
  798.3 8.4 %copy-start.99 = (f32[24,4096]{1,0:T(8,128)S(1)}, f32[24,4096]{1,0:T(8,128)}, u32[]{:S(2)}) copy-start(f32[24,4096]{1,0:T(8,128)} %get-tuple-element.435) | copy-start | bytes 1179652
  798.3 8.5 %copy-start.98 = (f32[24,4096]{1,0:T(8,128)S(1)}, f32[24,4096]{1,0:T(8,128)}, u32[]{:S(2)}) copy-start(f32[24,4096]{1,0:T(8,128)} %get-tuple-element.434) | copy-start | bytes 1179652
  806.8 4.3 copy-start.102
  806.8 4.3 copy-start.103
  (168 other events, 357.7 us)
Sparse Core Ops, SparseCore 0:
  200.1 47.3 all-gather.2
  305.1 43.9 all-gather.4
  453.2 43.9 reduce-scatter.2
  564.4 43.9 reduce-scatter.4

commit v2 on v1

--- a/solution.py
+++ b/solution.py
@@ -5,6 +5,25 @@
 from jax.experimental import pallas as pl
 from jax.experimental.pallas import tpu as pltpu
 from jax.sharding import PartitionSpec as P
+
+
+CONV = 4
+PRECISE = lax.Precision.HIGHEST
+
+
+def padded(shard, sides, width):
+    for axis, dim in sides:
+        count, length = (lax.axis_size(axis), shard.shape[dim])
+        up = [(i, (i + 1) % count) for i in range(count - 1)]
+        down = [(j, i) for i, j in up]
+        last = lax.slice_in_dim(shard, length - width, length, axis=dim)
+        leading = lax.slice_in_dim(shard, 0, width, axis=dim)
+        before = lax.ppermute(last, axis, up)
+        after = lax.ppermute(leading, axis, down)
+        shard = jnp.concatenate([before, shard, after], axis=dim)
+    return shard
+
+
 MESH = pl.DeviceIdType.MESH
 CORES = 2
 
@@ -259,36 +278,372 @@
         compiler_params=pltpu.CompilerParams(collective_id=collective_id, has_side_effects=True, vmem_limit_bytes=60 << 20),
         name="scatter_grads",
     )(*parts)
-
 HEADS = 12
 HEAD_DIM = 64
-CONV = 4
-
-
+CHUNK = 256
 NORM_EPS = 1e-06
 NEG_FILL = -1000000000.0
-PRECISE = lax.Precision.HIGHEST
-
-
-def padded(shard, sides, width):
-    for axis, dim in sides:
-        count, length = (lax.axis_size(axis), shard.shape[dim])
-        up = [(i, (i + 1) % count) for i in range(count - 1)]
-        down = [(j, i) for i, j in up]
-        last = lax.slice_in_dim(shard, length - width, length, axis=dim)
-        leading = lax.slice_in_dim(shard, 0, width, axis=dim)
-        before = lax.ppermute(last, axis, up)
-        after = lax.ppermute(leading, axis, down)
-        shard = jnp.concatenate([before, shard, after], axis=dim)
-    return shard
-
-
-def rms_scale(values, gain):
-    return values * lax.rsqrt(jnp.mean(values * values, -1, keepdims=True) + NORM_EPS) * gain
-
-
-def gated_unit(gate_act, up_act):
-    return jax.nn.gelu(gate_act, approximate=True) * up_act
+GELU_A = 0.7978845608028654
+GELU_B = 0.044715
+
+
+def dot(a, b):
+    return jnp.dot(a, b, preferred_element_type=jnp.float32)
+
+
+def dot_nt(a, b):
+    return lax.dot_general(a, b, (((1,), (1,)), ((), ())), preferred_element_type=jnp.float32)
+
+
+def low(v):
+    return v.astype(jnp.bfloat16)
+
+
+def flip(v):
+    return low(v.astype(jnp.float32).T)
+
+
+def inverse_rms(v):
+    return lax.rsqrt(jnp.mean(v * v, -1, keepdims=True) + NORM_EPS)
+
+
+def ends_of(lengths_ref):
+    ends, total = [], 0
+    for i in range(lengths_ref.shape[-1]):
+        total = total + lengths_ref[0, i]
+        ends.append(total)
+    return ends
+
+
+def segments(places, ends):
+    seg = jnp.zeros(places.shape, jnp.int32)
+    for end in ends:
+        seg = seg + jnp.where(places >= end, 1, 0)
+    return seg
+
+
+def heads_each():
+    return -(-HEADS // lax.axis_size("ctx"))
+
+
+def others():
+    size, me = lax.axis_size("ctx"), lax.axis_index("ctx")
+    return [lax.rem(me + 1 + i, size) for i in range(size)]
+
+
+def greet_group():
+    barrier = pltpu.get_barrier_semaphore()
+    peers_ = others()[:-1]
+    for p in peers_:
+        pl.semaphore_signal(barrier, inc=1, device_id=(lax.axis_index("dp"), p), device_id_type=MESH)
+    pl.semaphore_wait(barrier, len(peers_))
+
+
+def to_group(src, dst, sems, index, p):
+    return pltpu.make_async_remote_copy(
+        src_ref=src, dst_ref=dst, send_sem=sems.at[(0,) + index], recv_sem=sems.at[(1,) + index],
+        device_id=(lax.axis_index("dp"), p), device_id_type=MESH)
+
+
+def tokens_of(p, count):
+    return pl.ds(pl.multiple_of(p * count, count), count)
+
+
+def spread_heads(src, dst, sems, local_sem, each):
+    me = lax.axis_index("ctx")
+    count = src.shape[2]
+    copies = []
+    for h in range(each):
+        rows = pl.ds(h * HEAD_DIM, HEAD_DIM)
+        made = []
+        for i, p in enumerate(others()):
+            theirs = pl.ds(pl.multiple_of((p * each + h) * HEAD_DIM, HEAD_DIM), HEAD_DIM)
+            a, b = src.at[:, theirs], dst.at[:, rows, tokens_of(me, count)]
+            if i == lax.axis_size("ctx") - 1:
+                copy = pltpu.make_async_copy(a, b, local_sem.at[h])
+            else:
+                copy = to_group(a, b, sems, (h, i), p)
+            copy.start()
+            made.append(copy)
+        copies.append(made)
+    return copies
+
+
+def arrive(made):
+    for copy in made[:-1]:
+        copy.wait_recv()
+    made[-1].wait()
+
+
+def attention_forward(each, seg_all, ends, qkv, lse, out_send, att, qkv_copies, sems):
+    size, me = lax.axis_size("ctx"), lax.axis_index("ctx")
+    count = att.shape[1]
+    copies = []
+    for h in range(each):
+        arrive(qkv_copies[h])
+        rows = pl.ds(h * HEAD_DIM, HEAD_DIM)
+        key = flip(qkv[1, rows, :])
+        value_t = qkv[2, rows, :]
+        theirs = pl.ds(pl.multiple_of((me * each + h) * HEAD_DIM, HEAD_DIM), HEAD_DIM)
+        for i, p in enumerate(others()):
+            tokens = tokens_of(p, count)
+            seg_q = segments(2 * (p * count + lax.broadcasted_iota(jnp.int32, (1, count), 1)), ends)
+            scores = dot(key, qkv[0, rows, tokens])
+            scores = jnp.where(seg_all[...] == seg_q, scores, NEG_FILL)
+            top = jnp.max(scores, 0, keepdims=True)
+            probs = jnp.exp(scores - top)
+            total = jnp.sum(probs, 0, keepdims=True)
+            lse[h, :, tokens] = top + jnp.log(total)
+            result = low(dot(value_t, low(probs)) / total)
+            if i == size - 1:
+                att[theirs, :] = result
+            else:
+                out_send[h, i] = result
+                copy = to_group(out_send.at[h, i], att.at[theirs], sems, (h, i), p)
+                copy.start()
+                copies.append(copy)
+    return copies
+
+
+def gelu_parts(gate):
+    inner = jnp.tanh(GELU_A * (gate + GELU_B * gate * gate * gate))
+    half = 0.5 * (1.0 + inner)
+    slope = half + 0.5 * gate * (1.0 - inner * inner) * GELU_A * (1.0 + 3.0 * GELU_B * gate * gate)
+    return gate * half, slope
+
+
+def layer_forward_kernel(lengths, x, gain_a, gain_f, w_attn_hbm, w_ffn_hbm, w_down_hbm,
+                         out, middle, normed_t, qkv, lse, att, gate_out, up_out, nffn_t,
+                         w_attn, w_ffn, w_down, qkv_all, out_send, seg_all, nffn,
+                         sems_in, sems_out, local_sems, w_sems):
+    each = heads_each()
+    model = x.shape[1]
+    loads = [pltpu.make_async_copy(a, b, w_sems.at[i]) for i, (a, b) in enumerate(
+        ((w_attn_hbm, w_attn), (w_ffn_hbm, w_ffn), (w_down_hbm, w_down)))]
+    for load in loads:
+        load.start()
+    greet_group()
+    ends = ends_of(lengths)
+    seg_all[...] = segments(2 * lax.broadcasted_iota(jnp.int32, seg_all.shape, 0), ends)
+    stream = x[...]
+    normed = low(stream * inverse_rms(stream) * gain_a[...])
+    normed_t[...] = flip(normed)
+    if qkv_all.shape[1] > model:
+        qkv_all[:, model:, :] = jnp.zeros((3, qkv_all.shape[1] - model, qkv_all.shape[2]), jnp.bfloat16)
+    loads[0].wait()
+    for part in range(3):
+        for c in range(model // CHUNK):
+            columns = pl.ds(part * model + c * CHUNK, CHUNK)
+            qkv_all[part, c * CHUNK:(c + 1) * CHUNK, :] = low(dot(normed, w_attn[:, columns]).T)
+    qkv_copies = spread_heads(qkv_all, qkv, sems_in, local_sems, each)
+    out_copies = attention_forward(each, seg_all, ends, qkv, lse, out_send, att, qkv_copies, sems_out)
+    for copy in out_copies:
+        copy.wait_recv()
+    attended = flip(att[:model, :])
+    mid = stream + dot(attended, w_attn[:, 3 * model:])
+    middle[...] = mid
+    after = low(mid * inverse_rms(mid) * gain_f[...])
+    nffn[...] = after
+    nffn_t[...] = flip(after)
+    out[...] = mid
+    loads[1].wait()
+    loads[2].wait()
+    hidden_count = w_down.shape[0]
+
+    def step(c, carry):
+        columns = pl.ds(pl.multiple_of(c * CHUNK, CHUNK), CHUNK)
+        gate = dot(nffn[...], w_ffn[:, columns])
+        up = dot(nffn[...], w_ffn[:, pl.ds(pl.multiple_of(hidden_count + c * CHUNK, CHUNK), CHUNK)])
+        gate_out[:, columns] = gate
+        up_out[:, columns] = up
+        hidden = low(gelu_parts(gate)[0] * up)
+        out[...] += dot(hidden, w_down[columns, :])
+        return carry
+    lax.fori_loop(0, hidden_count // CHUNK, step, 0)
+    for made in qkv_copies:
+        for copy in made[:-1]:
+            copy.wait_send()
+    for copy in out_copies:
+        copy.wait_send()
+
+
+VMEM = pl.BlockSpec(memory_space=pltpu.VMEM)
+ANY = pl.BlockSpec(memory_space=pl.ANY)
+SMEM = pl.BlockSpec(memory_space=pltpu.SMEM)
+
+
+def layer_forward(lengths, x, gain_a, gain_f, w_attn, w_ffn, w_down, collective_id):
+    size, each = lax.axis_size("ctx"), heads_each()
+    count, model = x.shape
+    wide = w_down.shape[0]
+    group = count * size
+    rows = each * size * HEAD_DIM
+    f32, bf16 = jnp.float32, jnp.bfloat16
+    made = lambda shape, dtype: jax.ShapeDtypeStruct(shape, dtype)
+    return pl.pallas_call(
+        layer_forward_kernel,
+        out_shape=[made((count, model), f32), made((count, model), f32), made((model, count), bf16),
+                   made((3, each * HEAD_DIM, group), bf16), made((each, 1, group), f32), made((rows, count), bf16),
+                   made((count, wide), f32), made((count, wide), f32), made((model, count), bf16)],
+        in_specs=[SMEM, VMEM, VMEM, VMEM, ANY, ANY, ANY],
+        out_specs=[VMEM] * 9,
+        scratch_shapes=[
+            pltpu.VMEM(w_attn.shape, bf16), pltpu.VMEM(w_ffn.shape, bf16), pltpu.VMEM(w_down.shape, bf16),
+            pltpu.VMEM((3, rows, count), bf16), pltpu.VMEM((each, size - 1, HEAD_DIM, count), bf16),
+            pltpu.VMEM((group, count), jnp.int32), pltpu.VMEM((count, model), bf16),
+            pltpu.SemaphoreType.DMA((2, each, size - 1)), pltpu.SemaphoreType.DMA((2, each, size - 1)),
+            pltpu.SemaphoreType.DMA((each,)), pltpu.SemaphoreType.DMA((3,))],
+        compiler_params=pltpu.CompilerParams(collective_id=collective_id, has_side_effects=True, vmem_limit_bytes=56 << 20),
+        name="layer_forward",
+    )(lengths, x, gain_a, gain_f, w_attn, w_ffn, w_down)
+
+
+def layer_backward_kernel(lengths, grad, x, gain_a, gain_f, middle, normed_t, qkv, lse, att, gate_in, up_in, nffn_t,
+                          w_attn_hbm, w_ffn_hbm, w_down_hbm,
+                          grad_in, d_gain_a, d_gain_f, d_attn_hbm, d_ffn_hbm, d_down_hbm,
+                          w_attn, w_ffn, w_down, d_attn, d_ffn, d_down, go_all, go, dqkv, q_send, kv_send, seg_all, total,
+                          grad_low, mid_low, sems_in, sems_q, sems_kv, local_sems, w_sems, d_sems):
+    each = heads_each()
+    size, me = lax.axis_size("ctx"), lax.axis_index("ctx")
+    count, model = x.shape
+    wide = w_down.shape[0]
+    loads = [pltpu.make_async_copy(a, b, w_sems.at[i]) for i, (a, b) in enumerate(
+        ((w_down_hbm, w_down), (w_ffn_hbm, w_ffn), (w_attn_hbm, w_attn)))]
+    for load in loads:
+        load.start()
+    greet_group()
+    ends = ends_of(lengths)
+    seg_all[...] = segments(2 * lax.broadcasted_iota(jnp.int32, seg_all.shape, 0), ends)
+    grad_low[...] = low(grad[...])
+    total[...] = jnp.zeros(total.shape, jnp.float32)
+    loads[0].wait()
+    loads[1].wait()
+
+    def step(c, carry):
+        columns = pl.ds(pl.multiple_of(c * CHUNK, CHUNK), CHUNK)
+        later = pl.ds(pl.multiple_of(wide + c * CHUNK, CHUNK), CHUNK)
+        g_hidden = dot_nt(grad_low[...], w_down[columns, :])
+        up = up_in[:, columns]
+        act, slope = gelu_parts(gate_in[:, columns])
+        g_gate = low(g_hidden * up * slope)
+        g_up = low(g_hidden * act)
+        d_down[columns, :] = low(dot(low((act * up).T), grad_low[...]))
+        d_ffn[:, columns] = low(dot(nffn_t[...], g_gate))
+        d_ffn[:, later] = low(dot(nffn_t[...], g_up))
+        total[...] += dot_nt(g_gate, w_ffn[:, columns]) + dot_nt(g_up, w_ffn[:, later])
+        return carry
+    lax.fori_loop(0, wide // CHUNK, step, 0)
+    saves = [pltpu.make_async_copy(d_ffn, d_ffn_hbm, d_sems.at[0]), pltpu.make_async_copy(d_down, d_down_hbm, d_sems.at[1])]
+    for save in saves:
+        save.start()
+
+    def norm_back(values, gain, upstream):
+        scale = inverse_rms(values)
+        scaled = upstream * gain
+        along = jnp.mean(values * scaled, -1, keepdims=True)
+        return scale * scaled - values * (scale * scale * scale * along), jnp.sum(upstream * values * scale, 0, keepdims=True)
+
+    back, d_gain = norm_back(middle[...], gain_f[...], total[...])
+    d_gain_f[...] = d_gain
+    grad_in[...] = grad[...] + back
+    mid_low[...] = low(grad_in[...])
+    if go_all.shape[1] > model:
+        go_all[:, model:, :] = jnp.zeros((1, go_all.shape[1] - model, count), jnp.bfloat16)
+    loads[2].wait()
+    for c in range(model // CHUNK):
+        rows = slice(c * CHUNK, (c + 1) * CHUNK)
+        go_all[0, rows, :] = low(dot_nt(mid_low[...], w_attn[rows, 3 * model:]).T)
+    go_copies = spread_heads(go_all, go, sems_in, local_sems, each)
+    for c in range(model // CHUNK):
+        rows = slice(c * CHUNK, (c + 1) * CHUNK)
+        d_attn[rows, 3 * model:] = low(dot(att[rows, :], mid_low[...]))
+    sent = []
+    for h in range(each):
+        arrive(go_copies[h])
+        rows = pl.ds(h * HEAD_DIM, HEAD_DIM)
+        theirs = pl.ds(pl.multiple_of((me * each + h) * HEAD_DIM, HEAD_DIM), HEAD_DIM)
+        key_t = qkv[1, rows, :]
+        key, value = flip(key_t), flip(qkv[2, rows, :])
+        g_key = jnp.zeros((HEAD_DIM, count * size), jnp.float32)
+        g_value = jnp.zeros((HEAD_DIM, count * size), jnp.float32)
+        for i, p in enumerate(others()):
+            tokens = tokens_of(p, count)
+            seg_q = segments(2 * (p * count + lax.broadcasted_iota(jnp.int32, (1, count), 1)), ends)
+            query_t, go_t = qkv[0, rows, tokens], go[0, rows, tokens]
+            scores = jnp.where(seg_all[...] == seg_q, dot(key, query_t), NEG_FILL)
+            probs = jnp.exp(scores - lse[h, :, tokens])
+            g_probs = dot(value, go_t)
+            inner = jnp.sum(probs * g_probs, 0, keepdims=True)
+            g_scores = low(probs * (g_probs - inner))
+            g_query = low(dot(key_t, g_scores))
+            g_key = g_key + dot_nt(query_t, g_scores)
+            g_value = g_value + dot_nt(go_t, low(probs))
+            if i == size - 1:
+                dqkv[0, theirs, :] = g_query
+            else:
+                q_send[h, i] = g_query
+                copy = to_group(q_send.at[h, i], dqkv.at[0, theirs], sems_q, (h, i), p)
+                copy.start()
+                sent.append(copy)
+        kv_send[h, 0] = low(g_key)
+        kv_send[h, 1] = low(g_value)
+        for i, p in enumerate(others()):
+            if i == size - 1:
+                dqkv[1:, theirs, :] = kv_send[h, :, :, tokens_of(me, count)]
+            else:
+                copy = to_group(kv_send.at[h, :, :, tokens_of(p, count)], dqkv.at[pl.ds(1, 2), theirs], sems_kv, (h, i), p)
+                copy.start()
+                sent.append(copy)
+    for copy in sent:
+        copy.wait_recv()
+    summed = jnp.zeros((model, count), jnp.float32)
+    for part in range(3):
+        for c in range(model // CHUNK):
+            rows = slice(c * CHUNK, (c + 1) * CHUNK)
+            columns = slice(part * model + c * CHUNK, part * model + (c + 1) * CHUNK)
+            d_attn[:, columns] = low(dot_nt(normed_t[...], dqkv[part, rows, :]))
+        summed = summed + dot(w_attn[:, part * model:(part + 1) * model], dqkv[part, :model, :])
+    saves.append(pltpu.make_async_copy(d_attn, d_attn_hbm, d_sems.at[2]))
+    saves[-1].start()
+    back, d_gain = norm_back(x[...], gain_a[...], summed.T)
+    d_gain_a[...] = d_gain
+    grad_in[...] += back
+    for made in go_copies:
+        for copy in made[:-1]:
+            copy.wait_send()
+    for copy in sent:
+        copy.wait_send()
+    for save in saves:
+        save.wait()
+
+
+def layer_backward(lengths, grad, x, gain_a, gain_f, kept, w_attn, w_ffn, w_down, collective_id):
+    size, each = lax.axis_size("ctx"), heads_each()
+    count, model = x.shape
+    wide = w_down.shape[0]
+    group = count * size
+    rows = each * size * HEAD_DIM
+    f32, bf16 = jnp.float32, jnp.bfloat16
+    made = lambda shape, dtype: jax.ShapeDtypeStruct(shape, dtype)
+    return pl.pallas_call(
+        layer_backward_kernel,
+        out_shape=[made((count, model), f32), made((1, model), f32), made((1, model), f32),
+                   made(w_attn.shape, bf16), made(w_ffn.shape, bf16), made(w_down.shape, bf16)],
+        in_specs=[SMEM] + [VMEM] * 12 + [ANY] * 3,
+        out_specs=[VMEM] * 3 + [ANY] * 3,
+        scratch_shapes=[
+            pltpu.VMEM(w_attn.shape, bf16), pltpu.VMEM(w_ffn.shape, bf16), pltpu.VMEM(w_down.shape, bf16),
+            pltpu.VMEM(w_attn.shape, bf16), pltpu.VMEM(w_ffn.shape, bf16), pltpu.VMEM(w_down.shape, bf16),
+            pltpu.VMEM((1, rows, count), bf16), pltpu.VMEM((1, each * HEAD_DIM, group), bf16),
+            pltpu.VMEM((3, rows, count), bf16), pltpu.VMEM((each, size - 1, HEAD_DIM, count), bf16),
+            pltpu.VMEM((each, 2, HEAD_DIM, group), bf16), pltpu.VMEM((group, count), jnp.int32),
+            pltpu.VMEM((count, model), f32), pltpu.VMEM((count, model), bf16), pltpu.VMEM((count, model), bf16),
+            pltpu.SemaphoreType.DMA((2, each, size - 1)), pltpu.SemaphoreType.DMA((2, each, size - 1)),
+            pltpu.SemaphoreType.DMA((2, each, size - 1)), pltpu.SemaphoreType.DMA((each,)),
+            pltpu.SemaphoreType.DMA((3,)), pltpu.SemaphoreType.DMA((3,))],
+        compiler_params=pltpu.CompilerParams(collective_id=collective_id, has_side_effects=True, vmem_limit_bytes=60 << 20),
+        name="layer_backward",
+    )(lengths, grad, x, gain_a, gain_f, *kept, w_attn, w_ffn, w_down)
 
 
 def segment_of(places, ends):
@@ -340,211 +695,6 @@
     return chosen.reshape(byte_count // 2, 2, -1).mean(1)
 
 
-def block_scores(q_heads, key_block, q_seg, key_seg_row):
-    scores = jnp.einsum("qhd,khd->hqk", q_heads, key_block, preferred_element_type=jnp.float32)
-    same = q_seg[None, :, None] == key_seg_row[None, None, :]
-    return jnp.where(same, scores, NEG_FILL)
-
-
-def softmax_totals(q_heads, q_seg, key_blocks, seg_blocks):
-    row_count, head_count = (q_heads.shape[0], q_heads.shape[1])
-
-    def softmax_block_step(state_pair, block_item):
-        top_score, exp_total = state_pair
-        key_block, seg_row = block_item
-        scores = block_scores(q_heads, key_block, q_seg, seg_row)
-        new_top = jnp.maximum(top_score, jnp.max(scores, -1))
-        exp_total = exp_total * jnp.exp(top_score - new_top) + jnp.sum(
-            jnp.exp(scores - new_top[..., None]), -1
-        )
-        return ((new_top, exp_total), None)
-
-    initial = (
-        jnp.full((head_count, row_count), NEG_FILL, jnp.float32),
-        jnp.zeros((head_count, row_count), jnp.float32),
-    )
-    (top_score, exp_total), _ = lax.scan(softmax_block_step, initial, (key_blocks, seg_blocks))
-    return top_score + jnp.log(exp_total)
-
-
-def weighted_values(q_heads, q_seg, key_blocks, value_blocks, seg_blocks, log_total):
-
-    def weighted_block_step(running, block_item):
-        key_block, value_block, seg_row = block_item
-        attn_probs = jnp.exp(
-            block_scores(q_heads, key_block, q_seg, seg_row) - log_total[..., None]
-        )
-        running = running + jnp.einsum(
-            "hqk,khd->qhd",
-            attn_probs.astype(jnp.bfloat16),
-            value_block,
-            preferred_element_type=jnp.float32,
-        )
-        return (running, None)
-
-    running, _ = lax.scan(
-        weighted_block_step,
-        jnp.zeros(q_heads.shape, jnp.float32),
-        (key_blocks, value_blocks, seg_blocks),
-    )
-    return running
-
-
-def attention_back(q_heads, q_seg, key_blocks, value_blocks, seg_blocks, log_total, grad_heads):
-
-    def inner_step(running, block_item):
-        key_block, value_block, seg_row = block_item
-        attn_probs = jnp.exp(
-            block_scores(q_heads, key_block, q_seg, seg_row) - log_total[..., None]
-        )
-        grad_probs = jnp.einsum(
-            "qhd,khd->hqk", grad_heads, value_block, preferred_element_type=jnp.float32
-        )
-        return (running + jnp.sum(attn_probs * grad_probs, -1), None)
-
-    inner_sum, _ = lax.scan(
-        inner_step, jnp.zeros(log_total.shape, jnp.float32), (key_blocks, value_blocks, seg_blocks)
-    )
-
-    def grad_step(running, block_item):
-        key_block, value_block, seg_row = block_item
-        attn_probs = jnp.exp(
-            block_scores(q_heads, key_block, q_seg, seg_row) - log_total[..., None]
-        )
-        grad_probs = jnp.einsum(
-            "qhd,khd->hqk", grad_heads, value_block, preferred_element_type=jnp.float32
-        )
-        grad_scores = (attn_probs * (grad_probs - inner_sum[..., None])).astype(jnp.bfloat16)
-        running = running + jnp.einsum(
-            "hqk,khd->qhd", grad_scores, key_block, preferred_element_type=jnp.float32
-        )
-        grad_key = jnp.einsum(
-            "hqk,qhd->khd", grad_scores, q_heads, preferred_element_type=jnp.float32
-        )
-        grad_value = jnp.einsum(
-            "hqk,qhd->khd",
-            attn_probs.astype(jnp.bfloat16),
-            grad_heads,
-            preferred_element_type=jnp.float32,
-        )
-        return (running, (grad_key, grad_value))
-
-    grad_query, key_parts = lax.scan(
-        grad_step, jnp.zeros(q_heads.shape, jnp.float32), (key_blocks, value_blocks, seg_blocks)
-    )
-    grad_key, grad_value = key_parts
-    merged = grad_key.shape[2] * grad_key.shape[3]
-    return (grad_query, inner_sum, grad_key.reshape(-1, merged), grad_value.reshape(-1, merged))
-
-
-def layer_forward(stream_in, weights, masks):
-    gain_attn, w_query, w_key, w_value, w_out, gain_ffn, w_gate, w_up, w_down = weights
-    q_seg, tok_seg, seg_blocks = masks
-    row_count = stream_in.shape[0]
-    normed = rms_scale(stream_in, gain_attn.astype(jnp.float32)).astype(jnp.bfloat16)
-    query_act = jnp.dot(normed, w_query, preferred_element_type=jnp.float32).astype(jnp.bfloat16)
-    key_act = jnp.dot(normed, w_key, preferred_element_type=jnp.float32).astype(jnp.bfloat16)
-    value_act = jnp.dot(normed, w_value, preferred_element_type=jnp.float32).astype(jnp.bfloat16)
-    both = lax.all_gather(jnp.concatenate([key_act, value_act], 1), "ctx", axis=0, tiled=True)
-    key_all, value_all = both[:, : both.shape[1] // 2], both[:, both.shape[1] // 2 :]
-    block_count, block_rows = seg_blocks.shape
-    q_heads = query_act.reshape(row_count, HEADS, HEAD_DIM)
-    key_own = key_act.reshape(row_count, HEADS, HEAD_DIM)
-    value_own = value_act.reshape(row_count, HEADS, HEAD_DIM)
-    key_blocks = key_all.reshape(block_count, block_rows, HEADS, HEAD_DIM)
-    value_blocks = value_all.reshape(block_count, block_rows, HEADS, HEAD_DIM)
-    log_total = softmax_totals(q_heads, q_seg, key_blocks, seg_blocks)
-    attended = weighted_values(q_heads, q_seg, key_blocks, value_blocks, seg_blocks, log_total)
-    attended = attended.reshape(row_count, -1).astype(jnp.bfloat16)
-    middle = stream_in + jnp.dot(attended, w_out, preferred_element_type=jnp.float32)
-    normed_ffn = rms_scale(middle, gain_ffn.astype(jnp.float32)).astype(jnp.bfloat16)
-    gate_act = jnp.dot(normed_ffn, w_gate, preferred_element_type=jnp.float32)
-    up_act = jnp.dot(normed_ffn, w_up, preferred_element_type=jnp.float32)
-    hidden = gated_unit(gate_act, up_act).astype(jnp.bfloat16)
-    result = middle + jnp.dot(hidden, w_down, preferred_element_type=jnp.float32)
-    saved = (
-        normed,
-        q_heads,
-        key_own,
-        value_own,
-        key_blocks,
-        value_blocks,
-        log_total,
-        attended,
-        middle,
-        normed_ffn,
-        gate_act,
-        up_act,
-        hidden,
-    )
-    return (result, saved)
-
-
-def layer_backward(stream_in, weights, masks, saved, grad_out):
-    gain_attn, w_query, w_key, w_value, w_out, gain_ffn, w_gate, w_up, w_down = weights
-    q_seg, tok_seg, seg_blocks = masks
-    (
-        normed,
-        q_heads,
-        key_own,
-        value_own,
-        key_blocks,
-        value_blocks,
-        log_total,
-        attended,
-        middle,
-        normed_ffn,
-        gate_act,
-        up_act,
-        hidden,
-    ) = saved
-    row_count = stream_in.shape[0]
-    grad_f = grad_out.astype(jnp.bfloat16)
-    d_down = jnp.dot(hidden.T, grad_f, preferred_element_type=jnp.float32)
-    grad_hidden = jnp.dot(grad_f, w_down.T, preferred_element_type=jnp.float32)
-    _, gated_back = jax.vjp(gated_unit, gate_act, up_act)
-    grad_gate, grad_up = gated_back(grad_hidden)
-    grad_gate = grad_gate.astype(jnp.bfloat16)
-    grad_up = grad_up.astype(jnp.bfloat16)
-    d_gate = jnp.dot(normed_ffn.T, grad_gate, preferred_element_type=jnp.float32)
-    d_up = jnp.dot(normed_ffn.T, grad_up, preferred_element_type=jnp.float32)
-    grad_nffn = jnp.dot(grad_gate, w_gate.T, preferred_element_type=jnp.float32) + jnp.dot(
-        grad_up, w_up.T, preferred_element_type=jnp.float32
-    )
-    _, norm_back = jax.vjp(rms_scale, middle, gain_ffn.astype(jnp.float32))
-    grad_mid, d_gain_ffn = norm_back(grad_nffn)
-    grad_mid = grad_mid + grad_out
-    grad_att = grad_mid.astype(jnp.bfloat16)
-    d_out = jnp.dot(attended.T, grad_att, preferred_element_type=jnp.float32)
-    grad_heads = jnp.dot(grad_att, w_out.T, preferred_element_type=jnp.float32).astype(jnp.bfloat16)
-    grad_heads = grad_heads.reshape(row_count, HEADS, HEAD_DIM)
-    grad_query, inner_sum, grad_key_all, grad_value_all = attention_back(
-        q_heads, q_seg, key_blocks, value_blocks, seg_blocks, log_total, grad_heads
-    )
-    both = lax.psum_scatter(
-        jnp.concatenate([grad_key_all, grad_value_all], 1).astype(jnp.bfloat16), "ctx", scatter_dimension=0, tiled=True
-    )
-    grad_key, grad_value = both[:, : both.shape[1] // 2], both[:, both.shape[1] // 2 :]
-    grad_query = grad_query.reshape(row_count, -1).astype(jnp.bfloat16)
-    grad_key = grad_key.astype(jnp.bfloat16)
-    grad_value = grad_value.astype(jnp.bfloat16)
-    d_query = jnp.dot(normed.T, grad_query, preferred_element_type=jnp.float32)
-    d_key = jnp.dot(normed.T, grad_key, preferred_element_type=jnp.float32)
-    d_value = jnp.dot(normed.T, grad_value, preferred_element_type=jnp.float32)
-    grad_normed = (
-        jnp.dot(grad_query, w_query.T, preferred_element_type=jnp.float32)
-        + jnp.dot(grad_key, w_key.T, preferred_element_type=jnp.float32)
-        + jnp.dot(grad_value, w_value.T, preferred_element_type=jnp.float32)
-    )
-    _, first_back = jax.vjp(rms_scale, stream_in, gain_attn.astype(jnp.float32))
-    grad_in, d_gain_attn = first_back(grad_normed)
-    grad_in = grad_in + grad_mid
-    return (
-        grad_in,
-        (d_gain_attn, d_query, d_key, d_value, d_out, d_gain_ffn, d_gate, d_up, d_down),
-    )
-
-
 def packed_small(embed, conv_weight, conv_bias, scorer, norm_attn, norm_ffn):
     rows = jnp.concatenate([embed, conv_weight, conv_bias[None], scorer[None], norm_attn, norm_ffn], 0).T
     return jnp.pad(rows, ((0, 0), (0, -rows.shape[1] % 128)))
@@ -580,7 +730,6 @@
     vocab = embed.shape[0]
     model = query_w.shape[2]
     byte_count = byte_ids.shape[1]
-    tok_count = byte_count // 2
     seq_lengths = lengths[0]
     at = jnp.arange(seq_lengths.shape[0])
     ends = jnp.sum(jnp.where(at[:, None] >= at[None, :], seq_lengths[None, :], 0), 1).astype(jnp.int32)
@@ -591,13 +740,6 @@
     valid_ext = ((ext_places >= 0) & (ext_places < total_bytes)).astype(jnp.float32)
     seg_ext = segment_of(ext_places, ends)
     rel_ext = offset_in(ext_places, seg_ext, ends, seq_lengths)
-    group_tok = tok_count * ctx_count
-    block_rows = min(512, group_tok)
-    tok_seg = segment_of(2 * jnp.arange(group_tok, dtype=jnp.int32), ends)
-    q_seg = segment_of(first_byte + 2 * jnp.arange(tok_count, dtype=jnp.int32), ends)
-    seg_blocks = tok_seg.reshape(group_tok // block_rows, block_rows)
-    masks = (q_seg, tok_seg, seg_blocks)
-
     small = packed_small(embed, conv_weight, conv_bias, scorer, norm_attn, norm_ffn)
     shards = [small]
     for layer in range(layer_count):
@@ -617,24 +759,25 @@
         bias_full.astype(jnp.float32),
         scorer_full.astype(jnp.float32),
     )
+    gains_a, gains_f = norm_a.astype(jnp.float32), norm_f.astype(jnp.float32)
     kept = []
     for layer in range(layer_count):
-        attn, ffn, down = full[3 * layer : 3 * layer + 3]
-        weights = (norm_a[layer], attn[:, :model], attn[:, model : 2 * model], attn[:, 2 * model : 3 * model],
-                   attn[:, 3 * model :], norm_f[layer], ffn[:, : ffn.shape[1] // 2], ffn[:, ffn.shape[1] // 2 :], down)
+        weights = full[3 * layer : 3 * layer + 3]
         before = stream
-        stream, saved = layer_forward(stream, weights, masks)
-        kept.append((before, weights, saved))
+        stream, *saved = layer_forward(lengths, stream, gains_a[layer][None], gains_f[layer][None], *weights, 2)
+        kept.append((before, saved))
     encoded = stream.astype(jnp.bfloat16)[None]
     grad_stream = out_grad[0].astype(jnp.float32)
     partial = []
     gains = []
     for layer in reversed(range(layer_count)):
-        before, weights, saved = kept[layer]
-        grad_stream, grads = layer_backward(before, weights, masks, saved, grad_stream)
-        d_gain_attn, d_query, d_key, d_value, d_out, d_gain_ffn, d_gate, d_up, d_down = grads
-        partial = [jnp.concatenate([d_query, d_key, d_value, d_out], 1), jnp.concatenate([d_gate, d_up], 1), d_down] + partial
-        gains = [(d_gain_attn, d_gain_ffn)] + gains
+        before, saved = kept[layer]
+        weights = full[3 * layer : 3 * layer + 3]
+        grad_stream, d_gain_attn, d_gain_ffn, *grads = layer_backward(
+            lengths, grad_stream, before, gains_a[layer][None], gains_f[layer][None], saved, *weights, 3
+        )
+        partial = list(grads) + partial
+        gains = [(d_gain_attn[0], d_gain_ffn[0])] + gains
     grads = gbst_back(grad_stream)
     small_grad = packed_small(*grads, jnp.stack([a for a, _ in gains]), jnp.stack([f for _, f in gains]))
     outs = scatter_all([p.astype(jnp.bfloat16) for p in [small_grad] + partial], 1)

time: 826 us -> 559 us (0.68)
  matrix products: 183 us -> 10.5 us
  Pallas kernels: 300 us -> 455 us
  waiting for transfers between devices: 132 us -> 0.01 us
  local copies, waits for them, and re-layouts: 103 us -> 35 us
  other arithmetic: 74 us -> 40 us
  between operations: 17.1 us -> 1.44 us
    dot_general x78 -> x0, matrix products: 173 us -> none  [the longest x12 27.7 us: block_scores(): jnp.einsum('qhd,khd->hqk', q_heads, key_block, preferred_element_type=jnp...]
    pallas_call x0 -> x4, Pallas kernels: none -> 161 us  [the longest x2 90.1 us: layer_backward(): pl.pallas_call(layer_backward_kernel, out_shape=[made((count, model), f32...]
    all_gather x2 -> x0, waiting for transfers between devices: 82.7 us -> none  [layer_forward(): lax.all_gather(jnp.concatenate([key_act, value_act], 1), 'ctx', axis=0, t...]
    reduce_scatter x2 -> x0, waiting for transfers between devices: 49.7 us -> none  [layer_backward(): lax.psum_scatter(jnp.concatenate([grad_key_all, grad_value_all], 1).astyp...]
    unnamed x347 -> x51, local copies, waits for them, and re-layouts: 27.5 us -> 6.31 us
    concatenate x8 -> x0, other arithmetic: 17.7 us -> none  [the longest x2 6.86 us: on_device(): jnp.concatenate([d_gate, d_up], 1)]
    reduce_sum x5 -> x0, other arithmetic: 15.6 us -> none  [the longest x4 15.4 us: softmax_block_step(): jnp.sum(jnp.exp(scores - new_top[..., None]), -1)]
    another operation x8 -> x0, local copies, waits for them, and re-layouts: 14.6 us -> none
  transfers between devices with their start and end apart: 6 -> 2, of which waited for: 4 -> 0; matrix products, arithmetic and copies ran while one was open for 7% -> 3% of each run, Pallas kernels for 18% -> 27%
where the time goes in v2:
time: 559 us; the launch traced here: 549 us
  Pallas kernels  455 us (81%)
  other arithmetic  40 us (7%)
  local copies, waits for them, and re-layouts  35 us (6%)
  matrix products  10.5 us (2%)
  starting transfers between devices  6.75 us (1%)
    pallas_call x1, Pallas kernels, gather_all(): pl.pallas_call(functools.partial(gather_kernel, n), out_shape=[jax.ShapeD...  150 us
    pallas_call x1, Pallas kernels, scatter_all(): pl.pallas_call(functools.partial(scatter_kernel, n), out_shape=[jax.Shape...  144 us
    pallas_call x2, Pallas kernels, layer_backward(): pl.pallas_call(layer_backward_kernel, out_shape=[made((count, model), f32...  90.1 us
    pallas_call x2, Pallas kernels, layer_forward(): pl.pallas_call(layer_forward_kernel, out_shape=[made((count, model), f32)...  70.6 us
  transfers between devices with their start and end apart: 2, of which 0 were waited for; matrix products, arithmetic and copies ran while one was open for 3% of the time, Pallas kernels for 27%

profile of v2, /device:TPU:0, one launch (start us, length us, event | category | flops | bytes accessed | tf_op | source)
XLA Modules:
  0.0 548.6 jit_solution(8720676831989056005)
XLA Ops:
  0.7 0.7 slice_bitcast_fusion.32
  1.4 1.3 collective-permute-start.1
  2.7 5.5 collective-permute-start
  8.2 0.8 copy.60
  8.9 0.7 copy.61
  9.7 0.7 copy.62
  10.4 0.7 copy.63
  11.2 0.7 copy.64
  11.9 0.8 slice_bitcast_fusion.23
  12.7 0.8 slice_bitcast_fusion.24
  13.5 0.8 slice_bitcast_fusion.25
  14.3 0.8 slice_bitcast_fusion.26
  15.1 1.0 slice_bitcast_fusion.10
  16.1 1.0 slice_bitcast_fusion.11
  17.0 1.6 slice_bitcast_fusion.9
  19.4 0.8 pad_maximum_fusion.4
  20.1 0.7 pad_maximum_fusion.6
  20.9 150.3 %gather_weights.1 = (bf16[4,2,2,2,24,384]{5,4,3,2,1,0:T(8,128)(2,1)}, bf16[4,2,2,2,24,3072]{5,4,3,2,1,0:T(8,128)(2,1)}, bf16[4,2,2,2,24,4096]{5,4,3,2,1,0:T(8,12...) custom-call(bf16[24,384]{1,0:T(8,128)(2,1)} %pad.81.refs_0_, ...), custom_call_target="tpu_custom_call" | custom-call | tf_op jit(solution)/shard_map/gather_weights/pallas_call | solution.py:152
  171.2 1.3 copy.65
  173.3 0.7 fusion.49
  175.6 0.9 bitcast_convert_fusion.grad
  176.8 0.9 fusion.34
  177.7 1.0 add_multiply_fusion.1
  178.7 1.0 add_bitcast_fusion
  179.7 2.3 slice_bitcast_fusion.4
  182.1 3.8 fusion.54
  186.0 1.9 multiply_reduce_fusion.1
  187.9 3.0 reshape.152
  190.9 4.2 reduce_sum.127
  195.1 2.1 broadcast_multiply_fusion.2.x
  197.1 34.8 %layer_forward.2 = (f32[256,768]{1,0:T(8,128)}, f32[256,768]{1,0:T(8,128)}, bf16[768,256]{1,0:T(8,128)(2,1)}, bf16[3,192,1024]{2,1,0:T(8,128)(2,1)}, f32[3,1,102...) custom-call(s32[1,4]{1,0:T(1,128)} %lengths.7, ...), custom_call_target="tpu_custom_call" | custom-call | tf_op jit(solution)/shard_map/layer_forward/pallas_call | solution.py:483
  231.9 35.9 %layer_forward.3 = (f32[256,768]{1,0:T(8,128)}, f32[256,768]{1,0:T(8,128)}, bf16[768,256]{1,0:T(8,128)(2,1)}, bf16[3,192,1024]{2,1,0:T(8,128)(2,1)}, f32[3,1,102...) custom-call(s32[1,4]{1,0:T(1,128)} %lengths.7, ...), custom_call_target="tpu_custom_call" | custom-call | tf_op jit(solution)/shard_map/layer_forward/pallas_call | solution.py:483
  267.8 45.0 %layer_backward.2 = (f32[256,768]{1,0:T(8,128)}, f32[1,768]{1,0:T(1,128)}, f32[1,768]{1,0:T(1,128)}, bf16[768,3072]{1,0:T(8,128)(2,1)}, bf16[768,4096]{1,0:T(8,128)(2,1)}, /*index=5*/bf16[2048,768]{1,0:T(8,128)(2,1)}) custom-call(s32[1,4]{1,0:T(1,128)} %lengths.7, f32[256,768]{1,0:T(8,128)} %bitcast_convert_fusion.grad, f32[256,768]{1,0:T(8,128)} %get-tuple-element.62.x, ...), custom_call_target="tpu_custom_call" | custom-call | tf_op jit(solution)/shard_map/layer_backward/pallas_call | solution.py:628
  312.8 45.1 %layer_backward.3 = (f32[256,768]{1,0:T(8,128)}, f32[1,768]{1,0:T(1,128)}, f32[1,768]{1,0:T(1,128)}, bf16[768,3072]{1,0:T(8,128)(2,1)}, bf16[768,4096]{1,0:T(8,128)(2,1)}, /*index=5*/bf16[2048,768]{1,0:T(8,128)(2,1)}) custom-call(s32[1,4]{1,0:T(1,128)} %lengths.7, f32[256,768]{1,0:T(8,128)} %get-tuple-element.75.grad, ...), custom_call_target="tpu_custom_call" | custom-call | tf_op jit(solution)/shard_map/layer_backward/pallas_call | solution.py:628
  357.9 1.2 broadcast_multiply_fusion.1
  359.1 1.7 broadcast_in_dim.149
  360.8 3.1 reshape.159
  363.9 3.3 multiply_reduce_fusion
  367.3 0.8 multiply_add_fusion
  368.0 1.3 slice_bitcast_fusion
  369.3 3.2 fusion.25
  372.5 2.2 fusion.32
  374.7 6.7 %multiply_reduce_fusion.5 = (f32[768]{0:T(1024)S(1)}, f32[768]{0:T(1024)S(1)}, f32[768]{0:T(1024)S(1)}, f32[768]{0:T(1024)S(1)}, bf16[768]{0:T(1024)(128)(2,1)S(1)}, /*index=5*/f32[519,768]{1,0:T(8,128)S(1)}) fusion(f32[522,768]{1,0:T(8,128)S(1)} %fusion.34, f32[519]{0:T(1024)S(1)} %get-tuple-element.252, f32[519]{0:T(1024)S(1)} %get-tuple-element.253, ...), kind=kLoop, calls=%fused_computation.15 | loop fusion | flops 11156736 | bytes 33159792 | tf_op jit(solution)/shard_map/transpose(jvp())/reduce_sum | solution.py:670
  382.0 0.8 copy-done.1
  383.8 3.1 convolution_reduce_fusion
  386.9 2.8 fusion.18
  390.2 0.9 pad.106.clone
  391.1 143.9 %scatter_grads.1 = (f32[24,384]{1,0:T(8,128)}, f32[24,3072]{1,0:T(8,128)}, f32[24,4096]{1,0:T(8,128)}, f32[64,768]{1,0:T(8,128)}, f32[24,3072]{1,0:T(8,128)}, /*index=5*/f32[24,4096]{1,0:T(8,128)}, f32[64,768]{1,0:T(8,128)}) custom-call(bf16[4,2,2,2,24,384]{5,4,3,2,1,0:T(8,128)(2,1)} %bitcast.173, bf16[4,2,2,2,24,3072]{5,4,3,2,1,0:T(8,128)(2,1)} %bitcast.170, ...), custom_call_target="tpu_custom_call" | custom-call | tf_op jit(solution)/shard_map/scatter_grads/pallas_call | solution.py:272
  535.0 1.4 slice.352
  536.4 0.7 slice.353
  537.1 1.5 slice_reduce_fusion
  538.6 0.9 fusion.94
  539.5 0.8 convert_bitcast_fusion
  540.3 0.7 copy.68
  540.9 0.6 copy.69
  541.6 1.0 slice_bitcast_fusion.15
  542.6 0.6 copy.70
  543.4 0.7 pad_maximum_fusion.8
  544.0 0.7 pad_maximum_fusion.9
  544.7 0.7 pad_maximum_fusion.10
  545.4 0.7 pad_maximum_fusion.11
  546.1 0.8 pad_maximum_fusion.1
  546.8 0.8 pad_maximum_fusion.2
  547.6 0.8 pad_maximum_fusion.3
  (91 shorter events, 5.6 us)
Async XLA Ops:
  0.6 18.0 %copy-start.15 = (bf16[256,24]{0,1:T(8,128)(2,1)S(1)}, bf16[256,24]{0,1:T(8,128)(2,1)}, u32[]{:S(2)}) copy-start(bf16[256,24]{0,1:T(8,128)(2,1)} %param.18) | copy-start | bytes 36868
  1.4 175.3 %collective-permute-start.1 = (s32[5]{0:T(128)S(1)}, s32[5]{0:T(128)S(1)}, u32[]{:S(2)}, u32[]{:S(2)}) collective-permute-start(s32[5]{0:T(128)S(1)} %get-tuple-element.255), channel_id=1, source_target_pairs={{1,0},{2,1},{3,2},{5,4},{6,5},{7,6},{9,8},{10,9},{11,10},{13,12},{... | collective-permute-start | bytes 68 | tf_op jit(solution)/shard_map/ppermute | solution.py:22
  2.7 174.0 %collective-permute-start = (s32[5]{0:T(128)S(1)}, s32[5]{0:T(128)S(1)}, u32[]{:S(2)}, u32[]{:S(2)}) collective-permute-start(s32[5]{0:T(128)S(1)} %get-tuple-element.254), channel_id=1, source_target_pairs={{0,1},{1,2},{2,3},{4,5},{5,6},{6,7},{8,9},{9,10},{10,11},{12,13},{... | collective-permute-start | bytes 68 | tf_op jit(solution)/shard_map/ppermute | solution.py:21
  19.4 153.2 %copy-start.16 = (s32[1,4]{1,0:T(1,128)S(1)}, s32[1,4]{1,0:T(1,128)}, u32[]{:S(2)}) copy-start(s32[1,4]{1,0:T(1,128)} %lengths.7) | copy-start | bytes 52
  20.1 155.5 %copy-start.11 = (bf16[1,256,768]{2,1,0:T(8,128)(2,1)S(1)}, bf16[1,256,768]{2,1,0:T(8,128)(2,1)}, u32[]{:S(2)}) copy-start(bf16[1,256,768]{2,1,0:T(8,128)(2,1)} %param.31) | copy-start | bytes 1179652
  20.9 155.8 %copy-start.17 = (s32[1,512]{1,0:T(1,128)S(1)}, s32[1,512]{1,0:T(1,128)}, u32[]{:S(2)}) copy-start(s32[1,512]{1,0:T(1,128)} %param.16) | copy-start | bytes 6148
  172.5 5.2 copy-start.7
  179.7 6.3 %copy-start.5 = (f32[1,512,768]{2,1,0:T(8,128)}, f32[1,512,768]{2,1,0:T(8,128)S(1)}, u32[]{:S(2)}) copy-start(f32[1,512,768]{2,1,0:T(8,128)S(1)} %add_bitcast_fusion) | copy-start | bytes 4718596
  182.0 3.9 copy-start
  182.1 3.9 copy-start.2
  363.9 3.3 copy-start.4
  381.4 1.4 copy-start.1
  381.4 1.9 copy-start.3
  381.4 2.3 copy-start.6
  383.7 3.1 copy-start.21
  383.7 3.1 copy-start.19
  383.7 3.1 copy-start.20
  383.8 3.1 copy-start.18
  391.1 148.4 %copy-start.8 = (f32[256,768]{1,0:T(8,128)S(1)}, f32[256,768]{1,0:T(8,128)}, u32[]{:S(2)}) copy-start(f32[256,768]{1,0:T(8,128)} %get-tuple-element.66) | copy-start | bytes 2359300
  535.0 7.6 %copy-start.12 = (f32[24,3072]{1,0:T(8,128)S(1)}, f32[24,3072]{1,0:T(8,128)}, u32[]{:S(2)}) copy-start(f32[24,3072]{1,0:T(8,128)} %get-tuple-element.96) | copy-start | bytes 884740
  535.0 8.2 %copy-start.10 = (f32[24,4096]{1,0:T(8,128)S(1)}, f32[24,4096]{1,0:T(8,128)}, u32[]{:S(2)}) copy-start(f32[24,4096]{1,0:T(8,128)} %get-tuple-element.99) | copy-start | bytes 1179652
  539.5 3.8 copy-start.9
  543.3 4.3 copy-start.13
  543.3 4.3 copy-start.14

commit v3 on v2

--- a/solution.py
+++ b/solution.py
@@ -1,4 +1,5 @@
 import functools
+import math
 import jax
 import jax.numpy as jnp
 from jax import lax
@@ -7,25 +8,10 @@
 from jax.sharding import PartitionSpec as P
 
 
-CONV = 4
-PRECISE = lax.Precision.HIGHEST
-
-
-def padded(shard, sides, width):
-    for axis, dim in sides:
-        count, length = (lax.axis_size(axis), shard.shape[dim])
-        up = [(i, (i + 1) % count) for i in range(count - 1)]
-        down = [(j, i) for i, j in up]
-        last = lax.slice_in_dim(shard, length - width, length, axis=dim)
-        leading = lax.slice_in_dim(shard, 0, width, axis=dim)
-        before = lax.ppermute(last, axis, up)
-        after = lax.ppermute(leading, axis, down)
-        shard = jnp.concatenate([before, shard, after], axis=dim)
-    return shard
-
-
 MESH = pl.DeviceIdType.MESH
 CORES = 2
+LANES = 128
+THIRD = 0.18
 
 
 def grid_of():
@@ -45,116 +31,156 @@
     return (z * CORES + core, y * nx + x)
 
 
-def peers():
+def along(axis):
+    place = list(place_of())
     nz, ny, nx = grid_of()
+    size = (nz, CORES, ny, nx)[axis]
+    found = []
+    for i in range(1, size):
+        there = list(place)
+        there[axis] = lax.rem(place[axis] + i, size)
+        found.append((there[axis], device(*there)))
+    return found
+
+
+def sibling():
     z, core, y, x = place_of()
-    zs = [lax.rem(z + i, nz) for i in range(1, nz)]
-    ys = [lax.rem(y + i, ny) for i in range(1, ny)]
-    xs = [lax.rem(x + i, nx) for i in range(1, nx)]
-    return zs, ys, xs
-
-
-def greet(extra=()):
+    return device(z, 1 - core, y, x)
+
+
+def greet_all():
+    barrier = pltpu.get_barrier_semaphore()
+    targets = [target for axis in (0, 2, 3) for _, target in along(axis)] + [sibling()]
+    _, ny, nx = grid_of()
     z, core, y, x = place_of()
-    zs, ys, xs = peers()
-    barrier = pltpu.get_barrier_semaphore()
-    targets = [device(p, core, y, x) for p in zs]
-    targets += [device(z, core, p, x) for p in ys]
-    targets += [device(z, core, y, p) for p in xs]
-    targets += [device(z, 1 - core, y, x)]
-    targets += list(extra)
+    for i in range(1, ny):
+        for j in range(1, nx):
+            targets.append(device(z, core, lax.rem(y + i, ny), lax.rem(x + j, nx)))
     for target in targets:
         pl.semaphore_signal(barrier, inc=1, device_id=target, device_id_type=MESH)
     pl.semaphore_wait(barrier, len(targets))
-
-
-def remote(src, dst, sems, k, target):
-    return pltpu.make_async_remote_copy(
-        src_ref=src, dst_ref=dst, send_sem=sems.at[0, k], recv_sem=sems.at[1, k],
-        device_id=target, device_id_type=MESH)
-
-
-def halves(width):
-    left = -(-width // 256) * 128
-    return pl.ds(0, left), pl.ds(left, width - left)
-
-
-class GatherChunk:
-    def __init__(self, shard, out, sems, local_sem):
-        self.shard, self.out, self.sems, self.local_sem = shard, out, sems, local_sem
-        self.halves = halves(shard.shape[-1])
-        self.started = []
-
-    @staticmethod
-    def count():
-        nz, ny, nx = grid_of()
-        return (nz - 1) + 2 * (nx - 1) + 2 * (ny - 1) + 1
-
-    def send(self, where, target, kind):
-        k = sum(len(group) for group in self.started) + len(self.current)
-        copy = remote(self.out.at[where], self.out.at[where], self.sems, k, target)
+    return targets
+
+
+ORDERS = ((0, 3, 2), (0, 2, 3), (3, 2, 0))
+
+
+def pieces_of(width, third):
+    units = width // LANES
+    last = int(units * third)
+    left = (units - last + 1) // 2
+    found, at = [], 0
+    for order, size in zip(ORDERS, (left, units - last - left, last)):
+        if size:
+            found.append((pl.ds(at * LANES, size * LANES), order))
+        at += size
+    return found
+
+
+def hops(width, third):
+    nz, ny, nx = grid_of()
+    return len(pieces_of(width, third)) * (nz - 1 + ny - 1 + nx - 1) + 1
+
+
+class Sender:
+    def __init__(self, sems):
+        self.sems, self.count, self.flying = sems, 0, []
+
+    def send(self, src, dst, target):
+        copy = pltpu.make_async_remote_copy(
+            src_ref=src, dst_ref=dst, send_sem=self.sems.at[0, self.count], recv_sem=self.sems.at[1, self.count],
+            device_id=target, device_id_type=MESH)
         copy.start()
-        self.current.append(copy)
+        self.count += 1
+        self.flying.append(copy)
+        return copy
+
+    def finish(self):
+        for copy in self.flying:
+            copy.wait_send()
+
+
+class GatherChunk(Sender):
+    phases = 4
+
+    def __init__(self, shard, out, sems, local_sem, third):
+        super().__init__(sems)
+        self.shard, self.out, self.local_sem = shard, out, local_sem
+        self.pieces = pieces_of(shard.shape[-1], third)
+        self.waiting = []
 
     def stage(self, number):
-        z, core, y, x = place_of()
-        zs, ys, xs = peers()
-        left, right = self.halves
-        if number > 1:
-            for copy in self.started[-1]:
-                copy.wait_recv()
-        self.current = []
+        place = place_of()
+        for copy in self.waiting:
+            copy.wait_recv()
+        self.waiting = []
         if number == 0:
-            own = pltpu.make_async_copy(self.shard, self.out.at[z, core, y, x], self.local_sem)
-            own.start()
-            for i, p in enumerate(zs):
-                copy = remote(self.shard, self.out.at[z, core, y, x], self.sems, i, device(p, core, y, x))
-                copy.start()
-                self.current.append(copy)
-            self.own = own
-        elif number == 1:
-            for copy in self.started[-1]:
-                copy.wait_recv()
+            self.own = pltpu.make_async_copy(self.shard, self.out.at[place], self.local_sem)
+            self.own.start()
+        if number == 1:
             self.own.wait()
-            for p in xs:
-                self.send((slice(None), core, y, x, slice(None), left), device(z, core, y, p), 0)
-            for p in ys:
-                self.send((slice(None), core, y, x, slice(None), right), device(z, core, p, x), 0)
-        elif number == 2:
-            for p in ys:
-                self.send((slice(None), core, y, slice(None), slice(None), left), device(z, core, p, x), 0)
-            for p in xs:
-                self.send((slice(None), core, slice(None), x, slice(None), right), device(z, core, y, p), 0)
-        elif number == 3:
-            self.send((slice(None), core), device(z, 1 - core, y, x), 0)
-        self.started.append(self.current)
-        if number == 4:
-            for group in self.started:
-                for copy in group:
-                    copy.wait_send()
-
-
-def gather_kernel(n, *refs):
-    shards, outs, (sems, local_sems) = refs[:n], refs[n:2 * n], refs[2 * n:]
-    greet()
-    chunks = [GatherChunk(shards[i], outs[i], sems.at[i], local_sems.at[i]) for i in range(n)]
-    for t in range(n + 4):
-        for number in range(4):
-            if 0 <= t - number < n:
-                chunks[t - number].stage(number)
+        if number < 3:
+            for columns, order in self.pieces:
+                have = order[:number]
+                where = tuple(slice(None) if axis in have else place[axis] for axis in range(4)) + (slice(None), columns)
+                src = self.out.at[where] if number else self.shard.at[:, columns]
+                for _, target in along(order[number]):
+                    self.waiting.append(self.send(src, self.out.at[where], target))
+        else:
+            where = (slice(None), place[1])
+            self.waiting.append(self.send(self.out.at[where], self.out.at[where], sibling()))
+
+    def arrive(self):
+        for copy in self.waiting:
+            copy.wait_recv()
+        self.waiting = []
+
+
+class Ticker:
+    def __init__(self, chunks):
+        self.chunks, self.steps, self.done = chunks, [], [0] * len(chunks)
+        phases = chunks[0].phases
+        for t in range(len(chunks) + phases):
+            for number in [0] + list(range(phases - 1, 0, -1)):
+                if 0 <= t - number < len(chunks):
+                    self.steps.append((t - number, number))
+
+    def tick(self, count=1):
+        for _ in range(count):
+            if self.steps:
+                i, number = self.steps.pop(0)
+                self.chunks[i].stage(number)
+                self.done[i] = number + 1
+
+    def until(self, i):
+        while self.done[i] < self.chunks[i].phases:
+            self.tick()
+
+    def need(self, i):
+        self.until(i)
+        self.chunks[i].arrive()
+
+
+def gather_kernel(n, third, *refs):
+    shards, outs, sems, local_sems = refs[:n], refs[n:2 * n], refs[2 * n:3 * n], refs[3 * n]
+    greet_all()
+    chunks = [GatherChunk(shards[i], outs[i], sems[i], local_sems.at[i], third) for i in range(n)]
+    ticker = Ticker(chunks)
+    for i in range(n):
+        ticker.need(i)
     for chunk in chunks:
-        chunk.stage(4)
-
-
-def gather_all(shards, collective_id):
+        chunk.finish()
+
+
+def gather_all(shards, collective_id, third=THIRD):
     nz, ny, nx = grid_of()
     n = len(shards)
     outs = pl.pallas_call(
-        functools.partial(gather_kernel, n),
+        functools.partial(gather_kernel, n, third),
         out_shape=[jax.ShapeDtypeStruct((nz, CORES, ny, nx) + s.shape, s.dtype) for s in shards],
         in_specs=[pl.BlockSpec(memory_space=pl.ANY)] * n,
         out_specs=[pl.BlockSpec(memory_space=pl.ANY)] * n,
-        scratch_shapes=[pltpu.SemaphoreType.DMA((n, 2, GatherChunk.count())), pltpu.SemaphoreType.DMA((n,))],
+        scratch_shapes=[pltpu.SemaphoreType.DMA((2, hops(s.shape[-1], third))) for s in shards] + [pltpu.SemaphoreType.DMA((n,))],
         compiler_params=pltpu.CompilerParams(collective_id=collective_id, has_side_effects=True),
         name="gather_weights",
     )(*shards)
@@ -172,112 +198,105 @@
     lax.fori_loop(0, lead[0], body, 0)
 
 
-class ScatterChunk:
-    def __init__(self, parts, out, held, across, first, second, last, sems, local_sem):
-        self.parts, self.out, self.held, self.across = parts, out, held, across
-        self.first, self.second, self.last, self.sems, self.local_sem = first, second, last, sems, local_sem
-        self.halves = halves(parts.shape[-1])
-        self.copies = []
-        self.k = 0
-
-    count = GatherChunk.count
+class ScatterChunk(Sender):
+    phases = 5
+
+    def __init__(self, parts, out, scratch, sems, local_sem, third):
+        super().__init__(sems)
+        self.parts, self.out, self.local_sem = parts, out, local_sem
+        self.held, self.across, *landing = scratch
+        self.pieces = [(columns, order[::-1], landing[3 * i:3 * i + 3])
+                       for i, (columns, order) in enumerate(pieces_of(parts.shape[-1], third))]
+        self.waiting = []
 
     @staticmethod
-    def scratch(shape, dtype):
-        nz, ny, nx = grid_of()
-        r, n = shape
-        return [pltpu.VMEM((nz, ny, nx, r, n), dtype), pltpu.VMEM((nz, ny, nx, r, n), dtype),
-                pltpu.VMEM((nx - 1, nz, ny, r, halves(n)[0].size), dtype), pltpu.VMEM((ny - 1, nz, nx, r, halves(n)[1].size), dtype),
-                pltpu.VMEM((ny - 1, nz, r, halves(n)[0].size), dtype), pltpu.VMEM((nx - 1, nz, r, halves(n)[1].size), dtype),
-                pltpu.VMEM((nz - 1, r, n), dtype)]
-
-    def send(self, src, dst, target):
-        copy = remote(src, dst, self.sems, self.k, target)
-        self.k += 1
-        copy.start()
-        self.current.append(copy)
+    def scratch(shape, dtype, third):
+        sizes = dict(zip((0, 2, 3), grid_of()))
+        whole = (*sizes.values(), *shape)
+        found = [whole, whole]
+        for columns, order in pieces_of(shape[-1], third):
+            order = order[::-1]
+            for number in range(3):
+                rest = [sizes[a] for a in sizes if a in order[number + 1:]]
+                found.append((sizes[order[number]] - 1, *rest, shape[0], columns.size))
+        return [pltpu.VMEM(s, dtype) for s in found]
 
     def stage(self, number):
-        nz, ny, nx = grid_of()
-        z, core, y, x = place_of()
-        zs, ys, xs = peers()
-        left, right = self.halves
-        held = self.held
-        every = slice(None)
-        if number:
-            for copy in self.current:
-                copy.wait_recv()
-        done = self.current if number else []
-        self.current = []
+        place = place_of()
+        sizes = dict(zip((0, 2, 3), grid_of()))
+        for copy in self.waiting:
+            copy.wait_recv()
+        self.waiting = []
         if number == 0:
-            self.own = pltpu.make_async_copy(self.parts.at[:, core], held, self.local_sem)
+            self.own = pltpu.make_async_copy(self.parts.at[:, place[1]], self.held, self.local_sem)
             self.own.start()
-            self.send(self.parts.at[:, 1 - core], self.across, device(z, 1 - core, y, x))
-        elif number == 1:
+            self.waiting.append(self.send(self.parts.at[:, 1 - place[1]], self.across, sibling()))
+            return
+        if number == 1:
             self.own.wait()
-            add_into(held, self.across, (nz, ny, nx))
-            for i, p in enumerate(xs):
-                self.send(held.at[:, :, p, :, left], self.first[0].at[i], device(z, core, y, p))
-            for i, p in enumerate(ys):
-                self.send(held.at[:, p, :, :, right], self.first[1].at[i], device(z, core, p, x))
-        elif number == 2:
-            for i in range(nx - 1):
-                add_into(held.at[:, :, x, :, left], self.first[0].at[i], (nz, ny))
-            for i in range(ny - 1):
-                add_into(held.at[:, y, :, :, right], self.first[1].at[i], (nz, nx))
-            for i, p in enumerate(ys):
-                self.send(held.at[:, p, x, :, left], self.second[0].at[i], device(z, core, p, x))
-            for i, p in enumerate(xs):
-                self.send(held.at[:, y, p, :, right], self.second[1].at[i], device(z, core, y, p))
-        elif number == 3:
-            for i in range(ny - 1):
-                add_into(held.at[:, y, x, :, left], self.second[0].at[i], (nz,))
-            for i in range(nx - 1):
-                add_into(held.at[:, y, x, :, right], self.second[1].at[i], (nz,))
-            for i, p in enumerate(zs):
-                self.send(held.at[p, y, x], self.last.at[i], device(p, core, y, x))
-        elif number == 4:
-            total = held[z, y, x].astype(jnp.float32)
-            for i in range(nz - 1):
-                total = total + self.last[i].astype(jnp.float32)
-            self.out[...] = total
-        self.copies += done
-        if number == 4:
-            for copy in self.copies:
-                copy.wait_send()
-
-
-def scatter_kernel(n, *refs):
-    parts, outs, rest = refs[:n], refs[n:2 * n], refs[2 * n:]
-    sems, local_sems = rest[-2:]
-    greet()
+            add_into(self.held, self.across, list(sizes.values()))
+        for columns, order, landing in self.pieces:
+            if number > 1:
+                mine = order[:number - 1]
+                where = tuple(place[a] if a in mine else slice(None) for a in sizes) + (slice(None), columns)
+                lead = [sizes[a] for a in sizes if a not in mine]
+                landed = landing[number - 2]
+                if number < 4:
+                    for i in range(landed.shape[0]):
+                        add_into(self.held.at[where], landed.at[i], lead)
+                else:
+                    total = self.held[where].astype(jnp.float32)
+                    for i in range(landed.shape[0]):
+                        total = total + landed[i].astype(jnp.float32)
+                    self.out[:, columns] = total
+            if number < 4:
+                axis, mine = order[number - 1], order[:number - 1]
+                for i, (there, target) in enumerate(along(axis)):
+                    where = tuple(there if a == axis else place[a] if a in mine else slice(None) for a in sizes)
+                    src = self.held.at[where + (slice(None), columns)]
+                    self.waiting.append(self.send(src, landing[number - 1].at[i], target))
+
+
+def scatter_kernel(n, third, counts, *refs):
+    parts, outs, rest = refs[:n], refs[n:2 * n], list(refs[2 * n:])
+    greet_all()
     chunks = []
     for i in range(n):
-        s = rest[7 * i:7 * i + 7]
-        chunks.append(ScatterChunk(parts[i], outs[i], s[0], s[1], s[2:4], s[4:6], s[6], sems.at[i], local_sems.at[i]))
-    for t in range(n + 4):
-        for number in range(5):
-            if 0 <= t - number < n:
-                chunks[t - number].stage(number)
-
-
-def scatter_all(parts, collective_id):
+        scratch = [rest.pop(0) for _ in range(counts[i])]
+        chunks.append(ScatterChunk(parts[i], outs[i], scratch, rest.pop(0), rest.pop(0), third))
+    ticker = Ticker(chunks)
+    for i in range(n):
+        ticker.until(i)
+    for chunk in chunks:
+        chunk.finish()
+
+
+def scatter_scratch(shape, dtype, third):
+    scratch = ScatterChunk.scratch(shape, dtype, third)
+    return scratch + [pltpu.SemaphoreType.DMA((2, hops(shape[-1], third))), pltpu.SemaphoreType.DMA]
+
+
+def scatter_all(parts, collective_id, third=THIRD):
     nz, ny, nx = grid_of()
     n = len(parts)
     devices = nz * CORES * ny * nx
     parts = [p.reshape((nz, CORES, ny, nx, p.shape[0] // devices) + p.shape[1:]) for p in parts]
-    scratch = []
+    scratch, counts = [], []
     for p in parts:
-        scratch += ScatterChunk.scratch(p.shape[4:], p.dtype)
+        made = scatter_scratch(p.shape[4:], p.dtype, third)
+        counts.append(len(made) - 2)
+        scratch += made
     return pl.pallas_call(
-        functools.partial(scatter_kernel, n),
+        functools.partial(scatter_kernel, n, third, counts),
         out_shape=[jax.ShapeDtypeStruct(p.shape[4:], jnp.float32) for p in parts],
         in_specs=[pl.BlockSpec(memory_space=pl.ANY)] * n,
         out_specs=[pl.BlockSpec(memory_space=pltpu.VMEM)] * n,
-        scratch_shapes=scratch + [pltpu.SemaphoreType.DMA((n, 2, GatherChunk.count())), pltpu.SemaphoreType.DMA((n,))],
+        scratch_shapes=scratch,
         compiler_params=pltpu.CompilerParams(collective_id=collective_id, has_side_effects=True, vmem_limit_bytes=60 << 20),
         name="scatter_grads",
     )(*parts)
+
+
 HEADS = 12
 HEAD_DIM = 64
 CHUNK = 256
@@ -375,7 +394,7 @@
     made[-1].wait()
 
 
-def attention_forward(each, seg_all, ends, qkv, lse, out_send, att, qkv_copies, sems):
+def attention_forward(each, seg_all, ends, qkv, lse, out_send, att, qkv_copies, sems, tick=lambda: None):
     size, me = lax.axis_size("ctx"), lax.axis_index("ctx")
     count = att.shape[1]
     copies = []
@@ -402,6 +421,7 @@
                 copy = to_group(out_send.at[h, i], att.at[theirs], sems, (h, i), p)
                 copy.start()
                 copies.append(copy)
+            tick()
     return copies
 
 
@@ -646,53 +666,369 @@
     )(lengths, grad, x, gain_a, gain_f, *kept, w_attn, w_ffn, w_down)
 
 
-def segment_of(places, ends):
-    return jnp.sum((places[:, None] >= ends[None, :]).astype(jnp.int32), 1)
-
-
-def offset_in(places, segs, ends, seq_lengths):
-    starts = ends - seq_lengths
-    picks = segs[:, None] == jnp.arange(ends.shape[0], dtype=jnp.int32)[None, :]
-    return places - jnp.sum(jnp.where(picks, starts[None, :], 0), 1)
-
-
-def gbst_mix(byte_ext, valid_ext, seg_ext, rel_ext, embed_t, conv_w, conv_b, scorer_v):
-    width_ext = byte_ext.shape[0]
-    byte_count = width_ext - 10
-    onehot = (byte_ext[:, None] == jnp.arange(embed_t.shape[0], dtype=jnp.int32)[None, :]).astype(
-        jnp.float32
-    )
-    onehot = onehot * valid_ext[:, None]
-    embedded = jnp.dot(onehot, embed_t, precision=PRECISE)
-    conv_span = width_ext - 3
-    conv_out = conv_b[None, :] + sum(
-        (
-            conv_w[tap][None, :]
-            * embedded[tap : tap + conv_span]
-            * (seg_ext[tap : tap + conv_span] == seg_ext[1 : 1 + conv_span]).astype(jnp.float32)[
-                :, None
-            ]
-            for tap in range(4)
-        )
-    )
-    conv_out = conv_out * valid_ext[1 : 1 + conv_span, None]
-    own_seg = seg_ext[5 : 5 + byte_count]
-    own_rel = rel_ext[5 : 5 + byte_count]
-    pooled_list = []
-    for block_size in (1, 2, 3, 4):
-        pooled = jnp.zeros((byte_count, embed_t.shape[1]), jnp.float32)
-        for shift_by in range(1 - block_size, block_size):
-            same = (seg_ext[5 + shift_by : 5 + shift_by + byte_count] == own_seg) & (
-                (own_rel + shift_by) // block_size == own_rel // block_size
-            )
-            weight = jnp.where(same, 1.0 / block_size, 0.0).astype(jnp.float32)
-            pooled = pooled + weight[:, None] * conv_out[4 + shift_by : 4 + shift_by + byte_count]
-        pooled_list.append(pooled)
-    stacked = jnp.stack(pooled_list)
-    logits = jnp.einsum("bnd,d->bn", stacked, scorer_v, precision=PRECISE)
-    choose = jax.nn.softmax(logits, 0)
-    chosen = jnp.sum(choose[..., None] * stacked, 0)
-    return chosen.reshape(byte_count // 2, 2, -1).mean(1)
+CONV = 4
+BLOCKS = (1, 2, 3, 4)
+HALO = 64
+
+
+def halves_of(v):
+    high = low(v)
+    return high, low(v - high.astype(jnp.float32))
+
+
+def dot_split(a, b):
+    high, rest = halves_of(a)
+    return dot(high, b) + dot(rest, b)
+
+
+def dot_wide(a, b):
+    (ah, al), (bh, bl) = halves_of(a), halves_of(b)
+    return dot(ah, bh) + dot(ah, bl) + dot(al, bh)
+
+
+def block_starts(places, ends):
+    start = jnp.zeros(places.shape, jnp.int32)
+    for end in ends:
+        start = jnp.where(places >= end, end, start)
+    rel = places - start
+    found = []
+    for size in BLOCKS:
+        if size & (size - 1) == 0:
+            found.append(places - (rel & (size - 1)))
+        else:
+            count = jnp.floor((rel.astype(jnp.float32) + 0.5) * (1.0 / size)).astype(jnp.int32)
+            found.append(start + count * size)
+    return found
+
+
+def valid_of(places, ends):
+    return (places >= 0) & (places < ends[-1])
+
+
+def tap_ids(ids, first, span, ends):
+    places = first - HALO + lax.broadcasted_iota(jnp.int32, (1, span), 1)
+    own = segments(places, ends)
+    count = ids.shape[1] // 3
+    rows = []
+    for tap in range(CONV):
+        theirs = places + (tap - 1)
+        at = count - HALO + tap - 1
+        near = ids[:, at - at % 128:at - at % 128 + span + 128]
+        near = lax.slice_in_dim(near, at % 128, at % 128 + span, axis=1)
+        use = valid_of(places, ends) & valid_of(theirs, ends) & (segments(theirs, ends) == own)
+        rows.append(jnp.where(use, near, -1))
+    return rows, valid_of(places, ends)
+
+
+def one_hot(row, vocab):
+    return low(jnp.where(lax.broadcasted_iota(jnp.int32, (vocab, row.shape[1]), 0) == row, 1.0, 0.0))
+
+
+def mix_blocks(first, span, tokens, ends):
+    keys = block_starts(first - HALO + lax.broadcasted_iota(jnp.int32, (span, tokens), 0), ends)
+    found = []
+    for parity in range(2):
+        own = block_starts(first + 2 * lax.broadcasted_iota(jnp.int32, (1, tokens), 1) + parity, ends)
+        found.append([key == mine for key, mine in zip(keys, own)])
+    return found
+
+
+def gbst_forward(ends, ids, first, small, conv, choice, vocab, tokens, tick=lambda: None):
+    span = conv.shape[1]
+    taps, valid = tap_ids(ids, first, span, ends)
+    table = small[:, :vocab]
+    at = vocab + CONV
+    total = small[:, at:at + 1] * jnp.where(valid, 1.0, 0.0)
+    for tap in range(CONV):
+        total = total + dot_split(table * small[:, vocab + tap:vocab + tap + 1], one_hot(taps[tap], vocab))
+        tick()
+    conv[...] = total
+    scored = jnp.sum(total * small[:, at + 1:at + 2], 0, keepdims=True)
+    scored = jnp.broadcast_to(scored, (8, span))
+    parts = []
+    for _ in range(3):
+        parts.append(low(scored))
+        scored = scored - parts[-1].astype(jnp.float32)
+    mix = jnp.zeros((span, tokens), jnp.float32)
+    for parity, blocks in enumerate(mix_blocks(first, span, tokens, ends)):
+        logits = []
+        for size, block in zip(BLOCKS, blocks):
+            ones = low(jnp.where(block, 1.0, 0.0))
+            logits.append((dot(parts[0], ones) + dot(parts[1], ones) + dot(parts[2], ones))[:1] * (1.0 / size))
+        top = functools.reduce(jnp.maximum, logits)
+        raised = [jnp.exp(v - top) for v in logits]
+        whole = functools.reduce(jnp.add, raised)
+        for i, (size, block) in enumerate(zip(BLOCKS, blocks)):
+            chosen = raised[i] / whole
+            choice[len(BLOCKS) * parity + i:len(BLOCKS) * parity + i + 1, :] = chosen
+            mix = mix + jnp.where(block, chosen * (0.5 / size), 0.0)
+        tick()
+    return dot_wide(total, mix)
+
+
+def gbst_backward(ends, ids, first, small, conv, choice, grad_t, vocab, out):
+    span, tokens = conv.shape[1], grad_t.shape[1]
+    taps, valid = tap_ids(ids, first, span, ends)
+    at = vocab + CONV
+    total = conv[...]
+    along = dot_wide(total.T, grad_t)
+    mix = jnp.zeros((span, tokens), jnp.float32)
+    scored = jnp.zeros((span, tokens), jnp.float32)
+    for parity, blocks in enumerate(mix_blocks(first, span, tokens, ends)):
+        chosen = [choice[len(BLOCKS) * parity + i:len(BLOCKS) * parity + i + 1, :] for i in range(len(BLOCKS))]
+        grads = [jnp.sum(jnp.where(block, along, 0.0), 0, keepdims=True) * (0.5 / size) for size, block in zip(BLOCKS, blocks)]
+        inner = functools.reduce(jnp.add, [c * g for c, g in zip(chosen, grads)])
+        for i, (size, block) in enumerate(zip(BLOCKS, blocks)):
+            mix = mix + jnp.where(block, chosen[i] * (0.5 / size), 0.0)
+            scored = scored + jnp.where(block, chosen[i] * (grads[i] - inner) * (1.0 / size), 0.0)
+    g_scored = jnp.sum(scored.T, 0, keepdims=True)
+    g_conv = dot_wide(grad_t, mix.T) + small[:, at + 1:at + 2] * g_scored
+    out[:, at + 1:at + 2] = jnp.sum(total * g_scored, 1, keepdims=True)
+    g_conv = g_conv * jnp.where(valid, 1.0, 0.0)
+    out[:, at:at + 1] = jnp.sum(g_conv, 1, keepdims=True)
+    high, rest = halves_of(g_conv)
+    table = small[:, :vocab]
+    g_table = jnp.zeros(table.shape, jnp.float32)
+    for tap in range(CONV):
+        hot = one_hot(taps[tap], vocab)
+        g_tap = dot_nt(high, hot) + dot_nt(rest, hot)
+        g_table = g_table + g_tap * small[:, vocab + tap:vocab + tap + 1]
+        out[:, vocab + tap:vocab + tap + 1] = jnp.sum(g_tap * table, 1, keepdims=True)
+    out[:, :vocab] = g_table
+
+
+def gbst_forward_kernel(vocab, tokens, lengths, ids, small, out, conv, choice):
+    ends = ends_of(lengths)
+    first = lax.axis_index("ctx") * 2 * tokens
+    out[...] = gbst_forward(ends, ids, first, small, conv, choice, vocab, tokens).T
+
+
+def gbst_backward_kernel(vocab, lengths, ids, small, conv, choice, grad, out):
+    ends = ends_of(lengths)
+    first = lax.axis_index("ctx") * 2 * grad.shape[0]
+    out[...] = jnp.zeros(out.shape, jnp.float32)
+    gbst_backward(ends, ids, first, small, conv, choice, grad[...].T, vocab, out)
+
+
+class Keep:
+    def __init__(self, sems):
+        self.sems, self.count, self.flying = sems, 0, []
+
+    def __call__(self, src, dst):
+        copy = pltpu.make_async_copy(src, dst, self.sems.at[self.count])
+        copy.start()
+        self.count += 1
+        self.flying.append(copy)
+
+    def finish(self):
+        for copy in self.flying:
+            copy.wait()
+
+
+def unpack(blocks, dst):
+    nz, cores, ny, nx, rows, width = blocks.shape
+    each = ny * nx * rows
+    part = min(width, 512)
+
+    def body(i, carry):
+        for c in range(width // part):
+            columns = slice(c * part, (c + 1) * part)
+            found = [blocks[i // cores, i % cores, y, x, :, columns].astype(jnp.float32) for y in range(ny) for x in range(nx)]
+            dst[pl.ds(pl.multiple_of(i * each, each), each), columns] = low(jnp.concatenate(found, 0))
+        return carry
+    lax.fori_loop(0, nz * cores, body, 0)
+
+
+KEPT = ("x", "middle", "normed_t", "qkv", "lse", "att", "gate", "up", "nffn_t")
+
+
+def kept_shapes(count, model, wide):
+    size, each = lax.axis_size("ctx"), heads_each()
+    f32, bf16 = jnp.float32, jnp.bfloat16
+    return {
+        "x": ((count, model), f32), "middle": ((count, model), f32), "normed_t": ((model, count), bf16),
+        "qkv": ((3, each * HEAD_DIM, count * size), bf16), "lse": ((each, 1, count * size), f32),
+        "att": ((each * size * HEAD_DIM, count), bf16), "gate": ((count, wide), f32), "up": ((count, wide), f32),
+        "nffn_t": ((model, count), bf16)}
+
+
+def named(names, refs):
+    return dict(zip(names, refs, strict=True))
+
+
+def forward_kernel(layers, vocab, third, names, *refs):
+    r = named(names, refs)
+    ends = ends_of(r["lengths"])
+    size, me = lax.axis_size("ctx"), lax.axis_index("ctx")
+    each = heads_each()
+    keep = Keep(r["keep_sems"])
+    kinds = ["small"] + [f"{kind}{l}" for l in range(layers) for kind in ("attn", "ffn", "down")]
+    greet_all()
+    ids, count = r["ids"], r["byte_ids"].shape[1]
+    near = []
+    for i, (there, at) in enumerate(((lax.rem(me + 1, size), 0), (lax.rem(me + size - 1, size), 2))):
+        copy = to_group(r["byte_ids"], ids.at[:, pl.ds(at * count, count)], r["ids_sems"], (i,), there)
+        copy.start()
+        near.append(copy)
+    ids[:, count:2 * count] = r["byte_ids"][...]
+    chunks = [GatherChunk(r["shard_" + k], r["full_" + k], r["sems_" + k], r["local_sems"].at[i], third) for i, k in enumerate(kinds)]
+    ticker = Ticker(chunks)
+    tick = ticker.tick
+    tick(2)
+    tokens = count // 2
+    seg_all = r["seg_all"]
+    seg_all[...] = segments(2 * lax.broadcasted_iota(jnp.int32, seg_all.shape, 0), ends)
+    for copy in near:
+        copy.wait_recv()
+    ticker.need(0)
+    small = r["small_wide"]
+    for z in range(r["full_small"].shape[0]):
+        found = r["full_small"][z].astype(jnp.float32)
+        rows = math.prod(found.shape[:-1])
+        small[z * rows:(z + 1) * rows, :] = jnp.concatenate(
+            [found[i, j, k] for i in range(found.shape[0]) for j in range(found.shape[1]) for k in range(found.shape[2])], 0)
+    tick(2)
+    stream = gbst_forward(ends, ids[...], me * count, small[...], r["conv"], r["choice"], vocab, tokens, tick).T
+    at = vocab + CONV + 2
+    gains = small[:, at // 128 * 128:].T
+    at = at % 128
+    model = stream.shape[1]
+    keep(r["conv"], r["out_conv"])
+    for l in range(layers):
+        gain_a, gain_f = gains[at + l:at + l + 1, :], gains[at + layers + l:at + layers + l + 1, :]
+        kept = {k: r[f"{k}{l}"] for k in KEPT}
+        w_attn, w_ffn, w_down = r["w_attn"], r["w_ffn"], r["w_down"]
+        first = 1 + 3 * l
+
+        def fetch(i, dst, sem):
+            ticker.need(i)
+            copy = pltpu.make_async_copy(r["full_" + kinds[i]], dst, r["load_sems"].at[l, sem])
+            copy.start()
+            return copy
+        load = fetch(first, r["blocks_attn"], 0)
+        kept["x"][...] = stream
+        normed = low(stream * inverse_rms(stream) * gain_a)
+        kept["normed_t"][...] = flip(normed)
+        load.wait()
+        unpack(r["blocks_attn"], w_attn)
+        tick()
+        qkv_all = r["qkv_all"]
+        for part in range(3):
+            for c in range(model // CHUNK):
+                columns = pl.ds(part * model + c * CHUNK, CHUNK)
+                qkv_all[part, c * CHUNK:(c + 1) * CHUNK, :] = low(dot(normed, w_attn[:, columns]).T)
+        qkv_copies = spread_heads(qkv_all, kept["qkv"], r["sems_qkv"].at[l], r["own_sems"].at[l], each)
+        tick()
+        keep(kept["x"], r[f"out_x{l}"])
+        keep(kept["normed_t"], r[f"out_normed_t{l}"])
+        out_copies = attention_forward(each, seg_all, ends, kept["qkv"], kept["lse"], r["out_send"], kept["att"],
+                                       qkv_copies, r["sems_att"].at[l], tick)
+        for copy in out_copies:
+            copy.wait_recv()
+        keep(kept["qkv"], r[f"out_qkv{l}"])
+        keep(kept["lse"], r[f"out_lse{l}"])
+        keep(kept["att"], r[f"out_att{l}"])
+        attended = flip(kept["att"][:model, :])
+        mid = stream + dot(attended, w_attn[:, 3 * model:])
+        kept["middle"][...] = mid
+        after = low(mid * inverse_rms(mid) * gain_f)
+        r["nffn"][...] = after
+        kept["nffn_t"][...] = flip(after)
+        r["total"][...] = mid
+        keep(kept["middle"], r[f"out_middle{l}"])
+        keep(kept["nffn_t"], r[f"out_nffn_t{l}"])
+        load = fetch(first + 1, r["blocks_ffn"], 1)
+        load_down = fetch(first + 2, w_down, 2)
+        load.wait()
+        unpack(r["blocks_ffn"], w_ffn)
+        tick()
+        load_down.wait()
+        nz, cores, ny, nx, rows, _ = w_down.shape
+        wide, part = nz * cores * ny * nx * rows, ny * nx * rows
+
+        def step(c, carry):
+            columns = pl.ds(pl.multiple_of(c * part, part), part)
+            gate = dot(r["nffn"][...], w_ffn[:, columns])
+            up = dot(r["nffn"][...], w_ffn[:, pl.ds(pl.multiple_of(wide + c * part, part), part)])
+            kept["gate"][:, columns] = gate
+            kept["up"][:, columns] = up
+            hidden = low(gelu_parts(gate)[0] * up)
+            r["total"][...] += dot(hidden, w_down[c // cores, c % cores].reshape(part, model))
+            return carry
+        half = nz * cores // 2
+        lax.fori_loop(0, half, step, 0)
+        tick(2)
+        lax.fori_loop(half, nz * cores, step, 0)
+        keep(kept["gate"], r[f"out_gate{l}"])
+        keep(kept["up"], r[f"out_up{l}"])
+        stream = r["total"][...]
+        for made in qkv_copies:
+            for copy in made[:-1]:
+                copy.wait_send()
+        for copy in out_copies:
+            copy.wait_send()
+    r["encoded"][...] = low(stream)
+    for copy in near:
+        copy.wait_send()
+    for i in range(len(chunks)):
+        ticker.need(i)
+    for chunk in chunks:
+        chunk.finish()
+    keep.finish()
+
+
+def forward_pass(lengths, byte_ids, small, shards, layers, vocab, third, collective_id):
+    nz, ny, nx = grid_of()
+    size, each = lax.axis_size("ctx"), heads_each()
+    model = shards[0].shape[1] // 4
+    tokens = byte_ids.shape[1] // 2
+    wide = shards[1].shape[1] // 2
+    span = byte_ids.shape[1] + 2 * HALO
+    f32, bf16 = jnp.float32, jnp.bfloat16
+    made = lambda shape, dtype: jax.ShapeDtypeStruct(shape, dtype)
+    whole = lambda s: (nz, CORES, ny, nx) + s.shape
+    kinds = [f"{kind}{l}" for l in range(layers) for kind in ("attn", "ffn", "down")]
+    inputs = {"lengths": (lengths, SMEM), "byte_ids": (byte_ids, VMEM), "shard_small": (small, ANY)}
+    for k, s in zip(kinds, shards):
+        inputs["shard_" + k] = (s, ANY)
+    outputs = {"encoded": (made((tokens, model), bf16), VMEM), "small_wide": (made((model, small.shape[1]), f32), VMEM),
+               "ids": (made((1, 3 * byte_ids.shape[1]), jnp.int32), VMEM), "choice": (made((2 * len(BLOCKS), tokens), f32), VMEM),
+               "out_conv": (made((model, span), f32), ANY)}
+    for k, s in zip(kinds, shards):
+        outputs["full_" + k] = (made(whole(s), bf16), ANY)
+    shapes = kept_shapes(tokens, model, wide)
+    for l in range(layers):
+        for k in KEPT:
+            outputs[f"out_{k}{l}"] = (made(*shapes[k]), ANY)
+    rows = each * size * HEAD_DIM
+    dma = pltpu.SemaphoreType.DMA
+    scratch = {"full_small": pltpu.VMEM(whole(small), bf16), "conv": pltpu.VMEM((model, span), f32),
+               "w_attn": pltpu.VMEM((model, 4 * model), bf16), "w_ffn": pltpu.VMEM((model, 2 * wide), bf16),
+               "w_down": pltpu.VMEM(whole(shards[2]), bf16), "blocks_attn": pltpu.VMEM(whole(shards[0]), bf16),
+               "blocks_ffn": pltpu.VMEM(whole(shards[1]), bf16), "qkv_all": pltpu.VMEM((3, rows, tokens), bf16),
+               "out_send": pltpu.VMEM((each, size - 1, HEAD_DIM, tokens), bf16),
+               "seg_all": pltpu.VMEM((tokens * size, tokens), jnp.int32), "nffn": pltpu.VMEM((tokens, model), bf16),
+               "total": pltpu.VMEM((tokens, model), f32),
+               "keep_sems": dma((1 + layers * len(KEPT),)), "ids_sems": dma((2, 2)), "local_sems": dma((1 + len(kinds),)),
+               "load_sems": dma((layers, 3)), "own_sems": dma((layers, each)),
+               "sems_qkv": dma((layers, 2, each, size - 1)), "sems_att": dma((layers, 2, each, size - 1)),
+               "sems_small": dma((2, hops(small.shape[1], third)))}
+    for k, s in zip(kinds, shards):
+        scratch["sems_" + k] = dma((2, hops(s.shape[1], third)))
+    for l in range(layers):
+        for k in KEPT:
+            scratch[f"{k}{l}"] = pltpu.VMEM(*shapes[k])
+    names = [*inputs, *outputs, *scratch]
+    found = pl.pallas_call(
+        functools.partial(forward_kernel, layers, vocab, third, names),
+        out_shape=[s for s, _ in outputs.values()],
+        in_specs=[s for _, s in inputs.values()],
+        out_specs=[s for _, s in outputs.values()],
+        scratch_shapes=list(scratch.values()),
+        compiler_params=pltpu.CompilerParams(collective_id=collective_id, has_side_effects=True, vmem_limit_bytes=60 << 20),
+        name="forward_pass",
+    )(*[a for a, _ in inputs.values()])
+    return named(outputs, found)
 
 
 def packed_small(embed, conv_weight, conv_bias, scorer, norm_attn, norm_ffn):
@@ -704,6 +1040,47 @@
     at = vocab + CONV
     return (rows[:vocab], rows[vocab:at], rows[at], rows[at + 1], rows[at + 2 : at + 2 + layers],
             rows[at + 2 + layers : at + 2 + 2 * layers])
+
+
+def separate_forward(lengths, byte_ids, shards, layer_count, vocab, model):
+    ring, tokens = lax.axis_size("ctx"), byte_ids.shape[1] // 2
+    up = [(i, (i + 1) % ring) for i in range(ring)]
+    down = [(j, i) for i, j in up]
+    ids = jnp.concatenate([lax.ppermute(byte_ids, "ctx", up), byte_ids, lax.ppermute(byte_ids, "ctx", down)], 1)
+    small_full, *full = [a.reshape(-1, a.shape[-1]) for a in gather_all(shards, 0)]
+    small_wide = small_full.astype(jnp.float32)
+    gains = small_wide.T[vocab + CONV + 2 :]
+    stream, conv, choice = pl.pallas_call(
+        functools.partial(gbst_forward_kernel, vocab, tokens),
+        out_shape=[
+            jax.ShapeDtypeStruct((tokens, model), jnp.float32),
+            jax.ShapeDtypeStruct((model, byte_ids.shape[1] + 2 * HALO), jnp.float32),
+            jax.ShapeDtypeStruct((2 * len(BLOCKS), tokens), jnp.float32),
+        ],
+        in_specs=[SMEM, VMEM, VMEM],
+        out_specs=[VMEM] * 3,
+        compiler_params=pltpu.CompilerParams(vmem_limit_bytes=56 << 20),
+        name="mix_bytes",
+    )(lengths, ids, small_wide)
+    kept = []
+    for layer in range(layer_count):
+        before = stream
+        stream, *saved = layer_forward(
+            lengths, stream, gains[layer][None], gains[layer_count + layer][None], *full[3 * layer : 3 * layer + 3], 2
+        )
+        kept.append((before, saved))
+    return stream.astype(jnp.bfloat16), full, small_wide, ids, conv, choice, kept
+
+
+def fused_forward(lengths, byte_ids, shards, layer_count, vocab, model):
+    kinds = [f"{kind}{layer}" for layer in range(layer_count) for kind in ("attn", "ffn", "down")]
+    fwd = forward_pass(lengths, byte_ids, shards[0], shards[1:], layer_count, vocab, THIRD, 4)
+    full = [fwd["full_" + k].reshape(-1, fwd["full_" + k].shape[-1]) for k in kinds]
+    kept = []
+    for layer in range(layer_count):
+        saved = [fwd[f"out_{k}{layer}"] for k in KEPT]
+        kept.append((saved[0], saved[1:]))
+    return fwd["encoded"], full, fwd["small_wide"], fwd["ids"], fwd["out_conv"], fwd["choice"], kept
 
 
 def on_device(
@@ -730,43 +1107,19 @@
     vocab = embed.shape[0]
     model = query_w.shape[2]
     byte_count = byte_ids.shape[1]
-    seq_lengths = lengths[0]
-    at = jnp.arange(seq_lengths.shape[0])
-    ends = jnp.sum(jnp.where(at[:, None] >= at[None, :], seq_lengths[None, :], 0), 1).astype(jnp.int32)
-    total_bytes = ends[-1]
-    first_byte = ctx_place * byte_count
-    byte_ext = padded(byte_ids[0], (("ctx", 0),), 5)
-    ext_places = first_byte - 5 + jnp.arange(byte_count + 10, dtype=jnp.int32)
-    valid_ext = ((ext_places >= 0) & (ext_places < total_bytes)).astype(jnp.float32)
-    seg_ext = segment_of(ext_places, ends)
-    rel_ext = offset_in(ext_places, seg_ext, ends, seq_lengths)
     small = packed_small(embed, conv_weight, conv_bias, scorer, norm_attn, norm_ffn)
     shards = [small]
     for layer in range(layer_count):
         shards.append(jnp.concatenate([query_w[layer], key_w[layer], value_w[layer], attn_out_w[layer]], 1))
         shards.append(jnp.concatenate([gate_w[layer], up_w[layer]], 1))
         shards.append(down_w[layer])
-    small_full, *full = [a.reshape(-1, a.shape[-1]) for a in gather_all(shards, 0)]
-    embed_full, conv_full, bias_full, scorer_full, norm_a, norm_f = split_small(small_full.T, vocab, layer_count)
-
-    def gbst_local(embed_t, conv_w, conv_b, scorer_v):
-        return gbst_mix(byte_ext, valid_ext, seg_ext, rel_ext, embed_t, conv_w, conv_b, scorer_v)
-
-    stream, gbst_back = jax.vjp(
-        gbst_local,
-        embed_full.astype(jnp.float32),
-        conv_full.astype(jnp.float32),
-        bias_full.astype(jnp.float32),
-        scorer_full.astype(jnp.float32),
+    fused = shards[1].shape[0] % 8 == 0 and HEADS % lax.axis_size("ctx") == 0
+    encoded, full, small_wide, ids, conv, choice, kept = (fused_forward if fused else separate_forward)(
+        lengths, byte_ids, shards, layer_count, vocab, model
     )
-    gains_a, gains_f = norm_a.astype(jnp.float32), norm_f.astype(jnp.float32)
-    kept = []
-    for layer in range(layer_count):
-        weights = full[3 * layer : 3 * layer + 3]
-        before = stream
-        stream, *saved = layer_forward(lengths, stream, gains_a[layer][None], gains_f[layer][None], *weights, 2)
-        kept.append((before, saved))
-    encoded = stream.astype(jnp.bfloat16)[None]
+    encoded = encoded[None]
+    gains = small_wide.T[vocab + CONV + 2 :]
+    gains_a, gains_f = gains[:layer_count], gains[layer_count : 2 * layer_count]
     grad_stream = out_grad[0].astype(jnp.float32)
     partial = []
     gains = []
@@ -778,8 +1131,16 @@
         )
         partial = list(grads) + partial
         gains = [(d_gain_attn[0], d_gain_ffn[0])] + gains
-    grads = gbst_back(grad_stream)
-    small_grad = packed_small(*grads, jnp.stack([a for a, _ in gains]), jnp.stack([f for _, f in gains]))
+    small_grad = pl.pallas_call(
+        functools.partial(gbst_backward_kernel, vocab),
+        out_shape=jax.ShapeDtypeStruct(small_wide.shape, jnp.float32),
+        in_specs=[SMEM] + [VMEM] * 5,
+        out_specs=VMEM,
+        compiler_params=pltpu.CompilerParams(vmem_limit_bytes=56 << 20),
+        name="mix_bytes_backward",
+    )(lengths, ids, small_wide, conv, choice, grad_stream)
+    columns = jnp.stack([a for a, _ in gains] + [f for _, f in gains]).T
+    small_grad = lax.dynamic_update_slice(small_grad, columns, (0, vocab + CONV + 2))
     outs = scatter_all([p.astype(jnp.bfloat16) for p in [small_grad] + partial], 1)
     small_out, *rest = outs
     g_embed, g_conv, g_bias, g_scorer, g_norm_a, g_norm_f = split_small(small_out.T, vocab, layer_count)

time: 559 us -> 501 us (0.90)
  other arithmetic: 40 us -> 10.6 us
  matrix products: 10.5 us -> 0 us
  local copies, waits for them, and re-layouts: 35 us -> 26.8 us
  starting transfers between devices: 6.75 us -> 0 us
    reduce_sum x9 -> x0, other arithmetic: 16.3 us -> none  [the longest x1 6.69 us: gbst_mix(): conv_w[tap][None, :] * embedded[tap:tap + conv_span]]
    dot_general x4 -> x0, matrix products: 10.5 us -> none  [the longest x2 6.84 us: gbst_mix(): logits = jnp.einsum('bnd,d->bn', stacked, scorer_v, precision=PRECISE)]
    reshape x8 -> x0, local copies, waits for them, and re-layouts: 7.49 us -> none  [the longest x2 6.16 us: gbst_mix(): return chosen.reshape(byte_count // 2, 2, -1).mean(1)]
    mul x5 -> x0, other arithmetic: 6.89 us -> none  [the longest x2 5.36 us: gbst_mix(): weight[:, None] * conv_out[4 + shift_by:4 + shift_by + byte_count]]
    ppermute x2 -> x0, starting transfers between devices: 6.75 us -> none  [the longest x1 5.47 us: padded(): before = lax.ppermute(last, axis, up)]
    pallas_call x4 -> x3, Pallas kernels: 365 us -> 365 us  [the longest x1 212 us: forward_pass(): pl.pallas_call(functools.partial(forward_kernel, layers, vocab, third, na...]
  transfers between devices with their start and end apart: 2 -> 0, of which waited for: 0 -> 0; matrix products, arithmetic and copies ran while one was open for 3% -> 0% of each run, Pallas kernels for 27% -> 0%
where the time goes in v3:
time: 501 us; the launch traced here: 494 us
  Pallas kernels  455 us (91%)
  local copies, waits for them, and re-layouts  26.8 us (5%)
  other arithmetic  10.6 us (2%)
    pallas_call x1, Pallas kernels, forward_pass(): pl.pallas_call(functools.partial(forward_kernel, layers, vocab, third, na...  212 us
    pallas_call x1, Pallas kernels, scatter_all(): pl.pallas_call(functools.partial(scatter_kernel, n, third, counts), out_s...  143 us
    pallas_call x2, Pallas kernels, layer_backward(): pl.pallas_call(layer_backward_kernel, out_shape=[made((count, model), f32...  90.6 us
    pallas_call x1, Pallas kernels, on_device(): pl.pallas_call(functools.partial(gbst_backward_kernel, vocab), out_shape=...  10.1 us

profile of v3, /device:TPU:0, one launch (start us, length us, event | category | flops | bytes accessed | tf_op | source)
XLA Modules:
  0.0 493.9 jit_solution(4027729934950958991)
XLA Ops:
  0.6 0.0 copy-start.3
  0.7 0.8 copy.56
  1.5 0.7 copy.57
  2.2 0.7 copy.58
  3.0 0.7 copy.59
  3.7 0.7 copy.60
  4.5 0.8 concatenate.15
  5.3 0.6 pad.4.refs_2_
  5.9 0.8 slice_bitcast_fusion.21
  6.7 0.8 slice_bitcast_fusion.20
  7.5 0.8 slice_bitcast_fusion.19
  8.3 0.8 slice_bitcast_fusion.18
  9.0 0.7 pad_maximum_fusion.5
  9.8 1.0 slice_bitcast_fusion.6
  10.7 1.0 slice_bitcast_fusion.5
  11.7 0.8 pad_maximum_fusion.3
  12.5 1.6 slice_bitcast_fusion.4
  14.1 0.0 copy-done.3
  14.1 0.9 bitcast_convert_fusion.grad
  15.0 211.9 %forward_pass.1 = (bf16[256,768]{1,0:T(8,128)(2,1)}, f32[768,384]{1,0:T(8,128)}, s32[1,1536]{1,0:T(1,128)}, f32[8,256]{1,0:T(8,128)}, f32[768,640]{1,0:T(8,128)}...) custom-call(s32[1,4]{1,0:T(1,128)} %lengths.5, ...), custom_call_target="tpu_custom_call" | custom-call | tf_op jit(solution)/shard_map/forward_pass/pallas_call | solution.py:1022
  226.9 1.6 copy.61
  228.6 0.6 fusion
  229.2 45.4 %layer_backward.2 = (f32[256,768]{1,0:T(8,128)}, f32[1,768]{1,0:T(1,128)}, f32[1,768]{1,0:T(1,128)}, bf16[768,3072]{1,0:T(8,128)(2,1)}, bf16[768,4096]{1,0:T(8,128)(2,1)}, /*index=5*/bf16[2048,768]{1,0:T(8,128)(2,1)}) custom-call(s32[1,4]{1,0:T(1,128)} %lengths.5, f32[256,768]{1,0:T(8,128)} %bitcast_convert_fusion.grad, f32[256,768]{1,0:T(8,128)} %get-tuple-element.67.x, ...), custom_call_target="tpu_custom_call" | custom-call | tf_op jit(solution)/shard_map/layer_backward/pallas_call | solution.py:648
  274.6 45.1 %layer_backward.3 = (f32[256,768]{1,0:T(8,128)}, f32[1,768]{1,0:T(1,128)}, f32[1,768]{1,0:T(1,128)}, bf16[768,3072]{1,0:T(8,128)(2,1)}, bf16[768,4096]{1,0:T(8,128)(2,1)}, /*index=5*/bf16[2048,768]{1,0:T(8,128)(2,1)}) custom-call(s32[1,4]{1,0:T(1,128)} %lengths.5, f32[256,768]{1,0:T(8,128)} %get-tuple-element.79.grad, f32[256,768]{1,0:T(8,128)} %get-tuple-element.80.x, ...), custom_call_target="tpu_custom_call" | custom-call | tf_op jit(solution)/shard_map/layer_backward/pallas_call | solution.py:648
  319.7 0.0 copy-start.4
  319.8 0.0 copy-start.5
  319.8 0.0 copy-start.6
  319.8 0.0 copy-start.7
  319.8 10.1 %mix_bytes_backward.1 = f32[768,384]{1,0:T(8,128)} custom-call(s32[1,4]{1,0:T(1,128)} %lengths.5, s32[1,1536]{1,0:T(1,128)} %get-tuple-element.63.ids, f32[768,384]{1,0:T(8,128)} %get-tuple-element.64.small, f32[768,640]{1,0:T(8,128)} %get-tuple-element.65.conv, f32[8,256]{1,0:T(8,128)} %get-tuple-element.66.choice, f32[256,768]{1,0:T(8,128)} %get-tuple-element.92.grad), custom_call_target="tpu_custom_call" | custom-call | tf_op jit(solution)/shard_map/mix_bytes_backward/pallas_call | solution.py:1134
  329.9 0.0 copy-done.4
  329.9 0.0 copy-done.5
  329.9 0.0 copy-done.6
  329.9 0.0 copy-done.7
  329.9 0.2 copy.62
  330.1 3.2 dynamic_update_slice.3
  333.3 2.2 convert_element_type.12
  335.4 142.9 %scatter_grads.1 = (f32[24,384]{1,0:T(8,128)}, f32[24,3072]{1,0:T(8,128)}, f32[24,4096]{1,0:T(8,128)}, f32[64,768]{1,0:T(8,128)}, f32[24,3072]{1,0:T(8,128)}, /*index=5*/f32[24,4096]{1,0:T(8,128)}, f32[64,768]{1,0:T(8,128)}) custom-call(bf16[4,2,2,2,24,384]{5,4,3,2,1,0:T(8,128)(2,1)} %bitcast.89, bf16[4,2,2,2,24,3072]{5,4,3,2,1,0:T(8,128)(2,1)} %bitcast.82, ...), custom_call_target="tpu_custom_call" | custom-call | tf_op jit(solution)/shard_map/scatter_grads/pallas_call | solution.py:289
  478.4 0.0 copy-start.2
  478.4 0.0 copy-start.1
  478.4 1.5 slice_reduce_fusion
  479.9 0.7 slice.158
  480.6 0.7 copy.63
  481.3 1.3 slice.157
  482.6 0.9 fusion.1
  483.5 0.6 copy.65
  484.1 0.6 copy.64
  484.7 0.0 copy-start
  484.7 1.1 slice_bitcast_fusion.11
  485.8 1.0 slice_bitcast_fusion.10
  486.8 0.7 pad_maximum_fusion.10
  487.5 0.7 pad_maximum_fusion.9
  488.2 0.7 pad_maximum_fusion.8
  488.8 0.7 pad_maximum_fusion.7
  489.5 1.8 pad_maximum_fusion.2
  491.3 0.0 copy-done.2
  491.3 0.0 copy-done.1
  491.4 0.8 pad_maximum_fusion.1
  492.2 0.8 pad_maximum_fusion
  492.9 0.0 copy-done
  492.9 0.7 copy.68
  (3 shorter events, 0.1 us)
Async XLA Ops:
  0.6 13.4 %copy-start.3 = (bf16[1,256,768]{2,1,0:T(8,128)(2,1)S(1)}, bf16[1,256,768]{2,1,0:T(8,128)(2,1)}, u32[]{:S(2)}) copy-start(bf16[1,256,768]{2,1,0:T(8,128)(2,1)} %param.31) | copy-start | bytes 1179652
  319.7 10.1 %copy-start.4 = (f32[1,768]{1,0:T(1,128)S(1)}, f32[1,768]{1,0:T(1,128)}, u32[]{:S(2)}) copy-start(f32[1,768]{1,0:T(1,128)} %get-tuple-element.94) | copy-start | bytes 9220
  319.8 10.1 %copy-start.5 = (f32[1,768]{1,0:T(1,128)S(1)}, f32[1,768]{1,0:T(1,128)}, u32[]{:S(2)}) copy-start(f32[1,768]{1,0:T(1,128)} %get-tuple-element.96) | copy-start | bytes 9220
  319.8 10.1 %copy-start.6 = (f32[1,768]{1,0:T(1,128)S(1)}, f32[1,768]{1,0:T(1,128)}, u32[]{:S(2)}) copy-start(f32[1,768]{1,0:T(1,128)} %get-tuple-element.93) | copy-start | bytes 9220
  319.8 10.1 %copy-start.7 = (f32[1,768]{1,0:T(1,128)S(1)}, f32[1,768]{1,0:T(1,128)}, u32[]{:S(2)}) copy-start(f32[1,768]{1,0:T(1,128)} %get-tuple-element.95) | copy-start | bytes 9220
  478.4 12.9 %copy-start.2 = (f32[24,4096]{1,0:T(8,128)S(1)}, f32[24,4096]{1,0:T(8,128)}, u32[]{:S(2)}) copy-start(f32[24,4096]{1,0:T(8,128)} %get-tuple-element.106) | copy-start | bytes 1179652
  478.4 12.9 %copy-start.1 = (f32[24,4096]{1,0:T(8,128)S(1)}, f32[24,4096]{1,0:T(8,128)}, u32[]{:S(2)}) copy-start(f32[24,4096]{1,0:T(8,128)} %get-tuple-element.107) | copy-start | bytes 1179652
  484.7 8.2 %copy-start = (bf16[256,768]{1,0:T(8,128)(2,1)S(1)}, bf16[256,768]{1,0:T(8,128)(2,1)}, u32[]{:S(2)}) copy-start(bf16[256,768]{1,0:T(8,128)(2,1)} %get-tuple-element.62) | copy-start | bytes 1179652

commit v4 on v3

--- a/solution.py
+++ b/solution.py
@@ -1,5 +1,5 @@
 import functools
-import math
+import types
 import jax
 import jax.numpy as jnp
 from jax import lax
@@ -11,7 +11,9 @@
 MESH = pl.DeviceIdType.MESH
 CORES = 2
 LANES = 128
-THIRD = 0.18
+THIRD = 0.1
+DEPTH = 2
+SPLIT = 3
 
 
 def grid_of():
@@ -65,11 +67,17 @@
 ORDERS = ((0, 3, 2), (0, 2, 3), (3, 2, 0))
 
 
-def pieces_of(width, third):
+def splits_of(width, count):
+    units = width // LANES
+    cuts = [units * i // count * LANES for i in range(count + 1)]
+    return [(a, b - a) for a, b in zip(cuts, cuts[1:])]
+
+
+def pieces_of(width, third, first=0):
     units = width // LANES
     last = int(units * third)
     left = (units - last + 1) // 2
-    found, at = [], 0
+    found, at = [], first // LANES
     for order, size in zip(ORDERS, (left, units - last - left, last)):
         if size:
             found.append((pl.ds(at * LANES, size * LANES), order))
@@ -98,6 +106,7 @@
     def finish(self):
         for copy in self.flying:
             copy.wait_send()
+        self.flying = []
 
 
 class GatherChunk(Sender):
@@ -136,7 +145,7 @@
         self.waiting = []
 
 
-class Ticker:
+class Pipeline:
     def __init__(self, chunks):
         self.chunks, self.steps, self.done = chunks, [], [0] * len(chunks)
         phases = chunks[0].phases
@@ -165,7 +174,7 @@
     shards, outs, sems, local_sems = refs[:n], refs[n:2 * n], refs[2 * n:3 * n], refs[3 * n]
     greet_all()
     chunks = [GatherChunk(shards[i], outs[i], sems[i], local_sems.at[i], third) for i in range(n)]
-    ticker = Ticker(chunks)
+    ticker = Pipeline(chunks)
     for i in range(n):
         ticker.need(i)
     for chunk in chunks:
@@ -264,7 +273,7 @@
     for i in range(n):
         scratch = [rest.pop(0) for _ in range(counts[i])]
         chunks.append(ScatterChunk(parts[i], outs[i], scratch, rest.pop(0), rest.pop(0), third))
-    ticker = Ticker(chunks)
+    ticker = Pipeline(chunks)
     for i in range(n):
         ticker.until(i)
     for chunk in chunks:
@@ -766,7 +775,7 @@
     return dot_wide(total, mix)
 
 
-def gbst_backward(ends, ids, first, small, conv, choice, grad_t, vocab, out):
+def gbst_backward(ends, ids, first, small, conv, choice, grad_t, vocab, out, tick=lambda: None):
     span, tokens = conv.shape[1], grad_t.shape[1]
     taps, valid = tap_ids(ids, first, span, ends)
     at = vocab + CONV
@@ -794,6 +803,7 @@
         g_tap = dot_nt(high, hot) + dot_nt(rest, hot)
         g_table = g_table + g_tap * small[:, vocab + tap:vocab + tap + 1]
         out[:, vocab + tap:vocab + tap + 1] = jnp.sum(g_tap * table, 1, keepdims=True)
+        tick()
     out[:, :vocab] = g_table
 
 
@@ -810,6 +820,275 @@
     gbst_backward(ends, ids, first, small, conv, choice, grad[...].T, vocab, out)
 
 
+class Gather(Sender):
+    phases = 4
+
+    def __init__(self, sources, out, sems, local_sems, first=0, width=None):
+        super().__init__(sems)
+        self.out = out
+        self.columns = pl.ds(first, width or out.shape[-1])
+        self.pieces = pieces_of(self.columns.size, THIRD, first)
+        self.waiting = []
+        self.own = []
+        for i, (source, at) in enumerate(sources):
+            a, b = max(first, at), min(first + (width or out.shape[-1]), at + source.shape[-1])
+            if a < b:
+                there = out.at[place_of() + (slice(None), pl.ds(a, b - a))]
+                copy = pltpu.make_async_copy(source.at[:, pl.ds(a - at, b - a)], there, local_sems.at[i])
+                copy.start()
+                self.own.append(copy)
+
+    def stage(self, number):
+        place = place_of()
+        self.arrive()
+        if number == 0:
+            for copy in self.own:
+                copy.wait()
+        if number < 3:
+            for columns, order in self.pieces:
+                have = order[:number]
+                where = tuple(slice(None) if axis in have else place[axis] for axis in range(4)) + (slice(None), columns)
+                for _, target in along(order[number]):
+                    self.waiting.append(self.send(self.out.at[where], self.out.at[where], target))
+        else:
+            where = (slice(None), place[1]) + (slice(None),) * 3 + (self.columns,)
+            self.waiting.append(self.send(self.out.at[where], self.out.at[where], sibling()))
+
+    def arrive(self):
+        for copy in self.waiting:
+            copy.wait_recv()
+        self.waiting = []
+
+
+class GatherHeads(Sender):
+    phases = 3
+
+    def __init__(self, shard, out, sems, local_sem):
+        super().__init__(sems)
+        self.shard, self.out = shard, out
+        self.waiting = []
+        self.own = pltpu.make_async_copy(shard.at[lax.axis_index("ctx")], out.at[place_of()], local_sem)
+        self.own.start()
+
+    def stage(self, number):
+        z, core, y, x = place_of()
+        self.arrive()
+        if number == 0:
+            for p in others()[:-1]:
+                target = (lax.axis_index("dp"), p)
+                self.waiting.append(self.send(self.shard.at[p], self.out.at[z, core, y, x], target))
+        elif number == 1:
+            self.own.wait()
+            for _, target in along(0):
+                self.waiting.append(self.send(self.out.at[z, core], self.out.at[z, core], target))
+        else:
+            where = (slice(None), core)
+            self.waiting.append(self.send(self.out.at[where], self.out.at[where], sibling()))
+
+    arrive = Gather.arrive
+
+
+class Ticker:
+    def __init__(self):
+        self.chunks, self.steps = [], []
+
+    def pipeline(self, chunks):
+        self.chunks = chunks
+        self.done = [0] * len(chunks)
+        for t in range(len(chunks) + 4 * DEPTH):
+            for number in (0, 3, 2, 1):
+                i = t - DEPTH * number
+                if 0 <= i < len(chunks) and number < chunks[i].phases:
+                    self.steps.append((i, number))
+
+    def tick(self, count=1):
+        for _ in range(count):
+            if self.steps:
+                i, number = self.steps.pop(0)
+                self.chunks[i].stage(number)
+                self.done[i] = number + 1
+
+    def need(self, i):
+        while self.done[i] < self.chunks[i].phases:
+            self.tick()
+        self.chunks[i].arrive()
+
+
+class Scatter(Sender):
+    phases = 5
+
+    def __init__(self, parts, emit, scratch, sems, local_sem, before=None, credit=None, final=True, first=0):
+        super().__init__(sems)
+        self.parts, self.emit, self.local_sem, self.first = parts, emit, local_sem, first
+        self.held, self.across, *landing = scratch
+        self.pieces = [(columns, order[::-1], landing[3 * i:3 * i + 3])
+                       for i, (columns, order) in enumerate(pieces_of(self.held.shape[-1], THIRD))]
+        self.waiting, self.before, self.credit, self.final = [], before, credit, final
+
+    @staticmethod
+    def scratch(shape, dtype):
+        sizes = dict(zip((0, 2, 3), grid_of()))
+        whole = (*sizes.values(), *shape)
+        found = [whole, whole]
+        for columns, order in pieces_of(shape[-1], THIRD):
+            order = order[::-1]
+            for number in range(3):
+                rest = [sizes[a] for a in sizes if a in order[number + 1:]]
+                found.append((sizes[order[number]] - 1, *rest, shape[0], columns.size))
+        return [pltpu.VMEM(s, dtype) for s in found]
+
+    def targets(self):
+        return [target for axis in (0, 2, 3) for _, target in along(axis)] + [sibling()]
+
+    def open(self):
+        if self.before is not None:
+            self.before.finish()
+            pl.semaphore_wait(self.credit, len(self.targets()))
+
+    def close(self):
+        if not self.final:
+            for target in self.targets():
+                pl.semaphore_signal(self.credit, inc=1, device_id=target, device_id_type=MESH)
+
+    arrive = Gather.arrive
+
+    def stage(self, number):
+        place = place_of()
+        sizes = dict(zip((0, 2, 3), grid_of()))
+        self.arrive()
+        if number == 0:
+            self.open()
+            columns = (slice(None),) * 3 + (pl.ds(self.first, self.held.shape[-1]),)
+            self.own = pltpu.make_async_copy(self.parts.at[(slice(None), place[1]) + columns], self.held, self.local_sem)
+            self.own.start()
+            self.waiting.append(self.send(self.parts.at[(slice(None), 1 - place[1]) + columns], self.across, sibling()))
+            return
+        if number == 1:
+            self.own.wait()
+            add_into(self.held, self.across, list(sizes.values()))
+        for columns, order, landing in self.pieces:
+            if number > 1:
+                mine = order[:number - 1]
+                where = tuple(place[a] if a in mine else slice(None) for a in sizes) + (slice(None), columns)
+                lead = [sizes[a] for a in sizes if a not in mine]
+                landed = landing[number - 2]
+                if number < 4:
+                    for i in range(landed.shape[0]):
+                        add_into(self.held.at[where], landed.at[i], lead)
+                else:
+                    total = self.held[where].astype(jnp.float32)
+                    for i in range(landed.shape[0]):
+                        total = total + landed[i].astype(jnp.float32)
+                    self.emit(pl.ds(self.first + columns.start, columns.size), total)
+            if number < 4:
+                axis, mine = order[number - 1], order[:number - 1]
+                for i, (there, target) in enumerate(along(axis)):
+                    where = tuple(there if a == axis else place[a] if a in mine else slice(None) for a in sizes)
+                    src = self.held.at[where + (slice(None), columns)]
+                    self.waiting.append(self.send(src, landing[number - 1].at[i], target))
+        if number == 4:
+            self.close()
+
+
+class ScatterHeads(Scatter):
+    phases = 4
+
+    def __init__(self, parts, out, scratch, sems, local_sem, before=None, credit=None, final=True):
+        Sender.__init__(self, sems)
+        self.parts, self.out, self.local_sem = parts, out, local_sem
+        self.across, self.landed, self.sums = scratch
+        self.waiting, self.before, self.credit, self.final = [], before, credit, final
+
+    def targets(self):
+        return [target for _, target in along(0)] + [sibling()]
+
+    def stage(self, number):
+        nz, ny, nx = grid_of()
+        z, core, y, x = place_of()
+        me = lax.axis_index("ctx")
+        self.arrive()
+        if number == 0:
+            if self.before is not None:
+                pl.semaphore_wait(self.credit, len(self.targets()))
+            self.waiting.append(self.send(self.parts.at[:, 1 - core], self.across, sibling()))
+        elif number == 1:
+            add_into(self.parts.at[:, core], self.across, [nz, ny, nx])
+            for i, (there, target) in enumerate(along(0)):
+                self.waiting.append(self.send(self.parts.at[there, core], self.landed.at[i], target))
+        elif number == 2:
+            for j in range(ny):
+                for k in range(nx):
+                    total = self.parts[z, core, j, k].astype(jnp.float32)
+                    for i in range(nz - 1):
+                        total = total + self.landed[i, j, k].astype(jnp.float32)
+                    self.sums[j * nx + k] = total
+            self.close()
+            for p in others()[:-1]:
+                self.waiting.append(self.send(self.sums.at[p], self.out.at[me], (lax.axis_index("dp"), p)))
+            self.own = pltpu.make_async_copy(self.sums.at[me], self.out.at[me], self.local_sem)
+            self.own.start()
+
+    def finish(self):
+        self.arrive()
+        for copy in self.flying:
+            copy.wait_send()
+        self.flying = []
+        if self.own is not None:
+            self.own.wait()
+        self.own = None
+
+
+class Rota:
+    def __init__(self):
+        self.queue = []
+
+    def add(self, chunk):
+        chunk.stage(0)
+        self.queue.append([chunk, 1])
+
+    def tick(self, count=1):
+        for _ in range(count):
+            if not self.queue:
+                return
+            item = self.queue.pop(0)
+            item[0].stage(item[1])
+            item[1] += 1
+            if item[1] < item[0].phases:
+                self.queue.append(item)
+
+    def close(self, chunk):
+        while any(item[0] is chunk for item in self.queue):
+            self.tick()
+
+
+def run_kernel(body, inputs, outputs, scratch, collective_id, name):
+    def leaves(value):
+        return [v for part in value for v in leaves(part)] if isinstance(value, list) else [value]
+
+    def again(value, refs):
+        return [again(v, refs) for v in value] if isinstance(value, list) else next(refs)
+
+    def flat(group):
+        return leaves(list(group.values()))
+
+    def rebuilt(group, refs):
+        return {k: again(value, refs) for k, value in group.items()}
+
+    def kernel(*refs):
+        refs = iter(refs)
+        body(types.SimpleNamespace(**rebuilt(inputs, refs), **rebuilt(outputs, refs), **rebuilt(scratch, refs)))
+    found = pl.pallas_call(
+        kernel,
+        out_shape=[s for s, _ in flat(outputs)],
+        in_specs=[s for _, s in flat(inputs)],
+        out_specs=[s for _, s in flat(outputs)],
+        scratch_shapes=flat(scratch),
+        compiler_params=pltpu.CompilerParams(collective_id=collective_id, has_side_effects=True, vmem_limit_bytes=60 << 20),
+        name=name,
+    )(*[a for a, _ in flat(inputs)])
+    return types.SimpleNamespace(**rebuilt(outputs, iter(found)))
+
+
 class Keep:
     def __init__(self, sems):
         self.sems, self.count, self.flying = sems, 0, []
@@ -819,6 +1098,7 @@
         copy.start()
         self.count += 1
         self.flying.append(copy)
+        return copy
 
     def finish(self):
         for copy in self.flying:
@@ -828,7 +1108,7 @@
 def unpack(blocks, dst):
     nz, cores, ny, nx, rows, width = blocks.shape
     each = ny * nx * rows
-    part = min(width, 512)
+    part = next(p for p in (512, 256, 128) if width % p == 0)
 
     def body(i, carry):
         for c in range(width // part):
@@ -839,196 +1119,469 @@
     lax.fori_loop(0, nz * cores, body, 0)
 
 
-KEPT = ("x", "middle", "normed_t", "qkv", "lse", "att", "gate", "up", "nffn_t")
-
-
-def kept_shapes(count, model, wide):
-    size, each = lax.axis_size("ctx"), heads_each()
-    f32, bf16 = jnp.float32, jnp.bfloat16
-    return {
-        "x": ((count, model), f32), "middle": ((count, model), f32), "normed_t": ((model, count), bf16),
-        "qkv": ((3, each * HEAD_DIM, count * size), bf16), "lse": ((each, 1, count * size), f32),
-        "att": ((each * size * HEAD_DIM, count), bf16), "gate": ((count, wide), f32), "up": ((count, wide), f32),
-        "nffn_t": ((model, count), bf16)}
-
-
-def named(names, refs):
-    return dict(zip(names, refs, strict=True))
-
-
-def forward_kernel(layers, vocab, third, names, *refs):
-    r = named(names, refs)
-    ends = ends_of(r["lengths"])
+def to_blocks(dst, columns, values):
+    nz, cores, ny, nx, rows, _ = dst.shape
+    for b in range(nz * cores * ny * nx):
+        g, k = divmod(b, ny * nx)
+        dst[g // cores, g % cores, k // nx, k % nx, :, columns] = low(values[b * rows:(b + 1) * rows])
+
+
+def norm_back(values, gain, upstream):
+    scale = inverse_rms(values)
+    scaled = upstream * gain
+    mean = jnp.mean(values * scaled, -1, keepdims=True)
+    return scale * scaled - values * (scale * scale * scale * mean), jnp.sum(upstream * values * scale, 0, keepdims=True)
+
+
+def from_slot(i):
+    size, me = lax.axis_size("ctx"), lax.axis_index("ctx")
+    return lax.rem(me + size - 1 - i, size)
+
+
+def gain_rows(small, vocab, layers):
+    at = vocab + CONV + 2
+    rows = small[:, at // LANES * LANES:].T
+    at = at % LANES
+    return [rows[at + l:at + l + 1, :] for l in range(2 * layers)]
+
+
+def forward_body(vocab, layers, r):
+    ends = ends_of(r.lengths)
     size, me = lax.axis_size("ctx"), lax.axis_index("ctx")
     each = heads_each()
-    keep = Keep(r["keep_sems"])
-    kinds = ["small"] + [f"{kind}{l}" for l in range(layers) for kind in ("attn", "ffn", "down")]
+    base = each * HEAD_DIM
+    keep = Keep(r.keep_sems)
     greet_all()
-    ids, count = r["ids"], r["byte_ids"].shape[1]
+    ids, count = r.ids, r.byte_ids.shape[1]
     near = []
     for i, (there, at) in enumerate(((lax.rem(me + 1, size), 0), (lax.rem(me + size - 1, size), 2))):
-        copy = to_group(r["byte_ids"], ids.at[:, pl.ds(at * count, count)], r["ids_sems"], (i,), there)
+        copy = to_group(r.byte_ids, ids.at[:, pl.ds(at * count, count)], r.ids_sems, (i,), there)
         copy.start()
         near.append(copy)
-    ids[:, count:2 * count] = r["byte_ids"][...]
-    chunks = [GatherChunk(r["shard_" + k], r["full_" + k], r["sems_" + k], r["local_sems"].at[i], third) for i, k in enumerate(kinds)]
-    ticker = Ticker(chunks)
+    ids[:, count:2 * count] = r.byte_ids[...]
+    chunks = [Gather([(r.small, 0)], r.full_small, r.small_sems, r.local_sems.at[0])]
+    model = r.encoded.shape[1]
+    wide = r.gate_w.shape[2]
+    for l in range(layers):
+        chunks.append(GatherHeads(r.heads_w.at[l], r.full_heads[l], r.heads_sems.at[l], r.more_sems.at[l, 1]))
+        sources = [(r.gate_w.at[l], 0), (r.up_w.at[l], wide), (r.out_w.at[l], 2 * wide)]
+        for k, (at, part) in enumerate(splits_of(r.full_ffn[l].shape[-1], SPLIT)):
+            chunks.append(Gather(sources, r.full_ffn[l], r.ffn_sems.at[l, k], r.local_sems.at[1 + l * SPLIT + k], at, part))
+        chunks.append(Gather([(r.down_w.at[l], 0)], r.full_down[l], r.down_sems.at[l], r.more_sems.at[l]))
+    ticker = Ticker()
+    ticker.pipeline(chunks)
     tick = ticker.tick
     tick(2)
     tokens = count // 2
-    seg_all = r["seg_all"]
+    seg_all = r.seg_all
     seg_all[...] = segments(2 * lax.broadcasted_iota(jnp.int32, seg_all.shape, 0), ends)
     for copy in near:
         copy.wait_recv()
     ticker.need(0)
-    small = r["small_wide"]
-    for z in range(r["full_small"].shape[0]):
-        found = r["full_small"][z].astype(jnp.float32)
-        rows = math.prod(found.shape[:-1])
-        small[z * rows:(z + 1) * rows, :] = jnp.concatenate(
-            [found[i, j, k] for i in range(found.shape[0]) for j in range(found.shape[1]) for k in range(found.shape[2])], 0)
-    tick(2)
-    stream = gbst_forward(ends, ids[...], me * count, small[...], r["conv"], r["choice"], vocab, tokens, tick).T
-    at = vocab + CONV + 2
-    gains = small[:, at // 128 * 128:].T
-    at = at % 128
-    model = stream.shape[1]
-    keep(r["conv"], r["out_conv"])
+    small = r.small_wide
+    nz, cores, ny, nx, rows, _ = r.full_small.shape
+    for b in range(nz * cores * ny * nx):
+        place = (b // (cores * ny * nx), b // (ny * nx) % cores, b // nx % ny, b % nx)
+        small[b * rows:(b + 1) * rows, :] = r.full_small[place].astype(jnp.float32)
+    tick()
+    stream = gbst_forward(ends, ids[...], me * count, small[...], r.conv, r.choice, vocab, tokens, tick).T
+    gains = gain_rows(small, vocab, layers)
+    keep(r.conv, r.out_conv)
     for l in range(layers):
-        gain_a, gain_f = gains[at + l:at + l + 1, :], gains[at + layers + l:at + layers + l + 1, :]
-        kept = {k: r[f"{k}{l}"] for k in KEPT}
-        w_attn, w_ffn, w_down = r["w_attn"], r["w_ffn"], r["w_down"]
-        first = 1 + 3 * l
-
-        def fetch(i, dst, sem):
-            ticker.need(i)
-            copy = pltpu.make_async_copy(r["full_" + kinds[i]], dst, r["load_sems"].at[l, sem])
+        base_chunk = 1 + (2 + SPLIT) * l
+        nrm, qkv, att = r.nrm[l], r.qkv[l], r.att[l]
+        r.x[l][...] = stream
+        r.mine[...] = flip(low(stream * inverse_rms(stream) * gains[l]))
+        spread = []
+        for i, p in enumerate(others()[:-1]):
+            copy = to_group(r.mine, nrm.at[:, tokens_of(me, tokens)], r.nrm_sems.at[l], (i,), p)
             copy.start()
-            return copy
-        load = fetch(first, r["blocks_attn"], 0)
-        kept["x"][...] = stream
-        normed = low(stream * inverse_rms(stream) * gain_a)
-        kept["normed_t"][...] = flip(normed)
+            spread.append(copy)
+        nrm[:, tokens_of(me, tokens)] = r.mine[...]
+        keep(r.x[l], r.out_x[l])
+        ticker.need(base_chunk)
+        unpack(r.full_heads[l], r.w_heads[l])
+        keep(r.w_heads[l], r.out_w_heads[l])
+        r.w_turned[...] = flip(r.w_heads[l][...])
+        for i in range(-1, size - 1):
+            if i >= 0:
+                spread[i].wait_recv()
+            theirs = tokens_of(me if i < 0 else from_slot(i), tokens)
+            qkv[:, theirs] = low(dot(r.w_turned[...], nrm[:, theirs]))
+            tick()
+        keep(nrm, r.out_nrm[l])
+        keep(qkv, r.out_qkv[l])
+        copies = []
+        for h in range(each):
+            query = pl.ds(h * HEAD_DIM, HEAD_DIM)
+            key = flip(qkv[base + h * HEAD_DIM:base + (h + 1) * HEAD_DIM, :])
+            value_t = qkv[2 * base + h * HEAD_DIM:2 * base + (h + 1) * HEAD_DIM, :]
+            rows = pl.ds(pl.multiple_of((me * each + h) * HEAD_DIM, HEAD_DIM), HEAD_DIM)
+            for i, p in enumerate(others()):
+                theirs = tokens_of(p, tokens)
+                seg_q = segments(2 * (p * tokens + lax.broadcasted_iota(jnp.int32, (1, tokens), 1)), ends)
+                scores = jnp.where(seg_all[...] == seg_q, dot(key, qkv[query, theirs]), NEG_FILL)
+                top = jnp.max(scores, 0, keepdims=True)
+                probs = jnp.exp(scores - top)
+                total = jnp.sum(probs, 0, keepdims=True)
+                r.lse[l][h, :, theirs] = top + jnp.log(total)
+                result = low(dot(value_t, low(probs)) / total)
+                if i == size - 1:
+                    att[rows, :] = result
+                else:
+                    r.att_send[h, i] = result
+                    copy = to_group(r.att_send.at[h, i], att.at[rows], r.att_sems.at[l], (h, i), p)
+                    copy.start()
+                    copies.append(copy)
+                tick()
+        keep(r.lse[l], r.out_lse[l])
+        for k in range(SPLIT):
+            ticker.need(base_chunk + 1 + k)
+        load = pltpu.make_async_copy(r.full_ffn[l], r.blocks, r.load_sems.at[l, 0])
+        load.start()
+        for copy in copies:
+            copy.wait_recv()
+        keep(att, r.out_att[l])
         load.wait()
-        unpack(r["blocks_attn"], w_attn)
-        tick()
-        qkv_all = r["qkv_all"]
-        for part in range(3):
-            for c in range(model // CHUNK):
-                columns = pl.ds(part * model + c * CHUNK, CHUNK)
-                qkv_all[part, c * CHUNK:(c + 1) * CHUNK, :] = low(dot(normed, w_attn[:, columns]).T)
-        qkv_copies = spread_heads(qkv_all, kept["qkv"], r["sems_qkv"].at[l], r["own_sems"].at[l], each)
-        tick()
-        keep(kept["x"], r[f"out_x{l}"])
-        keep(kept["normed_t"], r[f"out_normed_t{l}"])
-        out_copies = attention_forward(each, seg_all, ends, kept["qkv"], kept["lse"], r["out_send"], kept["att"],
-                                       qkv_copies, r["sems_att"].at[l], tick)
-        for copy in out_copies:
-            copy.wait_recv()
-        keep(kept["qkv"], r[f"out_qkv{l}"])
-        keep(kept["lse"], r[f"out_lse{l}"])
-        keep(kept["att"], r[f"out_att{l}"])
-        attended = flip(kept["att"][:model, :])
-        mid = stream + dot(attended, w_attn[:, 3 * model:])
-        kept["middle"][...] = mid
-        after = low(mid * inverse_rms(mid) * gain_f)
-        r["nffn"][...] = after
-        kept["nffn_t"][...] = flip(after)
-        r["total"][...] = mid
-        keep(kept["middle"], r[f"out_middle{l}"])
-        keep(kept["nffn_t"], r[f"out_nffn_t{l}"])
-        load = fetch(first + 1, r["blocks_ffn"], 1)
-        load_down = fetch(first + 2, w_down, 2)
+        unpack(r.blocks, r.w_ffn)
+        mid = stream + dot(flip(att[...]), r.w_ffn[:, 2 * wide:])
+        r.middle[l][...] = mid
+        after = low(mid * inverse_rms(mid) * gains[layers + l])
+        r.nffn[...] = after
+        r.nffn_t[l][...] = flip(after)
+        r.total[...] = mid
+        keep(r.middle[l], r.out_middle[l])
+        keep(r.nffn_t[l], r.out_nffn_t[l])
+        ticker.need(base_chunk + 1 + SPLIT)
+        load = pltpu.make_async_copy(r.full_down[l], r.w_down, r.load_sems.at[l, 1])
+        load.start()
         load.wait()
-        unpack(r["blocks_ffn"], w_ffn)
-        tick()
-        load_down.wait()
-        nz, cores, ny, nx, rows, _ = w_down.shape
-        wide, part = nz * cores * ny * nx * rows, ny * nx * rows
+        part = wide // (nz * cores)
 
         def step(c, carry):
             columns = pl.ds(pl.multiple_of(c * part, part), part)
-            gate = dot(r["nffn"][...], w_ffn[:, columns])
-            up = dot(r["nffn"][...], w_ffn[:, pl.ds(pl.multiple_of(wide + c * part, part), part)])
-            kept["gate"][:, columns] = gate
-            kept["up"][:, columns] = up
+            gate = dot(r.nffn[...], r.w_ffn[:, columns])
+            up = dot(r.nffn[...], r.w_ffn[:, pl.ds(pl.multiple_of(wide + c * part, part), part)])
             hidden = low(gelu_parts(gate)[0] * up)
-            r["total"][...] += dot(hidden, w_down[c // cores, c % cores].reshape(part, model))
+            r.total[...] += dot(hidden, r.w_down[c // cores, c % cores].reshape(part, model))
             return carry
         half = nz * cores // 2
         lax.fori_loop(0, half, step, 0)
         tick(2)
         lax.fori_loop(half, nz * cores, step, 0)
-        keep(kept["gate"], r[f"out_gate{l}"])
-        keep(kept["up"], r[f"out_up{l}"])
-        stream = r["total"][...]
-        for made in qkv_copies:
-            for copy in made[:-1]:
-                copy.wait_send()
-        for copy in out_copies:
+        stream = r.total[...]
+        for copy in spread + copies:
             copy.wait_send()
-    r["encoded"][...] = low(stream)
+    r.encoded[...] = low(stream)
     for copy in near:
         copy.wait_send()
-    for i in range(len(chunks)):
+    for i, chunk in enumerate(chunks):
         ticker.need(i)
-    for chunk in chunks:
         chunk.finish()
     keep.finish()
 
 
-def forward_pass(lengths, byte_ids, small, shards, layers, vocab, third, collective_id):
+def like(shape, dtype):
+    return jax.ShapeDtypeStruct(shape, dtype)
+
+
+def kept_shapes(tokens, model):
+    size, each = lax.axis_size("ctx"), heads_each()
+    f32, bf16 = jnp.float32, jnp.bfloat16
+    turned = -(-3 * each * HEAD_DIM // LANES) * LANES
+    return dict(x=((tokens, model), f32), middle=((tokens, model), f32), nrm=((model, tokens * size), bf16),
+                qkv=((turned, tokens * size), bf16), lse=((each, 1, tokens * size), f32),
+                att=((each * size * HEAD_DIM, tokens), bf16), nffn_t=((model, tokens), bf16))
+
+
+def forward_pass(lengths, byte_ids, small, heads_w, out_w, gate_w, up_w, down_w, vocab):
     nz, ny, nx = grid_of()
     size, each = lax.axis_size("ctx"), heads_each()
-    model = shards[0].shape[1] // 4
+    layers, _, model = out_w.shape
+    wide = gate_w.shape[2]
     tokens = byte_ids.shape[1] // 2
-    wide = shards[1].shape[1] // 2
     span = byte_ids.shape[1] + 2 * HALO
     f32, bf16 = jnp.float32, jnp.bfloat16
-    made = lambda shape, dtype: jax.ShapeDtypeStruct(shape, dtype)
-    whole = lambda s: (nz, CORES, ny, nx) + s.shape
-    kinds = [f"{kind}{l}" for l in range(layers) for kind in ("attn", "ffn", "down")]
-    inputs = {"lengths": (lengths, SMEM), "byte_ids": (byte_ids, VMEM), "shard_small": (small, ANY)}
-    for k, s in zip(kinds, shards):
-        inputs["shard_" + k] = (s, ANY)
-    outputs = {"encoded": (made((tokens, model), bf16), VMEM), "small_wide": (made((model, small.shape[1]), f32), VMEM),
-               "ids": (made((1, 3 * byte_ids.shape[1]), jnp.int32), VMEM), "choice": (made((2 * len(BLOCKS), tokens), f32), VMEM),
-               "out_conv": (made((model, span), f32), ANY)}
-    for k, s in zip(kinds, shards):
-        outputs["full_" + k] = (made(whole(s), bf16), ANY)
-    shapes = kept_shapes(tokens, model, wide)
-    for l in range(layers):
-        for k in KEPT:
-            outputs[f"out_{k}{l}"] = (made(*shapes[k]), ANY)
-    rows = each * size * HEAD_DIM
-    dma = pltpu.SemaphoreType.DMA
-    scratch = {"full_small": pltpu.VMEM(whole(small), bf16), "conv": pltpu.VMEM((model, span), f32),
-               "w_attn": pltpu.VMEM((model, 4 * model), bf16), "w_ffn": pltpu.VMEM((model, 2 * wide), bf16),
-               "w_down": pltpu.VMEM(whole(shards[2]), bf16), "blocks_attn": pltpu.VMEM(whole(shards[0]), bf16),
-               "blocks_ffn": pltpu.VMEM(whole(shards[1]), bf16), "qkv_all": pltpu.VMEM((3, rows, tokens), bf16),
-               "out_send": pltpu.VMEM((each, size - 1, HEAD_DIM, tokens), bf16),
-               "seg_all": pltpu.VMEM((tokens * size, tokens), jnp.int32), "nffn": pltpu.VMEM((tokens, model), bf16),
-               "total": pltpu.VMEM((tokens, model), f32),
-               "keep_sems": dma((1 + layers * len(KEPT),)), "ids_sems": dma((2, 2)), "local_sems": dma((1 + len(kinds),)),
-               "load_sems": dma((layers, 3)), "own_sems": dma((layers, each)),
-               "sems_qkv": dma((layers, 2, each, size - 1)), "sems_att": dma((layers, 2, each, size - 1)),
-               "sems_small": dma((2, hops(small.shape[1], third)))}
-    for k, s in zip(kinds, shards):
-        scratch["sems_" + k] = dma((2, hops(s.shape[1], third)))
-    for l in range(layers):
-        for k in KEPT:
-            scratch[f"{k}{l}"] = pltpu.VMEM(*shapes[k])
-    names = [*inputs, *outputs, *scratch]
-    found = pl.pallas_call(
-        functools.partial(forward_kernel, layers, vocab, third, names),
-        out_shape=[s for s, _ in outputs.values()],
-        in_specs=[s for _, s in inputs.values()],
-        out_specs=[s for _, s in outputs.values()],
-        scratch_shapes=list(scratch.values()),
-        compiler_params=pltpu.CompilerParams(collective_id=collective_id, has_side_effects=True, vmem_limit_bytes=60 << 20),
-        name="forward_pass",
-    )(*[a for a, _ in inputs.values()])
-    return named(outputs, found)
+    dma, vmem = pltpu.SemaphoreType.DMA, pltpu.VMEM
+    blocks = lambda rows, width: (nz, CORES, ny, nx, rows, width)
+    shapes = kept_shapes(tokens, model)
+    per_layer = lambda made: [made] * layers
+    ffn = blocks(gate_w.shape[1], 2 * wide + model)
+    down = blocks(*down_w.shape[1:])
+    heads = blocks(*heads_w.shape[2:])
+    inputs = dict(lengths=(lengths, SMEM), byte_ids=(byte_ids, VMEM), small=(small, ANY), heads_w=(heads_w, ANY),
+                  out_w=(out_w, ANY), gate_w=(gate_w, ANY), up_w=(up_w, ANY), down_w=(down_w, ANY))
+    outputs = dict(
+        encoded=(like((tokens, model), bf16), VMEM), small_wide=(like((model, small.shape[1]), f32), VMEM),
+        ids=(like((1, 3 * byte_ids.shape[1]), jnp.int32), VMEM), choice=(like((2 * len(BLOCKS), tokens), f32), VMEM),
+        out_conv=(like((model, span), f32), ANY), full_ffn=per_layer((like(ffn, bf16), ANY)),
+        full_down=per_layer((like(down, bf16), ANY)), out_w_heads=per_layer((like((model, heads[-1]), bf16), ANY)),
+        out_x=per_layer((like(*shapes["x"]), ANY)), out_middle=per_layer((like(*shapes["middle"]), ANY)),
+        out_nrm=per_layer((like(*shapes["nrm"]), ANY)), out_qkv=per_layer((like(*shapes["qkv"]), ANY)),
+        out_lse=per_layer((like(*shapes["lse"]), ANY)), out_att=per_layer((like(*shapes["att"]), ANY)),
+        out_nffn_t=per_layer((like(*shapes["nffn_t"]), ANY)))
+    scratch = {k: per_layer(vmem(*v)) for k, v in shapes.items()}
+    scratch.update(
+        full_small=vmem(blocks(*small.shape), bf16), conv=vmem((model, span), f32), full_heads=per_layer(vmem(heads, bf16)),
+        w_heads=per_layer(vmem((model, heads[-1]), bf16)), w_turned=vmem((heads[-1], model), bf16), w_ffn=vmem((model, ffn[-1]), bf16),
+        w_down=vmem(down, bf16), blocks=vmem(ffn, bf16), mine=vmem((model, tokens), bf16),
+        att_send=vmem((each, size - 1, HEAD_DIM, tokens), bf16), seg_all=vmem((tokens * size, tokens), jnp.int32),
+        nffn=vmem((tokens, model), bf16), total=vmem((tokens, model), f32),
+        keep_sems=dma((1 + 8 * layers,)), ids_sems=dma((2, 2)), local_sems=dma((1 + layers * SPLIT, 3)), more_sems=dma((layers, 2)),
+        load_sems=dma((layers, 2)), nrm_sems=dma((layers, 2, size - 1)), att_sems=dma((layers, 2, each, size - 1)),
+        small_sems=dma((2, hops(small.shape[1], THIRD))), heads_sems=dma((layers, 2, size + nz - 1)),
+        ffn_sems=dma((layers, SPLIT, 2, hops(ffn[-1], THIRD))), down_sems=dma((layers, 2, hops(model, THIRD))))
+    return run_kernel(functools.partial(forward_body, vocab, layers), inputs, outputs, scratch, 4, "forward_pass")
+
+
+def backward_body(vocab, layers, r):
+    ends = ends_of(r.lengths)
+    size, me = lax.axis_size("ctx"), lax.axis_index("ctx")
+    each = heads_each()
+    base = each * HEAD_DIM
+    tokens, model = r.out_grad.shape
+    wide = r.w_down.shape[0]
+    nz, cores, ny, nx, rows, _ = r.block_ffn.shape[1:]
+    part = wide // (nz * cores)
+    loads = {}
+
+    def load(key, src, dst, sem):
+        loads[key] = pltpu.make_async_copy(src, dst, sem)
+        loads[key].start()
+
+    def load_ffn(l):
+        sems = r.load_sems.at[l]
+        load(0, r.in_nffn_t[l], r.nffn_t, sems.at[0])
+        load(1, r.in_w_down[l], r.w_down, sems.at[1])
+        load(2, r.in_w_ffn[l], r.w_ffn, sems.at[2])
+        load(3, r.in_middle[l], r.middle, sems.at[3])
+        load(4, r.in_att[l], r.att, sems.at[4])
+
+    def load_attention(l):
+        sems = r.load_sems.at[l]
+        load(5, r.in_qkv[l], r.qkv, sems.at[5])
+        load(6, r.in_lse[l], r.lse, sems.at[6])
+        load(7, r.in_w_heads[l], r.w_heads, sems.at[7])
+        load(8, r.in_nrm[l], r.nrm, sems.at[8])
+        load(9, r.in_x[l], r.x, sems.at[9])
+    load_ffn(layers - 1)
+    load_attention(layers - 1)
+    greet_all()
+    gains = gain_rows(r.small_wide, vocab, layers)
+    d_gains = [None] * (2 * layers)
+    seg_all = r.seg_all
+    seg_all[...] = segments(2 * lax.broadcasted_iota(jnp.int32, seg_all.shape, 0), ends)
+    r.dqkv[...] = jnp.zeros(r.dqkv.shape, jnp.bfloat16)
+    r.grad[...] = r.out_grad[...].astype(jnp.float32)
+    rota = Rota()
+    tick = rota.tick
+    before = [None] * (2 + SPLIT)
+    made = []
+
+    def begin(kind, chunk):
+        made.append(chunk)
+        before[kind] = chunk
+        rota.add(chunk)
+    for l in reversed(range(layers)):
+        r.grad_low[...] = low(r.grad[...])
+        r.total[...] = jnp.zeros(r.total.shape, jnp.float32)
+        for key in range(3):
+            loads[key].wait()
+        r.nffn[...] = flip(r.nffn_t[...])
+
+        def saves(c, slot):
+            sems = r.save_sems.at[slot]
+            columns = pl.ds(pl.multiple_of(c * part, part), part)
+            later = pl.ds(pl.multiple_of(wide + c * part, part), part)
+            where = (slice(None),) * 5
+            return [pltpu.make_async_copy(r.block_down.at[slot], r.parts_down[l].at[c // cores, c % cores], sems.at[0]),
+                    pltpu.make_async_copy(r.block_ffn.at[slot, :, :, :, :, :, pl.ds(0, part)], r.parts_ffn[l].at[where + (columns,)], sems.at[1]),
+                    pltpu.make_async_copy(r.block_ffn.at[slot, :, :, :, :, :, pl.ds(part, part)], r.parts_ffn[l].at[where + (later,)], sems.at[2])]
+
+        def step(c, carry):
+            columns = pl.ds(pl.multiple_of(c * part, part), part)
+            later = pl.ds(pl.multiple_of(wide + c * part, part), part)
+            slot = lax.rem(c, 2)
+
+            @pl.when(c >= 2)
+            def _():
+                for copy in saves(c - 2, slot):
+                    copy.wait()
+            gate = dot(r.nffn[...], r.w_ffn[:, columns])
+            up = dot(r.nffn[...], r.w_ffn[:, later])
+            g_hidden = dot_nt(r.grad_low[...], r.w_down[columns, :])
+            act, slope = gelu_parts(gate)
+            g_gate = low(g_hidden * up * slope)
+            g_up = low(g_hidden * act)
+            d_down = low(dot(low((act * up).T), r.grad_low[...]))
+            r.block_down[slot] = d_down.reshape(r.block_down.shape[1:])
+            to_blocks(r.block_ffn.at[slot], slice(0, part), dot(r.nffn_t[...], g_gate))
+            to_blocks(r.block_ffn.at[slot], slice(part, 2 * part), dot(r.nffn_t[...], g_up))
+            for copy in saves(c, slot):
+                copy.start()
+            r.total[...] += dot_nt(g_gate, r.w_ffn[:, columns]) + dot_nt(g_up, r.w_ffn[:, later])
+            return carry
+        for c in range(0, nz * cores, 2):
+            lax.fori_loop(c, c + 2, step, 0)
+            tick()
+        for c in (nz * cores - 2, nz * cores - 1):
+            for copy in saves(c, c % 2):
+                copy.wait()
+
+        def emit_down(columns, total, l=l):
+            r.d_down[l, :, columns] = total
+
+        def emit_ffn(columns, total, l=l):
+            first, last = columns.start, columns.start + columns.size
+            for out, start in ((r.d_gate, 0), (r.d_up, wide), (r.d_out, 2 * wide)):
+                a, b = max(first, start), min(last, start + out.shape[2])
+                if a < b:
+                    out[l, :, a - start:b - start] = total[:, a - first:b - first]
+        if before[0] is not None:
+            rota.close(before[0])
+        begin(0, Scatter(r.parts_down[l], emit_down, r.down_scratch, r.down_sems.at[l], r.own_sems.at[l, 0], before[0], r.credits.at[0], l == 0))
+        loads[3].wait()
+        loads[4].wait()
+        back, d_gains[layers + l] = norm_back(r.middle[...], gains[layers + l], r.total[...])
+        r.grad[...] += back
+        r.grad_low[...] = low(r.grad[...])
+        r.go_all[0] = flip(dot_nt(r.grad_low[...], r.w_ffn[:, 2 * wide:]))
+        go_copies = spread_heads(r.go_all, r.go, r.go_sems.at[l], r.go_own.at[l], each)
+        to_blocks(r.block_out, slice(0, model), dot(r.att[...], r.grad_low[...]))
+        save = pltpu.make_async_copy(r.block_out, r.parts_ffn[l].at[(slice(None),) * 5 + (pl.ds(2 * wide, model),)], r.own_sems.at[l, 3])
+        save.start()
+        save.wait()
+        for k, (at, _) in enumerate(splits_of(r.parts_ffn[l].shape[-1], SPLIT)):
+            if before[2 + k] is not None:
+                rota.close(before[2 + k])
+            begin(2 + k, Scatter(r.parts_ffn[l], emit_ffn, r.ffn_scratch[k], r.ffn_sems.at[l, k], r.ffn_own.at[l, k],
+                                 before[2 + k], r.credits.at[2 + k], l == 0, at))
+        if l:
+            load_ffn(l - 1)
+        for key in range(5, 8):
+            loads[key].wait()
+        for h in range(each):
+            arrive(go_copies[h])
+            rows_h = [slice(k * base + h * HEAD_DIM, k * base + (h + 1) * HEAD_DIM) for k in range(3)]
+            key_t = r.qkv[rows_h[1], :]
+            key, value = flip(key_t), flip(r.qkv[rows_h[2], :])
+            g_key = jnp.zeros((HEAD_DIM, tokens * size), jnp.float32)
+            g_value = jnp.zeros((HEAD_DIM, tokens * size), jnp.float32)
+            for p in range(size):
+                theirs = slice(p * tokens, (p + 1) * tokens)
+                seg_q = segments(2 * (p * tokens + lax.broadcasted_iota(jnp.int32, (1, tokens), 1)), ends)
+                query_t, go_t = r.qkv[rows_h[0], theirs], r.go[0, h * HEAD_DIM:(h + 1) * HEAD_DIM, theirs]
+                scores = jnp.where(seg_all[...] == seg_q, dot(key, query_t), NEG_FILL)
+                probs = jnp.exp(scores - r.lse[h, :, theirs])
+                g_probs = dot(value, go_t)
+                inner = jnp.sum(probs * g_probs, 0, keepdims=True)
+                g_scores = low(probs * (g_probs - inner))
+                r.dqkv[rows_h[0], theirs] = low(dot(key_t, g_scores))
+                g_key = g_key + dot_nt(query_t, g_scores)
+                g_value = g_value + dot_nt(go_t, low(probs))
+                tick()
+            r.dqkv[rows_h[1], :] = low(g_key)
+            r.dqkv[rows_h[2], :] = low(g_value)
+        spread = []
+        for i, p in enumerate(others()):
+            mine = dot(r.w_heads[...], r.dqkv[:, tokens_of(p, tokens)])
+            if i == size - 1:
+                r.summed[...] = mine
+            else:
+                r.sum_send[i] = low(mine)
+                copy = to_group(r.sum_send.at[i], r.sum_land.at[i], r.sum_sems.at[l], (i,), p)
+                copy.start()
+                spread.append(copy)
+        for key in (8, 9):
+            loads[key].wait()
+        if before[1] is not None:
+            rota.close(before[1])
+            before[1].finish()
+
+        def heads_step(i, carry):
+            each_rows = ny * nx * rows
+            found = dot_nt(r.nrm[pl.ds(pl.multiple_of(i * each_rows, each_rows), each_rows), :], r.dqkv[...])
+            for k in range(ny * nx):
+                r.block_heads[i // cores, i % cores, k // nx, k % nx] = low(found[k * rows:(k + 1) * rows])
+            return carry
+        lax.fori_loop(0, nz * cores, heads_step, 0)
+        begin(1, ScatterHeads(r.block_heads, r.d_heads[l], r.heads_scratch, r.heads_sems.at[l], r.own_sems.at[l, 2], before[1], r.credits.at[1], l == 0))
+        tick()
+        for i, copy in enumerate(spread):
+            copy.wait_recv()
+            r.summed[...] += r.sum_land[i].astype(jnp.float32)
+        back, d_gains[l] = norm_back(r.x[...], gains[l], r.summed[...].T)
+        r.grad[...] += back
+        if l:
+            load_attention(l - 1)
+        for copies in go_copies:
+            for copy in copies[:-1]:
+                copy.wait_send()
+        for copy in spread:
+            copy.wait_send()
+    out = r.small_grad
+    out[...] = jnp.zeros(out.shape, jnp.float32)
+    gbst_backward(ends, r.ids[...], me * 2 * tokens, r.small_wide[...], r.conv, r.choice, r.grad[...].T, vocab, out, tick)
+    at = vocab + CONV + 2
+    turned = jnp.concatenate(d_gains + [jnp.zeros((-2 * layers % 8, model), jnp.float32)], 0).T
+    for i in range(2 * layers):
+        out[:, at + i:at + i + 1] = turned[:, i:i + 1]
+    to_blocks(r.block_small, slice(None), out[...])
+
+    def emit_small(columns, total):
+        r.d_small[:, columns] = total
+    begin(0, Scatter(r.block_small, emit_small, r.small_scratch, r.small_sems, r.own_sems.at[layers, 0]))
+    while rota.queue:
+        tick()
+    for chunk in made:
+        chunk.finish()
+
+
+def backward_pass(lengths, out_grad, fwd, vocab, heads_width):
+    nz, ny, nx = grid_of()
+    size, each = lax.axis_size("ctx"), heads_each()
+    tokens, model = out_grad.shape
+    layers = len(fwd.full_ffn)
+    w_ffn = [w.reshape(-1, w.shape[-1]) for w in fwd.full_ffn]
+    w_down = [w.reshape(-1, w.shape[-1]) for w in fwd.full_down]
+    wide = w_down[0].shape[0]
+    part = wide // (nz * CORES)
+    f32, bf16 = jnp.float32, jnp.bfloat16
+    dma, vmem = pltpu.SemaphoreType.DMA, pltpu.VMEM
+    shapes = kept_shapes(tokens, model)
+    per_layer = lambda found: [found] * layers
+    ffn, down = fwd.full_ffn[0].shape, fwd.full_down[0].shape
+    heads = ffn[:5] + (heads_width,)
+    small = ffn[:5] + (fwd.small_wide.shape[1],)
+    anywhere = lambda arrays: [(a, ANY) for a in arrays]
+    inputs = dict(
+        lengths=(lengths, SMEM), out_grad=(out_grad, VMEM), small_wide=(fwd.small_wide, VMEM), ids=(fwd.ids, VMEM),
+        choice=(fwd.choice, VMEM), conv=(fwd.out_conv, VMEM), in_w_heads=anywhere(fwd.out_w_heads), in_w_ffn=anywhere(w_ffn),
+        in_w_down=anywhere(w_down), in_x=anywhere(fwd.out_x), in_middle=anywhere(fwd.out_middle), in_nrm=anywhere(fwd.out_nrm),
+        in_qkv=anywhere(fwd.out_qkv), in_lse=anywhere(fwd.out_lse), in_att=anywhere(fwd.out_att), in_nffn_t=anywhere(fwd.out_nffn_t))
+    outputs = dict(
+        d_small=(like(small[4:], f32), VMEM), d_heads=per_layer((like((size,) + heads[4:], f32), ANY)),
+        d_gate=(like((layers, ffn[4], wide), f32), VMEM), d_up=(like((layers, ffn[4], wide), f32), VMEM),
+        d_out=(like((layers, ffn[4], model), f32), VMEM), d_down=(like((layers,) + down[4:], f32), VMEM),
+        parts_ffn=per_layer((like(ffn, bf16), ANY)), parts_down=per_layer((like(down, bf16), ANY)))
+    scratch = {k: vmem(*v) for k, v in shapes.items()}
+    scratch.update(
+        grad=vmem((tokens, model), f32), total=vmem((tokens, model), f32), grad_low=vmem((tokens, model), bf16),
+        nffn=vmem((tokens, model), bf16), w_heads=vmem((model, heads_width), bf16), w_ffn=vmem(w_ffn[0].shape, bf16),
+        w_down=vmem(w_down[0].shape, bf16), block_ffn=vmem((2,) + ffn[:5] + (2 * part,), bf16), block_down=vmem((2,) + down[2:], bf16),
+        block_out=vmem(ffn[:5] + (model,), bf16), block_heads=vmem(heads, bf16), block_small=vmem(small, bf16),
+        go_all=vmem((1,) + shapes["att"][0], bf16), go=vmem((1, each * HEAD_DIM, tokens * size), bf16), dqkv=vmem(*shapes["qkv"]),
+        summed=vmem((model, tokens), f32), sum_send=vmem((size - 1, model, tokens), bf16),
+        sum_land=vmem((size - 1, model, tokens), bf16),
+        seg_all=vmem((tokens * size, tokens), jnp.int32), small_grad=vmem(fwd.small_wide.shape, f32),
+        down_scratch=Scatter.scratch(down[4:], bf16), ffn_scratch=[Scatter.scratch((ffn[4], w), bf16) for _, w in splits_of(ffn[-1], SPLIT)], ffn_own=dma((layers, SPLIT)),
+        small_scratch=Scatter.scratch(small[4:], bf16),
+        heads_scratch=[vmem((nz, ny, nx) + heads[4:], bf16), vmem((nz - 1, ny, nx) + heads[4:], bf16), vmem((size,) + heads[4:], f32)],
+        load_sems=dma((layers, 10)), save_sems=dma((2, 3)), own_sems=dma((layers + 1, 4)), go_own=dma((layers, each)),
+        go_sems=dma((layers, 2, each, size - 1)), sum_sems=dma((layers, 2, size - 1)), heads_sems=dma((layers, 2, size + nz - 1)),
+        ffn_sems=dma((layers, SPLIT, 2, hops(ffn[-1], THIRD))), down_sems=dma((layers, 2, hops(model, THIRD))),
+        small_sems=dma((2, hops(small[-1], THIRD))), credits=pltpu.SemaphoreType.REGULAR((2 + SPLIT,)))
+    return run_kernel(functools.partial(backward_body, vocab, layers), inputs, outputs, scratch, 5, "backward_pass")
 
 
 def packed_small(embed, conv_weight, conv_bias, scorer, norm_attn, norm_ffn):
@@ -1072,55 +1625,35 @@
     return stream.astype(jnp.bfloat16), full, small_wide, ids, conv, choice, kept
 
 
-def fused_forward(lengths, byte_ids, shards, layer_count, vocab, model):
-    kinds = [f"{kind}{layer}" for layer in range(layer_count) for kind in ("attn", "ffn", "down")]
-    fwd = forward_pass(lengths, byte_ids, shards[0], shards[1:], layer_count, vocab, THIRD, 4)
-    full = [fwd["full_" + k].reshape(-1, fwd["full_" + k].shape[-1]) for k in kinds]
-    kept = []
-    for layer in range(layer_count):
-        saved = [fwd[f"out_{k}{layer}"] for k in KEPT]
-        kept.append((saved[0], saved[1:]))
-    return fwd["encoded"], full, fwd["small_wide"], fwd["ids"], fwd["out_conv"], fwd["choice"], kept
-
-
-def on_device(
-    byte_ids,
-    lengths,
-    embed,
-    conv_weight,
-    conv_bias,
-    scorer,
-    norm_attn,
-    query_w,
-    key_w,
-    value_w,
-    attn_out_w,
-    norm_ffn,
-    gate_w,
-    up_w,
-    down_w,
-    out_grad,
-):
-    ctx_count = lax.axis_size("ctx")
-    ctx_place = lax.axis_index("ctx")
-    layer_count = query_w.shape[0]
-    vocab = embed.shape[0]
-    model = query_w.shape[2]
-    byte_count = byte_ids.shape[1]
-    small = packed_small(embed, conv_weight, conv_bias, scorer, norm_attn, norm_ffn)
+def head_columns(query_w, key_w, value_w):
+    layers, rows, model = query_w.shape
+    size = lax.axis_size("ctx")
+    found = [w.reshape(layers, rows, size, model // size).transpose(0, 2, 1, 3) for w in (query_w, key_w, value_w)]
+    found = jnp.concatenate(found, 3)
+    return jnp.pad(found, ((0, 0),) * 3 + ((0, -found.shape[3] % LANES),))
+
+
+def fused_step(lengths, byte_ids, small, heads_w, out_w, gate_w, up_w, down_w, out_grad, vocab):
+    fwd = forward_pass(lengths, byte_ids, small, heads_w, out_w, gate_w, up_w, down_w, vocab)
+    back = backward_pass(lengths, out_grad, fwd, vocab, heads_w.shape[3])
+    layers, rows, model = out_w.shape
+    each = model // lax.axis_size("ctx")
+    heads = jnp.stack(back.d_heads)
+    columns = [heads[..., i * each : (i + 1) * each].transpose(0, 2, 1, 3).reshape(layers, rows, model) for i in range(3)]
+    return fwd.encoded, back.d_small, (*columns, back.d_out, back.d_gate, back.d_up, back.d_down)
+
+
+def separate_step(lengths, byte_ids, small, query_w, key_w, value_w, out_w, gate_w, up_w, down_w, out_grad, vocab):
+    layer_count, _, model = query_w.shape
     shards = [small]
     for layer in range(layer_count):
-        shards.append(jnp.concatenate([query_w[layer], key_w[layer], value_w[layer], attn_out_w[layer]], 1))
+        shards.append(jnp.concatenate([w[layer] for w in (query_w, key_w, value_w, out_w)], 1))
         shards.append(jnp.concatenate([gate_w[layer], up_w[layer]], 1))
         shards.append(down_w[layer])
-    fused = shards[1].shape[0] % 8 == 0 and HEADS % lax.axis_size("ctx") == 0
-    encoded, full, small_wide, ids, conv, choice, kept = (fused_forward if fused else separate_forward)(
-        lengths, byte_ids, shards, layer_count, vocab, model
-    )
-    encoded = encoded[None]
+    encoded, full, small_wide, ids, conv, choice, kept = separate_forward(lengths, byte_ids, shards, layer_count, vocab, model)
     gains = small_wide.T[vocab + CONV + 2 :]
     gains_a, gains_f = gains[:layer_count], gains[layer_count : 2 * layer_count]
-    grad_stream = out_grad[0].astype(jnp.float32)
+    grad_stream = out_grad.astype(jnp.float32)
     partial = []
     gains = []
     for layer in reversed(range(layer_count)):
@@ -1143,26 +1676,46 @@
     small_grad = lax.dynamic_update_slice(small_grad, columns, (0, vocab + CONV + 2))
     outs = scatter_all([p.astype(jnp.bfloat16) for p in [small_grad] + partial], 1)
     small_out, *rest = outs
-    g_embed, g_conv, g_bias, g_scorer, g_norm_a, g_norm_f = split_small(small_out.T, vocab, layer_count)
     attn_out, ffn_out, down_out = rest[0::3], rest[1::3], rest[2::3]
     columns = [jnp.stack([a[:, i * model : (i + 1) * model] for a in attn_out]) for i in range(4)]
     wide = ffn_out[0].shape[1] // 2
-    return (
-        encoded,
-        g_embed,
-        g_conv,
-        g_bias,
-        g_scorer,
-        g_norm_a,
-        columns[0],
-        columns[1],
-        columns[2],
-        columns[3],
-        g_norm_f,
-        jnp.stack([a[:, :wide] for a in ffn_out]),
-        jnp.stack([a[:, wide:] for a in ffn_out]),
-        jnp.stack(down_out),
-    )
+    halves_out = [jnp.stack([a[:, :wide] for a in ffn_out]), jnp.stack([a[:, wide:] for a in ffn_out])]
+    return encoded, small_out, (*columns, *halves_out, jnp.stack(down_out))
+
+
+def on_device(
+    byte_ids,
+    lengths,
+    embed,
+    conv_weight,
+    conv_bias,
+    scorer,
+    norm_attn,
+    query_w,
+    key_w,
+    value_w,
+    attn_out_w,
+    norm_ffn,
+    gate_w,
+    up_w,
+    down_w,
+    out_grad,
+):
+    layers, vocab = query_w.shape[0], embed.shape[0]
+    small = packed_small(embed, conv_weight, conv_bias, scorer, norm_attn, norm_ffn)
+    if query_w.shape[1] % 8 == 0 and HEADS % lax.axis_size("ctx") == 0:
+        heads_w = head_columns(query_w, key_w, value_w)
+        encoded, small_out, wide_grads = fused_step(
+            lengths, byte_ids, small, heads_w, attn_out_w, gate_w, up_w, down_w, out_grad[0], vocab
+        )
+    else:
+        encoded, small_out, wide_grads = separate_step(
+            lengths, byte_ids, small, query_w, key_w, value_w, attn_out_w, gate_w, up_w, down_w, out_grad[0], vocab
+        )
+    d_query, d_key, d_value, d_out, d_gate, d_up, d_down = wide_grads
+    d_embed, d_conv, d_bias, d_scorer, d_norm_attn, d_norm_ffn = split_small(small_out.T, vocab, layers)
+    return (encoded[None], d_embed, d_conv, d_bias, d_scorer, d_norm_attn, d_query, d_key, d_value, d_out, d_norm_ffn,
+            d_gate, d_up, d_down)
 
 
 def solution(mesh):

time: 501 us -> 429 us (0.86)
  Pallas kernels: 455 us -> 397 us
  other arithmetic: 10.6 us -> 2.1 us
  local copies, waits for them, and re-layouts: 26.8 us -> 21 us
    pallas_call x5 -> x2, Pallas kernels: 455 us -> 397 us  [run_kernel(): pl.pallas_call(kernel, out_shape=[s for s, _ in flat(outputs)], in_specs=...]
    squeeze x7 -> x0, local copies, waits for them, and re-layouts: 6.7 us -> none  [the longest x2 1.91 us: on_device(): shards.append(jnp.concatenate([gate_w[layer], up_w[layer]], 1))]
    another operation x8 -> x0, other arithmetic: 6.04 us -> none  [the longest x4 2.68 us: on_device(): jnp.stack([a[:, i * model:(i + 1) * model] for a in attn_out])]
    reshape x0 -> x7, local copies, waits for them, and re-layouts: none -> 5.51 us  [the longest x4 3.09 us: head_columns(): w.reshape(layers, rows, size, model // size).transpose(0, 2, 1, 3)]
where the time goes in v4:
time: 429 us; the launch traced here: 421 us
  Pallas kernels  397 us (93%)
  local copies, waits for them, and re-layouts  21 us (5%)
    pallas_call x2, Pallas kernels, run_kernel(): pl.pallas_call(kernel, out_shape=[s for s, _ in flat(outputs)], in_specs=...  397 us

profile of v4, /device:TPU:0, one launch (start us, length us, event | category | flops | bytes accessed | tf_op | source)
XLA Modules:
  0.0 421.1 jit_solution(3416590638230300226)
XLA Ops:
  0.6 0.8 copy.38
  1.4 0.7 copy.39
  2.2 0.7 copy.40
  2.9 0.7 copy.41
  3.7 0.7 copy.42
  4.4 0.8 concatenate.6
  5.2 0.6 pad.8.refs_2_
  5.8 1.0 reshape.58
  6.9 1.0 reshape.59
  7.9 1.0 reshape.60
  9.0 0.8 fusion.4.refs_3_
  9.8 186.1 %forward_pass.1 = (bf16[256,768]{1,0:T(8,128)(2,1)}, f32[768,384]{1,0:T(8,128)}, s32[1,1536]{1,0:T(1,128)}, f32[8,256]{1,0:T(8,128)}, f32[768,640]{1,0:T(8,128)}...) custom-call(s32[1,4]{1,0:T(1,128)} %refs_0_.3, ...), custom_call_target="tpu_custom_call" | custom-call | tf_op jit(solution)/shard_map/forward_pass/pallas_call | solution.py:1080
  195.9 210.9 %backward_pass.1 = (f32[24,384]{1,0:T(8,128)}, f32[4,24,640]{2,1,0:T(8,128)}, f32[4,24,640]{2,1,0:T(8,128)}, f32[2,24,2048]{2,1,0:T(8,128)}, f32[2,24,2048]{2,1,...) custom-call(s32[1,4]{1,0:T(1,128)} %refs_0_.3, ...), custom_call_target="tpu_custom_call" | custom-call | tf_op jit(solution)/shard_map/backward_pass/pallas_call | solution.py:1080
  406.8 0.0 copy-start
  406.8 0.0 copy-start.4
  406.8 0.0 copy-start.3
  406.9 0.0 copy-start.2
  406.9 0.0 copy-start.1
  406.9 1.5 slice_reduce_fusion
  408.4 0.7 slice.37
  409.1 0.7 copy.49
  409.8 1.3 slice.36
  411.1 0.9 fusion.10
  412.0 0.6 copy.51
  412.6 0.6 copy.50
  413.3 1.3 fusion.9
  414.6 0.1 copy.48
  414.6 0.8 reshape.67
  415.4 0.1 copy.46
  415.5 0.8 reshape.65
  416.3 0.1 copy.47
  416.4 0.8 reshape.66
  417.2 0.0 copy-done
  417.2 0.7 copy.61
  418.0 0.0 copy-done.4
  418.0 0.7 copy.62
  418.6 0.0 copy-done.3
  418.6 0.7 copy.63
  419.4 0.0 copy-done.2
  419.4 0.7 copy.64
  420.1 0.0 copy-done.1
  420.1 0.7 copy.65
  (2 shorter events, 0.0 us)
Async XLA Ops:
  406.8 10.4 %copy-start = (bf16[256,768]{1,0:T(8,128)(2,1)S(1)}, bf16[256,768]{1,0:T(8,128)(2,1)}, u32[]{:S(2)}) copy-start(bf16[256,768]{1,0:T(8,128)(2,1)} %get-tuple-element.46) | copy-start | bytes 1179652
  406.8 11.1 %copy-start.4 = (f32[2,24,768]{2,1,0:T(8,128)S(1)}, f32[2,24,768]{2,1,0:T(8,128)}, u32[]{:S(2)}) copy-start(f32[2,24,768]{2,1,0:T(8,128)} %get-tuple-element.138) | copy-start | bytes 442372
  406.8 11.8 %copy-start.3 = (f32[2,24,2048]{2,1,0:T(8,128)S(1)}, f32[2,24,2048]{2,1,0:T(8,128)}, u32[]{:S(2)}) copy-start(f32[2,24,2048]{2,1,0:T(8,128)} %get-tuple-element.140) | copy-start | bytes 1179652
  406.9 12.5 %copy-start.2 = (f32[2,24,2048]{2,1,0:T(8,128)S(1)}, f32[2,24,2048]{2,1,0:T(8,128)}, u32[]{:S(2)}) copy-start(f32[2,24,2048]{2,1,0:T(8,128)} %get-tuple-element.141) | copy-start | bytes 1179652
  406.9 13.3 %copy-start.1 = (f32[2,64,768]{2,1,0:T(8,128)S(1)}, f32[2,64,768]{2,1,0:T(8,128)}, u32[]{:S(2)}) copy-start(f32[2,64,768]{2,1,0:T(8,128)} %get-tuple-element.142) | copy-start | bytes 1179652

commit v5 on v4

--- a/solution.py
+++ b/solution.py
@@ -14,6 +14,7 @@
 THIRD = 0.1
 DEPTH = 2
 SPLIT = 3
+LAG = 1
 
 
 def grid_of():
@@ -1040,24 +1041,26 @@
 
 class Rota:
     def __init__(self):
-        self.queue = []
+        self.queue, self.count = [], 0
 
     def add(self, chunk):
         chunk.stage(0)
-        self.queue.append([chunk, 1])
+        self.queue.append([LAG + self.count, chunk, 1])
+        self.count += 1
 
     def tick(self, count=1):
         for _ in range(count):
             if not self.queue:
                 return
-            item = self.queue.pop(0)
-            item[0].stage(item[1])
-            item[1] += 1
-            if item[1] < item[0].phases:
-                self.queue.append(item)
+            item = min(self.queue, key=lambda found: found[0])
+            item[1].stage(item[2])
+            item[0] += LAG
+            item[2] += 1
+            if item[2] == item[1].phases:
+                self.queue.remove(item)
 
     def close(self, chunk):
-        while any(item[0] is chunk for item in self.queue):
+        while any(item[1] is chunk for item in self.queue):
             self.tick()
 
 
@@ -1143,6 +1146,16 @@
     rows = small[:, at // LANES * LANES:].T
     at = at % LANES
     return [rows[at + l:at + l + 1, :] for l in range(2 * layers)]
+
+
+def head_columns(query_w, key_w, value_w, dst):
+    layers, size, rows, width = dst.shape
+    each = query_w.shape[2] // size
+    rest = [jnp.zeros((rows, width - 3 * each), jnp.float32)] if width > 3 * each else []
+    for l in range(layers):
+        whole = [w[l].astype(jnp.float32) for w in (query_w, key_w, value_w)]
+        for p in range(size):
+            dst[l, p] = low(jnp.concatenate([w[:, p * each:(p + 1) * each] for w in whole] + rest, 1))
 
 
 def forward_body(vocab, layers, r):
@@ -1159,6 +1172,7 @@
         copy.start()
         near.append(copy)
     ids[:, count:2 * count] = r.byte_ids[...]
+    head_columns(r.query_w, r.key_w, r.value_w, r.heads_w)
     chunks = [Gather([(r.small, 0)], r.full_small, r.small_sems, r.local_sems.at[0])]
     model = r.encoded.shape[1]
     wide = r.gate_w.shape[2]
@@ -1233,12 +1247,13 @@
                     copy = to_group(r.att_send.at[h, i], att.at[rows], r.att_sems.at[l], (h, i), p)
                     copy.start()
                     copies.append(copy)
-                tick()
+                tick(i != 3)
         keep(r.lse[l], r.out_lse[l])
         for k in range(SPLIT):
             ticker.need(base_chunk + 1 + k)
         load = pltpu.make_async_copy(r.full_ffn[l], r.blocks, r.load_sems.at[l, 0])
         load.start()
+        tick()
         for copy in copies:
             copy.wait_recv()
         keep(att, r.out_att[l])
@@ -1294,7 +1309,7 @@
                 att=((each * size * HEAD_DIM, tokens), bf16), nffn_t=((model, tokens), bf16))
 
 
-def forward_pass(lengths, byte_ids, small, heads_w, out_w, gate_w, up_w, down_w, vocab):
+def forward_pass(lengths, byte_ids, small, query_w, key_w, value_w, out_w, gate_w, up_w, down_w, vocab):
     nz, ny, nx = grid_of()
     size, each = lax.axis_size("ctx"), heads_each()
     layers, _, model = out_w.shape
@@ -1308,9 +1323,9 @@
     per_layer = lambda made: [made] * layers
     ffn = blocks(gate_w.shape[1], 2 * wide + model)
     down = blocks(*down_w.shape[1:])
-    heads = blocks(*heads_w.shape[2:])
-    inputs = dict(lengths=(lengths, SMEM), byte_ids=(byte_ids, VMEM), small=(small, ANY), heads_w=(heads_w, ANY),
-                  out_w=(out_w, ANY), gate_w=(gate_w, ANY), up_w=(up_w, ANY), down_w=(down_w, ANY))
+    heads = blocks(query_w.shape[1], shapes["qkv"][0][0])
+    inputs = dict(lengths=(lengths, SMEM), byte_ids=(byte_ids, VMEM), small=(small, ANY), query_w=(query_w, VMEM), key_w=(key_w, VMEM),
+                  value_w=(value_w, VMEM), out_w=(out_w, ANY), gate_w=(gate_w, ANY), up_w=(up_w, ANY), down_w=(down_w, ANY))
     outputs = dict(
         encoded=(like((tokens, model), bf16), VMEM), small_wide=(like((model, small.shape[1]), f32), VMEM),
         ids=(like((1, 3 * byte_ids.shape[1]), jnp.int32), VMEM), choice=(like((2 * len(BLOCKS), tokens), f32), VMEM),
@@ -1322,7 +1337,7 @@
         out_nffn_t=per_layer((like(*shapes["nffn_t"]), ANY)))
     scratch = {k: per_layer(vmem(*v)) for k, v in shapes.items()}
     scratch.update(
-        full_small=vmem(blocks(*small.shape), bf16), conv=vmem((model, span), f32), full_heads=per_layer(vmem(heads, bf16)),
+        heads_w=vmem((layers, size) + heads[4:], bf16), full_small=vmem(blocks(*small.shape), bf16), conv=vmem((model, span), f32), full_heads=per_layer(vmem(heads, bf16)),
         w_heads=per_layer(vmem((model, heads[-1]), bf16)), w_turned=vmem((heads[-1], model), bf16), w_ffn=vmem((model, ffn[-1]), bf16),
         w_down=vmem(down, bf16), blocks=vmem(ffn, bf16), mine=vmem((model, tokens), bf16),
         att_send=vmem((each, size - 1, HEAD_DIM, tokens), bf16), seg_all=vmem((tokens * size, tokens), jnp.int32),
@@ -1479,14 +1494,14 @@
                 r.dqkv[rows_h[0], theirs] = low(dot(key_t, g_scores))
                 g_key = g_key + dot_nt(query_t, g_scores)
                 g_value = g_value + dot_nt(go_t, low(probs))
-                tick()
+                tick(p != 3)
             r.dqkv[rows_h[1], :] = low(g_key)
             r.dqkv[rows_h[2], :] = low(g_value)
         spread = []
         for i, p in enumerate(others()):
             mine = dot(r.w_heads[...], r.dqkv[:, tokens_of(p, tokens)])
             if i == size - 1:
-                r.summed[...] = mine
+                r.small_grad[:, :tokens] = mine
             else:
                 r.sum_send[i] = low(mine)
                 copy = to_group(r.sum_send.at[i], r.sum_land.at[i], r.sum_sems.at[l], (i,), p)
@@ -1509,8 +1524,8 @@
         tick()
         for i, copy in enumerate(spread):
             copy.wait_recv()
-            r.summed[...] += r.sum_land[i].astype(jnp.float32)
-        back, d_gains[l] = norm_back(r.x[...], gains[l], r.summed[...].T)
+            r.small_grad[:, :tokens] += r.sum_land[i].astype(jnp.float32)
+        back, d_gains[l] = norm_back(r.x[...], gains[l], r.small_grad[:, :tokens].T)
         r.grad[...] += back
         if l:
             load_attention(l - 1)
@@ -1535,9 +1550,12 @@
         tick()
     for chunk in made:
         chunk.finish()
-
-
-def backward_pass(lengths, out_grad, fwd, vocab, heads_width):
+    for l in range(layers):
+        for k, found in enumerate((r.d_query, r.d_key, r.d_value)):
+            found[l] = jnp.concatenate([r.d_heads[l][p, :, k * base:(k + 1) * base] for p in range(size)], 1)
+
+
+def backward_pass(lengths, out_grad, fwd, vocab):
     nz, ny, nx = grid_of()
     size, each = lax.axis_size("ctx"), heads_each()
     tokens, model = out_grad.shape
@@ -1550,6 +1568,7 @@
     dma, vmem = pltpu.SemaphoreType.DMA, pltpu.VMEM
     shapes = kept_shapes(tokens, model)
     per_layer = lambda found: [found] * layers
+    heads_width = fwd.out_w_heads[0].shape[1]
     ffn, down = fwd.full_ffn[0].shape, fwd.full_down[0].shape
     heads = ffn[:5] + (heads_width,)
     small = ffn[:5] + (fwd.small_wide.shape[1],)
@@ -1560,7 +1579,8 @@
         in_w_down=anywhere(w_down), in_x=anywhere(fwd.out_x), in_middle=anywhere(fwd.out_middle), in_nrm=anywhere(fwd.out_nrm),
         in_qkv=anywhere(fwd.out_qkv), in_lse=anywhere(fwd.out_lse), in_att=anywhere(fwd.out_att), in_nffn_t=anywhere(fwd.out_nffn_t))
     outputs = dict(
-        d_small=(like(small[4:], f32), VMEM), d_heads=per_layer((like((size,) + heads[4:], f32), ANY)),
+        d_small=(like(small[4:], f32), VMEM), d_query=(like((layers, ffn[4], model), f32), VMEM),
+        d_key=(like((layers, ffn[4], model), f32), VMEM), d_value=(like((layers, ffn[4], model), f32), VMEM),
         d_gate=(like((layers, ffn[4], wide), f32), VMEM), d_up=(like((layers, ffn[4], wide), f32), VMEM),
         d_out=(like((layers, ffn[4], model), f32), VMEM), d_down=(like((layers,) + down[4:], f32), VMEM),
         parts_ffn=per_layer((like(ffn, bf16), ANY)), parts_down=per_layer((like(down, bf16), ANY)))
@@ -1571,12 +1591,12 @@
         w_down=vmem(w_down[0].shape, bf16), block_ffn=vmem((2,) + ffn[:5] + (2 * part,), bf16), block_down=vmem((2,) + down[2:], bf16),
         block_out=vmem(ffn[:5] + (model,), bf16), block_heads=vmem(heads, bf16), block_small=vmem(small, bf16),
         go_all=vmem((1,) + shapes["att"][0], bf16), go=vmem((1, each * HEAD_DIM, tokens * size), bf16), dqkv=vmem(*shapes["qkv"]),
-        summed=vmem((model, tokens), f32), sum_send=vmem((size - 1, model, tokens), bf16),
+        sum_send=vmem((size - 1, model, tokens), bf16),
         sum_land=vmem((size - 1, model, tokens), bf16),
         seg_all=vmem((tokens * size, tokens), jnp.int32), small_grad=vmem(fwd.small_wide.shape, f32),
         down_scratch=Scatter.scratch(down[4:], bf16), ffn_scratch=[Scatter.scratch((ffn[4], w), bf16) for _, w in splits_of(ffn[-1], SPLIT)], ffn_own=dma((layers, SPLIT)),
         small_scratch=Scatter.scratch(small[4:], bf16),
-        heads_scratch=[vmem((nz, ny, nx) + heads[4:], bf16), vmem((nz - 1, ny, nx) + heads[4:], bf16), vmem((size,) + heads[4:], f32)],
+        d_heads=per_layer(vmem((size,) + heads[4:], f32)), heads_scratch=[vmem((nz, ny, nx) + heads[4:], bf16), vmem((nz - 1, ny, nx) + heads[4:], bf16), vmem((size,) + heads[4:], f32)],
         load_sems=dma((layers, 10)), save_sems=dma((2, 3)), own_sems=dma((layers + 1, 4)), go_own=dma((layers, each)),
         go_sems=dma((layers, 2, each, size - 1)), sum_sems=dma((layers, 2, size - 1)), heads_sems=dma((layers, 2, size + nz - 1)),
         ffn_sems=dma((layers, SPLIT, 2, hops(ffn[-1], THIRD))), down_sems=dma((layers, 2, hops(model, THIRD))),
@@ -1625,22 +1645,11 @@
     return stream.astype(jnp.bfloat16), full, small_wide, ids, conv, choice, kept
 
 
-def head_columns(query_w, key_w, value_w):
-    layers, rows, model = query_w.shape
-    size = lax.axis_size("ctx")
-    found = [w.reshape(layers, rows, size, model // size).transpose(0, 2, 1, 3) for w in (query_w, key_w, value_w)]
-    found = jnp.concatenate(found, 3)
-    return jnp.pad(found, ((0, 0),) * 3 + ((0, -found.shape[3] % LANES),))
-
-
-def fused_step(lengths, byte_ids, small, heads_w, out_w, gate_w, up_w, down_w, out_grad, vocab):
-    fwd = forward_pass(lengths, byte_ids, small, heads_w, out_w, gate_w, up_w, down_w, vocab)
-    back = backward_pass(lengths, out_grad, fwd, vocab, heads_w.shape[3])
-    layers, rows, model = out_w.shape
-    each = model // lax.axis_size("ctx")
-    heads = jnp.stack(back.d_heads)
-    columns = [heads[..., i * each : (i + 1) * each].transpose(0, 2, 1, 3).reshape(layers, rows, model) for i in range(3)]
-    return fwd.encoded, back.d_small, (*columns, back.d_out, back.d_gate, back.d_up, back.d_down)
+def fused_step(lengths, byte_ids, small, query_w, key_w, value_w, out_w, gate_w, up_w, down_w, out_grad, vocab):
+    fwd = forward_pass(lengths, byte_ids, small, query_w, key_w, value_w, out_w, gate_w, up_w, down_w, vocab)
+    back = backward_pass(lengths, out_grad, fwd, vocab)
+    grads = (back.d_query, back.d_key, back.d_value, back.d_out, back.d_gate, back.d_up, back.d_down)
+    return fwd.encoded, back.d_small, grads
 
 
 def separate_step(lengths, byte_ids, small, query_w, key_w, value_w, out_w, gate_w, up_w, down_w, out_grad, vocab):
@@ -1704,14 +1713,12 @@
     layers, vocab = query_w.shape[0], embed.shape[0]
     small = packed_small(embed, conv_weight, conv_bias, scorer, norm_attn, norm_ffn)
     if query_w.shape[1] % 8 == 0 and HEADS % lax.axis_size("ctx") == 0:
-        heads_w = head_columns(query_w, key_w, value_w)
-        encoded, small_out, wide_grads = fused_step(
-            lengths, byte_ids, small, heads_w, attn_out_w, gate_w, up_w, down_w, out_grad[0], vocab
-        )
+        step = fused_step
     else:
-        encoded, small_out, wide_grads = separate_step(
-            lengths, byte_ids, small, query_w, key_w, value_w, attn_out_w, gate_w, up_w, down_w, out_grad[0], vocab
-        )
+        step = separate_step
+    encoded, small_out, wide_grads = step(
+        lengths, byte_ids, small, query_w, key_w, value_w, attn_out_w, gate_w, up_w, down_w, out_grad[0], vocab
+    )
     d_query, d_key, d_value, d_out, d_gate, d_up, d_down = wide_grads
     d_embed, d_conv, d_bias, d_scorer, d_norm_attn, d_norm_ffn = split_small(small_out.T, vocab, layers)
     return (encoded[None], d_embed, d_conv, d_bias, d_scorer, d_norm_attn, d_query, d_key, d_value, d_out, d_norm_ffn,

time: 429 us -> 414 us (0.965)
  Pallas kernels: 397 us -> 383 us
    pallas_call x2, Pallas kernels: 397 us -> 383 us  [run_kernel(): pl.pallas_call(kernel, out_shape=[s for s, _ in flat(outputs)], in_specs=...]
    unnamed x21 -> x20, local copies, waits for them, and re-layouts: 7.86 us -> 14.5 us
    reshape x7 -> x0, local copies, waits for them, and re-layouts: 5.51 us -> none  [the longest x4 3.09 us: head_columns(): w.reshape(layers, rows, size, model // size).transpose(0, 2, 1, 3)]
where the time goes in v5:
time: 414 us; the launch traced here: 406 us
  Pallas kernels  383 us (93%)
  local copies, waits for them, and re-layouts  21.8 us (5%)
    pallas_call x2, Pallas kernels, run_kernel(): pl.pallas_call(kernel, out_shape=[s for s, _ in flat(outputs)], in_specs=...  383 us
    unnamed x20, local copies, waits for them, and re-layouts  14.5 us

profile of v5, /device:TPU:0, one launch (start us, length us, event | category | flops | bytes accessed | tf_op | source)
XLA Modules:
  0.0 406.2 jit_solution(7716850715030060105)
XLA Ops:
  0.6 0.8 copy.38
  1.4 0.7 copy.39
  2.2 0.7 copy.40
  2.9 0.7 copy.41
  3.7 0.7 copy.42
  4.4 0.8 concatenate.3
  5.2 0.6 pad.4.refs_2_
  5.8 184.8 %forward_pass.1 = (bf16[256,768]{1,0:T(8,128)(2,1)}, f32[768,384]{1,0:T(8,128)}, s32[1,1536]{1,0:T(1,128)}, f32[8,256]{1,0:T(8,128)}, f32[768,640]{1,0:T(8,128)}...) custom-call(s32[1,4]{1,0:T(1,128)} %refs_0_.3, ...), custom_call_target="tpu_custom_call" | custom-call | tf_op jit(solution)/shard_map/forward_pass/pallas_call | solution.py:1083
  190.6 0.0 copy-start
  190.6 198.6 %backward_pass.1 = (f32[24,384]{1,0:T(8,128)}, f32[2,24,768]{2,1,0:T(8,128)}, f32[2,24,768]{2,1,0:T(8,128)}, f32[2,24,768]{2,1,0:T(8,128)}, f32[2,24,2048]{2,1,0...) custom-call(s32[1,4]{1,0:T(1,128)} %refs_0_.3, ...), custom_call_target="tpu_custom_call" | custom-call | tf_op jit(solution)/shard_map/backward_pass/pallas_call | solution.py:1083
  389.3 0.0 copy-start.2
  389.3 0.0 copy-start.1
  389.3 1.5 slice_reduce_fusion
  390.8 0.7 slice.25
  391.5 0.7 copy.43
  392.1 1.3 slice.24
  393.5 0.9 fusion
  394.3 0.6 copy.45
  395.0 0.6 copy.44
  395.6 0.0 copy-done
  395.6 0.7 copy.54
  396.4 1.6 copy.55
  397.9 1.6 copy.56
  399.5 1.6 copy.57
  401.1 1.6 copy.58
  402.7 1.8 copy.59
  404.5 0.0 copy-done.2
  404.5 0.7 copy.60
  405.2 0.0 copy-done.1
  405.2 0.7 copy.61
Async XLA Ops:
  190.6 205.0 %copy-start = (bf16[256,768]{1,0:T(8,128)(2,1)S(1)}, bf16[256,768]{1,0:T(8,128)(2,1)}, u32[]{:S(2)}) copy-start(bf16[256,768]{1,0:T(8,128)(2,1)} %get-tuple-element.47) | copy-start | bytes 1179652
  389.3 15.2 %copy-start.2 = (f32[2,24,2048]{2,1,0:T(8,128)S(1)}, f32[2,24,2048]{2,1,0:T(8,128)}, u32[]{:S(2)}) copy-start(f32[2,24,2048]{2,1,0:T(8,128)} %get-tuple-element.138) | copy-start | bytes 1179652
  389.3 15.9 %copy-start.1 = (f32[2,64,768]{2,1,0:T(8,128)S(1)}, f32[2,64,768]{2,1,0:T(8,128)}, u32[]{:S(2)}) copy-start(f32[2,64,768]{2,1,0:T(8,128)} %get-tuple-element.139) | copy-start | bytes 1179652

commit v6 on v5

--- a/solution.py
+++ b/solution.py
@@ -1249,16 +1249,23 @@
                     copies.append(copy)
                 tick(i != 3)
         keep(r.lse[l], r.out_lse[l])
-        for k in range(SPLIT):
+        held = None
+        for k, (at, width) in enumerate(splits_of(r.w_ffn.shape[1], SPLIT)):
             ticker.need(base_chunk + 1 + k)
-        load = pltpu.make_async_copy(r.full_ffn[l], r.blocks, r.load_sems.at[l, 0])
-        load.start()
+            columns = pl.ds(at, width)
+            part_of = (slice(None),) * 5 + (columns,)
+            load = pltpu.make_async_copy(r.full_ffn[l].at[part_of], r.blocks.at[part_of], r.load_sems.at[l, 1 + k])
+            load.start()
+            if held is not None:
+                held[0].wait()
+                unpack(r.blocks.at[held[1]], r.w_ffn.at[:, held[2]])
+            held = (load, part_of, columns)
         tick()
+        held[0].wait()
+        unpack(r.blocks.at[held[1]], r.w_ffn.at[:, held[2]])
         for copy in copies:
             copy.wait_recv()
         keep(att, r.out_att[l])
-        load.wait()
-        unpack(r.blocks, r.w_ffn)
         mid = stream + dot(flip(att[...]), r.w_ffn[:, 2 * wide:])
         r.middle[l][...] = mid
         after = low(mid * inverse_rms(mid) * gains[layers + l])
@@ -1268,7 +1275,7 @@
         keep(r.middle[l], r.out_middle[l])
         keep(r.nffn_t[l], r.out_nffn_t[l])
         ticker.need(base_chunk + 1 + SPLIT)
-        load = pltpu.make_async_copy(r.full_down[l], r.w_down, r.load_sems.at[l, 1])
+        load = pltpu.make_async_copy(r.full_down[l], r.w_down, r.load_sems.at[l, 0])
         load.start()
         load.wait()
         part = wide // (nz * cores)
@@ -1343,7 +1350,7 @@
         att_send=vmem((each, size - 1, HEAD_DIM, tokens), bf16), seg_all=vmem((tokens * size, tokens), jnp.int32),
         nffn=vmem((tokens, model), bf16), total=vmem((tokens, model), f32),
         keep_sems=dma((1 + 8 * layers,)), ids_sems=dma((2, 2)), local_sems=dma((1 + layers * SPLIT, 3)), more_sems=dma((layers, 2)),
-        load_sems=dma((layers, 2)), nrm_sems=dma((layers, 2, size - 1)), att_sems=dma((layers, 2, each, size - 1)),
+        load_sems=dma((layers, 1 + SPLIT)), nrm_sems=dma((layers, 2, size - 1)), att_sems=dma((layers, 2, each, size - 1)),
         small_sems=dma((2, hops(small.shape[1], THIRD))), heads_sems=dma((layers, 2, size + nz - 1)),
         ffn_sems=dma((layers, SPLIT, 2, hops(ffn[-1], THIRD))), down_sems=dma((layers, 2, hops(model, THIRD))))
     return run_kernel(functools.partial(forward_body, vocab, layers), inputs, outputs, scratch, 4, "forward_pass")

time: 414 us -> 415 us (level)
  no operation moved by 1% of the time
where the time goes in v6:
time: 415 us; the launch traced here: 408 us
  Pallas kernels  386 us (93%)
  local copies, waits for them, and re-layouts  21.8 us (5%)
    pallas_call x2, Pallas kernels, run_kernel(): pl.pallas_call(kernel, out_shape=[s for s, _ in flat(outputs)], in_specs=...  386 us
    unnamed x20, local copies, waits for them, and re-layouts  14.5 us

profile of v6, /device:TPU:0, one launch (start us, length us, event | category | flops | bytes accessed | tf_op | source)
XLA Modules:
  0.0 408.3 jit_solution(12189395227492172114)
XLA Ops:
  0.6 0.8 copy.38
  1.4 0.7 copy.39
  2.2 0.7 copy.40
  2.9 0.7 copy.41
  3.7 0.7 copy.42
  4.4 0.8 concatenate.3
  5.2 0.6 pad.4.refs_2_
  5.8 185.3 %forward_pass.1 = (bf16[256,768]{1,0:T(8,128)(2,1)}, f32[768,384]{1,0:T(8,128)}, s32[1,1536]{1,0:T(1,128)}, f32[8,256]{1,0:T(8,128)}, f32[768,640]{1,0:T(8,128)}...) custom-call(s32[1,4]{1,0:T(1,128)} %refs_0_.3, ...), custom_call_target="tpu_custom_call" | custom-call | tf_op jit(solution)/shard_map/forward_pass/pallas_call | solution.py:1083
  191.1 0.0 copy-start
  191.1 200.3 %backward_pass.1 = (f32[24,384]{1,0:T(8,128)}, f32[2,24,768]{2,1,0:T(8,128)}, f32[2,24,768]{2,1,0:T(8,128)}, f32[2,24,768]{2,1,0:T(8,128)}, f32[2,24,2048]{2,1,0...) custom-call(s32[1,4]{1,0:T(1,128)} %refs_0_.3, ...), custom_call_target="tpu_custom_call" | custom-call | tf_op jit(solution)/shard_map/backward_pass/pallas_call | solution.py:1083
  391.4 0.0 copy-start.2
  391.4 0.0 copy-start.1
  391.4 1.5 slice_reduce_fusion
  392.9 0.7 slice.25
  393.6 0.7 copy.43
  394.3 1.3 slice.24
  395.6 0.9 fusion
  396.5 0.6 copy.45
  397.1 0.6 copy.44
  397.8 0.0 copy-done
  397.8 0.7 copy.54
  398.5 1.6 copy.55
  400.1 1.6 copy.56
  401.7 1.6 copy.57
  403.3 1.6 copy.58
  404.8 1.8 copy.59
  406.6 0.0 copy-done.2
  406.6 0.7 copy.60
  407.4 0.0 copy-done.1
  407.4 0.7 copy.61
Async XLA Ops:
  191.1 206.7 %copy-start = (bf16[256,768]{1,0:T(8,128)(2,1)S(1)}, bf16[256,768]{1,0:T(8,128)(2,1)}, u32[]{:S(2)}) copy-start(bf16[256,768]{1,0:T(8,128)(2,1)} %get-tuple-element.47) | copy-start | bytes 1179652
  391.4 15.2 %copy-start.2 = (f32[2,24,2048]{2,1,0:T(8,128)S(1)}, f32[2,24,2048]{2,1,0:T(8,128)}, u32[]{:S(2)}) copy-start(f32[2,24,2048]{2,1,0:T(8,128)} %get-tuple-element.138) | copy-start | bytes 1179652
  391.4 15.9 %copy-start.1 = (f32[2,64,768]{2,1,0:T(8,128)S(1)}, f32[2,64,768]{2,1,0:T(8,128)}, u32[]{:S(2)}) copy-start(f32[2,64,768]{2,1,0:T(8,128)} %get-tuple-element.139) | copy-start | bytes 1179652
